TPU v7x, 32 devices: a whole 2x2x4 slice. The times are simulated.
32 devices in a mesh: dp: 8 (over z, x), heads: 4 (over y, core).
Axes of the slice: x: 2, y: 2, z: 4, core: 2. Of those that a mesh axis runs over, the one named last changes fastest.
Arguments:
- token_ids: int32 [32, 512], P('dp'), may hold values from 0 to 50687
- row_lengths: int32 [32], P('dp'), may hold values from 64 to 512, as said below
- replaced: int32 [32, 512], P('dp'), may hold values 0 or 1
- embedding: float32 [768, 50688], P('dp', 'heads'), may hold values from -0.3 to 0.3
- relative: float32 [512, 768], P(None, 'dp'), may hold values from -0.12 to 0.12
- project: float32 [768, 3, 768], P('dp', None, 'heads'), may hold values from -0.21875 to 0.21875
- combine: float32 [768, 768], P('heads', 'dp'), may hold values from -0.625 to 0.625
- expand: float32 [768, 3072], P('dp', 'heads'), may hold values from -0.21875 to 0.21875
- contract: float32 [3072, 768], P('heads', 'dp'), may hold values from -0.109375 to 0.109375
- readout: float32 [768, 768], P('dp'), may hold values from -0.21875 to 0.21875
- vectors: float32 [11, 768], P(None, 'dp')
- embedding_mean: float32 [768, 50688], P('dp', 'heads'), may hold values from -4.4703484e-08 to 4.4703484e-08
- relative_mean: float32 [512, 768], P(None, 'dp'), may hold values from -4.7683716e-07 to 4.7683716e-07
- project_mean: float32 [768, 3, 768], P('dp', None, 'heads'), may hold values from -4.7683716e-07 to 4.7683716e-07
- combine_mean: float32 [768, 768], P('heads', 'dp'), may hold values from -4.7683716e-07 to 4.7683716e-07
- expand_mean: float32 [768, 3072], P('dp', 'heads'), may hold values from -4.7683716e-07 to 4.7683716e-07
- contract_mean: float32 [3072, 768], P('heads', 'dp'), may hold values from -4.7683716e-07 to 4.7683716e-07
- readout_mean: float32 [768, 768], P('dp'), may hold values from -4.7683716e-07 to 4.7683716e-07
- vectors_mean: float32 [11, 768], P(None, 'dp'), may hold values from -1.9073486e-06 to 1.9073486e-06
- embedding_square: float32 [768, 50688], P('dp', 'heads'), may hold values from 5.3194024e-16 to 2.127761e-15
- relative_square: float32 [512, 768], P(None, 'dp'), may hold values from 5.3194024e-16 to 2.127761e-15
- project_square: float32 [768, 3, 768], P('dp', None, 'heads'), may hold values from 5.3194024e-16 to 2.127761e-15
- combine_square: float32 [768, 768], P('heads', 'dp'), may hold values from 5.3194024e-16 to 2.127761e-15
- expand_square: float32 [768, 3072], P('dp', 'heads'), may hold values from 5.3194024e-16 to 2.127761e-15
- contract_square: float32 [3072, 768], P('heads', 'dp'), may hold values from 5.3194024e-16 to 2.127761e-15
- readout_square: float32 [768, 768], P('dp'), may hold values from 5.3194024e-16 to 2.127761e-15
- vectors_square: float32 [11, 768], P(None, 'dp'), may hold values from 1.0638805e-12 to 4.255522e-12
Outputs:
- loss_sum: float32 [], replicated
- token_total: float32 [], replicated
- grad_norm: float32 [], replicated
- embedding_first: float32 [768, 50688], P('dp', 'heads')
- embedding_second: float32 [768, 50688], P('dp', 'heads')
- embedding_master: float32 [768, 50688], P('dp', 'heads')
- relative_first: float32 [512, 768], P(None, 'dp')
- relative_second: float32 [512, 768], P(None, 'dp')
- relative_master: float32 [512, 768], P(None, 'dp')
- project_first: float32 [768, 3, 768], P('dp', None, 'heads')
- project_second: float32 [768, 3, 768], P('dp', None, 'heads')
- project_master: float32 [768, 3, 768], P('dp', None, 'heads')
- combine_first: float32 [768, 768], P('heads', 'dp')
- combine_second: float32 [768, 768], P('heads', 'dp')
- combine_master: float32 [768, 768], P('heads', 'dp')
- expand_first: float32 [768, 3072], P('dp', 'heads')
- expand_second: float32 [768, 3072], P('dp', 'heads')
- expand_master: float32 [768, 3072], P('dp', 'heads')
- contract_first: float32 [3072, 768], P('heads', 'dp')
- contract_second: float32 [3072, 768], P('heads', 'dp')
- contract_master: float32 [3072, 768], P('heads', 'dp')
- readout_first: float32 [768, 768], P('dp')
- readout_second: float32 [768, 768], P('dp')
- readout_master: float32 [768, 768], P('dp')
- vectors_first: float32 [11, 768], P(None, 'dp')
- vectors_second: float32 [11, 768], P(None, 'dp')
- vectors_master: float32 [11, 768], P(None, 'dp')
- relative_bias_grad: float32 [768], P('dp')
Inputs may be any that keep to these rules, and one draw needn't show every extreme that they name: `row_lengths`: one row among the last 4 rows has length 512; lengths tend to grow with the row's index.
All inputs are finite; a program needn't handle non-finite values. No bound on the sum of `replaced` on one device may be relied on, other than what follows from the above.
Results may differ from a plain program's by a relative error of at most 0.0091.
Values may be sent and summed in bfloat16 or wider, within the bound.
A program may use at most 320 MiB of HBM per device.

v0:
```python
import jax
import jax.numpy as jnp
from jax import lax
from jax.sharding import PartitionSpec as P

HEAD_DIM = 64
STEP = 10


layer_eps = 1e-07
clip_level = 0.005
rate_steps = (0.1, 0.05, 0.05, 0.05, 0.05, 0.05, 0.05, 1.0)
beta_first = 0.9
beta_second = 0.999
adam_eps = 1e-08
weight_decay = 0.01


def matmul(matrix, operand):
    return jnp.dot(matrix, operand, preferred_element_type=jnp.float32)


def inner_left(matrix, operand):
    return lax.dot_general(
        matrix, operand, (((0,), (0,)), ((), ())), preferred_element_type=jnp.float32
    )


def times_transposed(matrix, operand):
    return lax.dot_general(
        matrix, operand, (((1,), (1,)), ((), ())), preferred_element_type=jnp.float32
    )


def normalize(values, gain_row, bias_row):
    center = values - jnp.mean(values, -1, keepdims=True)
    spread_sq = jnp.mean(center * center, -1, keepdims=True)
    return center * lax.rsqrt(spread_sq + layer_eps) * gain_row + bias_row


def gelu(values):
    return jax.nn.gelu(values, approximate=False)


def rel_skew(table):
    head_count, seq_len, width = table.shape
    span = width // 2
    low_end = jnp.broadcast_to(
        table[:, :, width - 1 : width], (head_count, seq_len, seq_len - span)
    )
    high_end = jnp.broadcast_to(table[:, :, 0:1], (head_count, seq_len, seq_len - 1 - span))
    padding = jnp.zeros((head_count, seq_len, 1), table.dtype)
    extended = jnp.concatenate([low_end, table[:, :, ::-1], high_end, padding], 2)
    flat = extended.reshape(head_count, seq_len * 2 * seq_len)
    window = flat[:, seq_len - 1 : seq_len - 1 + seq_len * (2 * seq_len - 1)]
    return window.reshape(head_count, seq_len, 2 * seq_len - 1)[:, :, :seq_len]


def spread_rows(values):
    return lax.all_gather(values, "heads", axis=0, tiled=True)


def collect_rows(values):
    return lax.psum_scatter(values, "heads", scatter_dimension=0, tiled=True)


def pick_rows(vocab_table, id_list, holder):
    vocab_slab = vocab_table.shape[1]
    local_ids = id_list - holder * vocab_slab
    inside = (local_ids >= 0) & (local_ids < vocab_slab)
    found = jnp.take(vocab_table, jnp.clip(local_ids, 0, vocab_slab - 1), axis=1).T
    return jnp.where(inside[:, None], found, jnp.zeros((), vocab_table.dtype))


def add_rows(grad_rows, id_list, holder, vocab_slab):
    local_ids = id_list - holder * vocab_slab
    inside = (local_ids >= 0) & (local_ids < vocab_slab)
    kept_rows = jnp.where(inside[:, None], grad_rows, 0.0)
    empty_table = jnp.zeros((grad_rows.shape[1], vocab_slab), jnp.float32)
    return empty_table.at[:, jnp.clip(local_ids, 0, vocab_slab - 1)].add(kept_rows.T)


def row_scores(queries, key_rows, rel_q, rel_k, length):
    seq_len = queries.shape[0]
    direct_scores = jnp.einsum(
        "ihe,jhe->hij", queries, key_rows, preferred_element_type=jnp.float32
    )
    near_scores = jnp.einsum("ihe,rhe->hir", queries, rel_k, preferred_element_type=jnp.float32)
    far_scores = jnp.einsum("jhe,rhe->hjr", key_rows, rel_q, preferred_element_type=jnp.float32)
    scores = (direct_scores + rel_skew(near_scores) + jnp.swapaxes(rel_skew(far_scores), 1, 2)) * (
        3 * HEAD_DIM
    ) ** (-0.5)
    valid = jnp.arange(seq_len) < length
    return (jnp.where(valid[None, None, :], scores, -1000000000.0), near_scores.shape)


def row_forward(blocks, rel_q, rel_k):
    queries, key_rows, value_rows, length = blocks
    scores, unused_shape = row_scores(queries, key_rows, rel_q, rel_k, length)
    row_max = jnp.max(scores, -1, keepdims=True)
    expo = jnp.exp(scores - row_max)
    row_sum = jnp.sum(expo, -1, keepdims=True)
    probs = expo / row_sum
    attn_mixed = jnp.einsum(
        "hij,jhe->ihe", probs.astype(jnp.bfloat16), value_rows, preferred_element_type=jnp.float32
    )
    return (attn_mixed.astype(jnp.bfloat16), (row_max + jnp.log(row_sum))[..., 0])


def row_backward(totals, blocks, rel_q, rel_k):
    queries, key_rows, value_rows, grad_mixed, log_sum, length = blocks
    scores, table_shape = row_scores(queries, key_rows, rel_q, rel_k, length)
    probs = jnp.exp(scores - log_sum[..., None])
    grad_values = jnp.einsum(
        "hij,ihe->jhe", probs.astype(jnp.bfloat16), grad_mixed, preferred_element_type=jnp.float32
    )
    grad_probs = jnp.einsum(
        "ihe,jhe->hij", grad_mixed, value_rows, preferred_element_type=jnp.float32
    )
    grad_scores = (
        probs
        * (grad_probs - jnp.sum(probs * grad_probs, -1, keepdims=True))
        * (3 * HEAD_DIM) ** (-0.5)
    )
    direct_low = grad_scores.astype(jnp.bfloat16)
    unused, skew_back = jax.vjp(rel_skew, jnp.zeros(table_shape, jnp.float32))
    near_low = skew_back(grad_scores)[0].astype(jnp.bfloat16)
    far_low = skew_back(jnp.swapaxes(grad_scores, 1, 2))[0].astype(jnp.bfloat16)
    grad_queries = jnp.einsum(
        "hij,jhe->ihe", direct_low, key_rows, preferred_element_type=jnp.float32
    ) + jnp.einsum("hir,rhe->ihe", near_low, rel_k, preferred_element_type=jnp.float32)
    grad_keys = jnp.einsum(
        "hij,ihe->jhe", direct_low, queries, preferred_element_type=jnp.float32
    ) + jnp.einsum("hjr,rhe->jhe", far_low, rel_q, preferred_element_type=jnp.float32)
    new_totals = (
        totals[0]
        + jnp.einsum("hjr,jhe->rhe", far_low, key_rows, preferred_element_type=jnp.float32),
        totals[1]
        + jnp.einsum("hir,ihe->rhe", near_low, queries, preferred_element_type=jnp.float32),
    )
    return (
        new_totals,
        (
            grad_queries.astype(jnp.bfloat16),
            grad_keys.astype(jnp.bfloat16),
            grad_values.astype(jnp.bfloat16),
        ),
    )


def adamw(weight, gradient, mean, square, rate_now):
    first = beta_first * mean + (1.0 - beta_first) * gradient
    second = beta_second * square + (1.0 - beta_second) * gradient * gradient
    mean_hat = first / (1.0 - beta_first**STEP)
    square_hat = second / (1.0 - beta_second**STEP)
    master = weight - rate_now * (
        mean_hat / (jnp.sqrt(square_hat) + adam_eps) + weight_decay * weight
    )
    return (first, second, master)


def norm_at(first_row):

    def apply_norm(values, gain_rows):
        return normalize(values, gain_rows[first_row], gain_rows[first_row + 1])

    return apply_norm


def per_device(
    token_ids,
    row_lengths,
    replaced,
    embedding,
    relative,
    project,
    combine,
    expand,
    contract,
    readout,
    vectors,
    embedding_mean,
    relative_mean,
    project_mean,
    combine_mean,
    expand_mean,
    contract_mean,
    readout_mean,
    vectors_mean,
    embedding_square,
    relative_square,
    project_square,
    combine_square,
    expand_square,
    contract_square,
    readout_square,
    vectors_square,
):
    row_count, seq_len = token_ids.shape
    pieces = lax.axis_size("heads")
    holder = lax.axis_index("heads")
    quarter = row_count * seq_len // pieces
    low_type = jnp.bfloat16
    w_project, w_combine, w_expand, w_contract, w_readout = (
        lax.all_gather(project.astype(low_type), "dp", axis=0, tiled=True),
        lax.all_gather(combine.astype(low_type), "dp", axis=1, tiled=True),
        lax.all_gather(expand.astype(low_type), "dp", axis=0, tiled=True),
        lax.all_gather(contract.astype(low_type), "dp", axis=1, tiled=True),
        lax.all_gather(readout.astype(low_type), "dp", axis=0, tiled=True),
    )
    rel_full, vec_full = (
        lax.all_gather(relative, "dp", axis=1, tiled=True),
        lax.all_gather(vectors, "dp", axis=1, tiled=True),
    )
    live_rows = jnp.arange(seq_len)[None, :] < row_lengths[:, None]
    token_total = lax.psum(jnp.sum(live_rows.astype(jnp.float32)), "dp")
    flat_ids = token_ids.reshape(-1)
    vocab_slab = embedding.shape[1]
    vocab_table = lax.all_gather(embedding.astype(low_type), "dp", axis=0, tiled=True)
    partial_words = pick_rows(vocab_table, flat_ids, holder).astype(jnp.float32)
    word_rows = collect_rows(partial_words)
    first_row = holder * quarter
    live_part = lax.dynamic_slice_in_dim(live_rows.reshape(-1), first_row, quarter)
    flag_part = lax.dynamic_slice_in_dim(replaced.reshape(-1), first_row, quarter).astype(
        jnp.float32
    )
    hidden_in, back_in = jax.vjp(norm_at(0), word_rows, vec_full)
    hidden_low = spread_rows(hidden_in.astype(low_type))
    local_width = w_project.shape[2]
    heads_here = local_width // HEAD_DIM
    qkv_rows = jnp.einsum(
        "td,dkc->tkc", hidden_low, w_project, preferred_element_type=jnp.float32
    ).astype(low_type)
    rel_norm, back_rel = jax.vjp(norm_at(2), rel_full, vec_full)
    rel_low = rel_norm.astype(low_type)
    rel_qh = matmul(rel_low, w_project[:, 0]).astype(low_type).reshape(-1, heads_here, HEAD_DIM)
    rel_kh = matmul(rel_low, w_project[:, 1]).astype(low_type).reshape(-1, heads_here, HEAD_DIM)

    def head_split(matrix):
        return matrix.reshape(row_count, seq_len, heads_here, HEAD_DIM)

    split_q = head_split(qkv_rows[:, 0])
    split_k = head_split(qkv_rows[:, 1])
    split_v = head_split(qkv_rows[:, 2])

    def forward_row(blocks):
        return row_forward(blocks, rel_qh, rel_kh)

    attn_mixed, log_sums = lax.map(forward_row, (split_q, split_k, split_v, row_lengths))
    mixed_flat = attn_mixed.reshape(row_count * seq_len, local_width)
    attended = collect_rows(matmul(mixed_flat, w_combine))
    hidden_mid, back_mid = jax.vjp(norm_at(4), hidden_in + attended, vec_full)
    mid_low = spread_rows(hidden_mid.astype(low_type))
    gate_in = matmul(mid_low, w_expand)
    gate_act, back_gate = jax.vjp(gelu, gate_in)
    gate_low = gate_act.astype(low_type)
    ffn_out = collect_rows(matmul(gate_low, w_contract))
    hidden_out, back_out = jax.vjp(norm_at(6), hidden_mid + ffn_out, vec_full)
    out_low = hidden_out.astype(low_type)
    dense_out = matmul(out_low, w_readout)

    def head_loss(dense_rows, gain_rows):
        head_norm = normalize(gelu(dense_rows), gain_rows[8], gain_rows[9])
        logits = jnp.sum(head_norm * gain_rows[10], -1)
        losses = jax.nn.softplus(logits) - flag_part * logits
        return jnp.sum(jnp.where(live_part, losses, 0.0))

    loss_part, back_head = jax.vjp(head_loss, dense_out, vec_full)
    grad_dense, grad_vec = back_head(1.0 / token_total)
    dense_low = grad_dense.astype(low_type)
    grad_readout = inner_left(out_low, dense_low)
    grad_sum, grad_gain = back_out(times_transposed(dense_low, w_readout))
    grad_vec = grad_vec + grad_gain
    ffn_low = spread_rows(grad_sum.astype(low_type))
    grad_contract = inner_left(gate_low, ffn_low)
    gate_grad = back_gate(times_transposed(ffn_low, w_contract))[0].astype(low_type)
    grad_expand = inner_left(mid_low, gate_grad)
    grad_mid = grad_sum + collect_rows(times_transposed(gate_grad, w_expand))
    grad_sum, grad_gain = back_mid(grad_mid)
    grad_vec = grad_vec + grad_gain
    attend_low = spread_rows(grad_sum.astype(low_type))
    grad_mixed = times_transposed(attend_low, w_combine).astype(low_type)
    grad_combine = inner_left(mixed_flat, attend_low)
    zero_rel = jnp.zeros(rel_qh.shape, jnp.float32)

    def backward_row(totals, blocks):
        return row_backward(totals, blocks, rel_qh, rel_kh)

    rel_totals, qkv_grads = lax.scan(
        backward_row,
        (zero_rel, zero_rel),
        (split_q, split_k, split_v, head_split(grad_mixed), log_sums, row_lengths),
    )
    grad_joined = jnp.stack([part_grad.reshape(-1, local_width) for part_grad in qkv_grads], 1)
    relq_low = rel_totals[0].reshape(-1, local_width).astype(low_type)
    relk_low = rel_totals[1].reshape(-1, local_width).astype(low_type)
    grad_project = jnp.einsum(
        "td,tkc->dkc", hidden_low, grad_joined, preferred_element_type=jnp.float32
    )
    grad_project = (
        grad_project.at[:, 0]
        .add(inner_left(rel_low, relq_low))
        .at[:, 1]
        .add(inner_left(rel_low, relk_low))
    )
    grad_hidden = grad_sum + collect_rows(
        jnp.einsum("tkc,dkc->td", grad_joined, w_project, preferred_element_type=jnp.float32)
    )
    grad_rel_norm = times_transposed(relq_low, w_project[:, 0]) + times_transposed(
        relk_low, w_project[:, 1]
    )
    grad_relative, grad_gain = back_rel(grad_rel_norm)
    grad_vec = grad_vec + grad_gain
    grad_words, grad_gain = back_in(grad_hidden)
    grad_vec = grad_vec + grad_gain
    word_grads = lax.all_gather(
        grad_words.astype(jnp.bfloat16), "heads", axis=0, tiled=True
    ).astype(grad_words.dtype)
    grad_embedding = lax.psum_scatter(
        add_rows(word_grads, flat_ids, holder, vocab_slab), "dp", scatter_dimension=0, tiled=True
    )
    grad_relative, grad_readout, grad_vec = (
        lax.psum(grad_relative.astype(jnp.bfloat16), "heads").astype(jnp.float32),
        lax.psum(grad_readout.astype(jnp.bfloat16), "heads").astype(jnp.float32),
        lax.psum(grad_vec.astype(jnp.bfloat16), "heads").astype(jnp.float32),
    )
    (
        grad_project,
        grad_combine,
        grad_expand,
        grad_contract,
        grad_readout,
        grad_relative,
        grad_vec,
    ) = (
        lax.psum_scatter(grad_project, "dp", scatter_dimension=0, tiled=True),
        lax.psum_scatter(grad_combine, "dp", scatter_dimension=1, tiled=True),
        lax.psum_scatter(grad_expand, "dp", scatter_dimension=0, tiled=True),
        lax.psum_scatter(grad_contract, "dp", scatter_dimension=1, tiled=True),
        lax.psum_scatter(grad_readout, "dp", scatter_dimension=0, tiled=True),
        lax.psum_scatter(grad_relative, "dp", scatter_dimension=1, tiled=True),
        lax.psum_scatter(grad_vec, "dp", scatter_dimension=1, tiled=True),
    )
    shared_part = (holder == 0).astype(jnp.float32)
    own_grads = (grad_embedding, grad_project, grad_combine, grad_expand, grad_contract)
    common_grads = (grad_relative, grad_readout, grad_vec)
    squares_local = sum(
        (jnp.sum(gradient * gradient) for gradient in own_grads)
    ) + shared_part * sum((jnp.sum(gradient * gradient) for gradient in common_grads))
    squares_total, loss_sum = lax.psum((squares_local, loss_part), ("dp", "heads"))
    grad_norm = jnp.sqrt(squares_total)
    factor = jnp.minimum(1.0, clip_level / grad_norm)
    weights = (embedding, relative, project, combine, expand, contract, readout, vectors)
    gradients = (
        grad_embedding,
        grad_relative,
        grad_project,
        grad_combine,
        grad_expand,
        grad_contract,
        grad_readout,
        grad_vec,
    )
    means = (
        embedding_mean,
        relative_mean,
        project_mean,
        combine_mean,
        expand_mean,
        contract_mean,
        readout_mean,
        vectors_mean,
    )
    squares = (
        embedding_square,
        relative_square,
        project_square,
        combine_square,
        expand_square,
        contract_square,
        readout_square,
        vectors_square,
    )
    updates = [
        adamw(weight, gradient * factor, mean, square, rate_now)
        for weight, gradient, mean, square, rate_now in zip(
            weights, gradients, means, squares, rate_steps
        )
    ]
    return (
        loss_sum,
        token_total,
        grad_norm,
        updates[0][0],
        updates[0][1],
        updates[0][2],
        updates[1][0],
        updates[1][1],
        updates[1][2],
        updates[2][0],
        updates[2][1],
        updates[2][2],
        updates[3][0],
        updates[3][1],
        updates[3][2],
        updates[4][0],
        updates[4][1],
        updates[4][2],
        updates[5][0],
        updates[5][1],
        updates[5][2],
        updates[6][0],
        updates[6][1],
        updates[6][2],
        updates[7][0],
        updates[7][1],
        updates[7][2],
        grad_vec[3] * factor,
    )


def solution(mesh):
    placed = (
        P("dp", None),
        P("dp"),
        P("dp", None),
        P("dp", "heads"),
        P(None, "dp"),
        P("dp", None, "heads"),
        P("heads", "dp"),
        P("dp", "heads"),
        P("heads", "dp"),
        P("dp", None),
        P(None, "dp"),
        P("dp", "heads"),
        P(None, "dp"),
        P("dp", None, "heads"),
        P("heads", "dp"),
        P("dp", "heads"),
        P("heads", "dp"),
        P("dp", None),
        P(None, "dp"),
        P("dp", "heads"),
        P(None, "dp"),
        P("dp", None, "heads"),
        P("heads", "dp"),
        P("dp", "heads"),
        P("heads", "dp"),
        P("dp", None),
        P(None, "dp"),
    )
    return jax.shard_map(
        per_device,
        mesh=mesh,
        in_specs=placed,
        out_specs=(
            P(),
            P(),
            P(),
            P("dp", "heads"),
            P("dp", "heads"),
            P("dp", "heads"),
            P(None, "dp"),
            P(None, "dp"),
            P(None, "dp"),
            P("dp", None, "heads"),
            P("dp", None, "heads"),
            P("dp", None, "heads"),
            P("heads", "dp"),
            P("heads", "dp"),
            P("heads", "dp"),
            P("dp", "heads"),
            P("dp", "heads"),
            P("dp", "heads"),
            P("heads", "dp"),
            P("heads", "dp"),
            P("heads", "dp"),
            P("dp", None),
            P("dp", None),
            P("dp", None),
            P(None, "dp"),
            P(None, "dp"),
            P(None, "dp"),
            P("dp"),
        ),
        check_vma=False,
    )
```

profile of v0, /device:TPU:0, one launch (start us, length us, event | category | flops | bytes accessed | tf_op | source)
XLA Modules:
  0.0 4002.3 jit_solution(17610172861436972796)
XLA Ops:
  12.7 375.0 %all-gather.12.cloned.1.call-done = bf16[768,12672]{1,0:T(8,128)(2,1)} async-done(((bf16[96,12672]{1,0:T(8,128)(2,1)}), bf16[768,12672]{1,0:T(8,128)(2,1)}) %all-gather.12.cloned.1.call-update) | async-done | bytes 19464208 | tf_op jit(solution)/shard_map/all_gather | solution.py:219
  387.7 26.1 copy.384
  413.8 17.5 gather_fusion
  436.2 30.5 all-gather
  467.5 26.4 reduce-scatter.24.cloned.1.call-done
  497.9 42.4 %all_gather.42 = bf16[768,3,192]{2,1,0:T(4,128)(2,1)S(1)} all-gather(bf16[96,3,192]{2,1,0:T(4,128)(2,1)S(1)} %copy.386), channel_id=1, replica_groups=mesh['dp'=8,'heads'=4] {'dp'}, dimensions={0}, use_global_device_ids=true | all-gather | bytes 995328 | tf_op jit(solution)/shard_map/all_gather | solution.py:205
  542.4 33.9 all_gather.44
  591.8 529.5 %while.33 = (s32[]{:T(128)}, bf16[4,512,3,64]{1,3,2,0:T(8,128)(2,1)}, f32[4,3,512]{2,1,0:T(4,128)}, bf16[4,512,3,64]{1,3,2,0:T(8,128)(2,1)}, s32[4]{0:T(128)S(1)...) while((s32[]{:T(128)}, ...), condition=%wide.region_8.9_spmd, body=%wide.region_5.8_spmd.sunk | while | flops 420051968 | bytes 196738416 | solution.py:249
  615.3 15.5 rev.29
  866.7 15.5 rev.29
  992.5 15.5 rev.29
  1012.2 15.5 rev.28
  1129.6 56.3 %reduce-scatter.26.cloned.1.call-done = f32[512,768]{1,0:T(8,128)} async-done(((f32[2048,768]{1,0:T(8,128)}), f32[512,768]{1,0:T(8,128)}) %reduce-scatter.26.cloned.1.call-update) | async-done | bytes 1572880 | tf_op jit(solution)/shard_map/reduce_scatter | solution.py:64
  1190.9 38.7 all-gather.20.cloned.1.call-done
  1229.6 29.5 all-gather.18.cloned.1.call-done
  1259.1 18.7 multiply_convert_fusion
  1277.7 25.2 all-gather.22.cloned.1.call-done
  1312.8 20.0 psum.43
  1334.7 32.9 reduce-scatter.28.cloned.1.call-done
  1371.3 40.3 %all-gather.24.cloned.1.call-done = bf16[768,768]{1,0:T(8,128)(2,1)} async-done(((bf16[96,768]{1,0:T(8,128)(2,1)}), bf16[768,768]{1,0:T(8,128)(2,1)}) %all-gather.24.cloned.1.call-update) | async-done | bytes 1179664 | tf_op jit(solution)/shard_map/all_gather | solution.py:209
  1427.5 27.4 all-gather.26.cloned.1.call-done
  1470.6 58.5 %reduce-scatter.30.cloned.1.call-done = f32[512,768]{1,0:T(8,128)} async-done(((f32[2048,768]{1,0:T(8,128)}), f32[512,768]{1,0:T(8,128)}) %reduce-scatter.30.cloned.1.call-update) | async-done | bytes 1572880 | tf_op jit(solution)/shard_map/reduce_scatter | solution.py:64
  1534.8 28.6 all-gather.28.cloned.1.call-done
  1570.2 1092.8 %while.34 = (s32[]{:T(128)}, f32[512,3,64]{0,2,1:T(8,128)}, f32[512,3,64]{0,2,1:T(8,128)}, bf16[4,512,3,64]{1,3,2,0:T(8,128)(2,1)}, bf16[4,512,3,64]{1,3,2,0:T(8...) while((s32[]{:T(128)}, f32[512,3,64]{0,2,1:T(8,128)}, ...), condition=%wide.region_35.36_spmd.clone, body=%wide.region_29.35_spmd.clone.sunk | while | flops 1345680896 | bytes 415093312 | solution.py:289
  1579.9 15.6 rev.31
  1739.2 22.5 rev.33
  1806.1 22.3 rev.32
  1850.9 15.6 rev.31
  2010.3 22.5 rev.33
  2077.4 22.3 rev.32
  2122.3 15.6 rev.31
  2281.8 22.5 rev.33
  2348.8 22.3 rev.32
  2393.8 15.6 rev.31
  2553.3 22.5 rev.33
  2620.3 22.3 rev.32
  2683.7 49.0 %reduce-scatter.32.cloned.1.call-done = f32[512,768]{1,0:T(8,128)} async-done(((f32[2048,768]{1,0:T(8,128)}), f32[512,768]{1,0:T(8,128)}) %reduce-scatter.32.cloned.1.call-update) | async-done | bytes 1572880 | tf_op jit(solution)/shard_map/reduce_scatter | solution.py:64
  2763.5 21.1 all-reduce.23.cloned.1.call-done
  2814.9 31.2 scatter_custom_fusion
  2846.1 39.0 copy.417
  2889.4 70.8 %reduce-scatter.36.cloned.1.call-done = f32[768,96]{0,1:T(8,128)} async-done(((f32[768,768]{0,1:T(8,128)}), f32[768,96]{0,1:T(8,128)}) %reduce-scatter.36.cloned.1.call-update) | async-done | bytes 294928 | tf_op jit(solution)/shard_map/reduce_scatter | solution.py:339
  2961.9 63.6 %reduce-scatter.44.cloned.1.call-done = f32[96,192]{1,0:T(8,128)} async-done(((f32[768,192]{1,0:T(8,128)}), f32[96,192]{1,0:T(8,128)}) %reduce-scatter.44.cloned.1.call-update) | async-done | bytes 73744
  3027.1 68.2 %reduce-scatter.42.cloned.1.call-done = f32[96,576]{1,0:T(8,128)} async-done(((f32[768,576]{1,0:T(8,128)}), f32[96,576]{1,0:T(8,128)}) %reduce-scatter.42.cloned.1.call-update) | async-done | bytes 221200
  3097.0 65.8 %reduce-scatter.46.cloned.1.call-done = f32[96,512]{1,0:T(8,128)} async-done(((f32[768,512]{1,0:T(8,128)}), f32[96,512]{1,0:T(8,128)}) %reduce-scatter.46.cloned.1.call-update) | async-done | bytes 196624
  3164.5 70.6 %reduce-scatter.38.cloned.1.call-done = f32[96,768]{1,0:T(8,128)} async-done(((f32[768,768]{1,0:T(8,128)}), f32[96,768]{1,0:T(8,128)}) %reduce-scatter.38.cloned.1.call-update) | async-done | bytes 294928 | tf_op jit(solution)/shard_map/reduce_scatter | solution.py:340
  3238.0 60.8 %reduce-scatter.48.cloned.1.call-done = f32[96,11]{1,0:T(8,128)} async-done(((f32[768,11]{1,0:T(8,128)}), f32[96,11]{1,0:T(8,128)}) %reduce-scatter.48.cloned.1.call-update) | async-done | bytes 4240
  3301.0 616.5 %reduce-scatter.40.cloned.1.call-done = f32[96,12672]{1,0:T(8,128)} async-done(((f32[768,12672]{1,0:T(8,128)}), f32[96,12672]{1,0:T(8,128)}) %reduce-scatter.40.cloned.1.call-update) | async-done | bytes 4866064 | tf_op jit(solution)/shard_map/reduce_scatter | solution.py:319
  3931.4 39.9 all-reduce.19
  (916 shorter events, 1514.8 us)
Async XLA Ops:
  7.2 380.5 %all-gather.12.cloned.1.call-start = ((), (), s32[]{:S(2)}) async-start(), calls=%async_computation.13 | async-start | bytes 21897216 | tf_op jit(solution)/shard_map/all_gather | solution.py:219
  11.3 482.5 %reduce-scatter.24.cloned.1.call-start = ((), (), s32[]{:S(2)}) async-start(), calls=%async_computation.14 | async-start | bytes 7864320 | tf_op jit(solution)/shard_map/reduce_scatter | solution.py:64
  12.0 419.3 %copy-start.105 = (pred[1,4,4,128]{3,1,2,0:T(4,128)(4,1)}, pred[1,4,4,128]{3,1,2,0:T(4,128)(4,1)S(1)}, u32[]{:S(2)}) copy-start(pred[1,4,4,128]{3,1,2,0:T(4,128)(4,1)S(1)} %copy.447) | copy-start | bytes 6148
  435.4 140.9 %all-gather.16.cloned.1.call-start = ((), (), s32[]{:S(2)}) async-start(), calls=%async_computation.16 | async-start | bytes 1769472 | tf_op jit(solution)/shard_map/all_gather | solution.py:212
  436.1 145.2 %all-gather.14.cloned.1.call-start = ((), (), s32[]{:S(2)}) async-start(), calls=%async_computation.15 | async-start | bytes 3932160 | tf_op jit(solution)/shard_map/all_gather | solution.py:60
  467.5 30.0 copy-start.67
  467.5 30.0 copy-start.85
  467.5 111.6 %copy-start.76 = (f32[768]{0:T(1024)}, f32[768]{0:T(1024)S(1)}, u32[]{:S(2)}) copy-start(f32[768]{0:T(1024)S(1)} %get-tuple-element.608) | copy-start | bytes 9220
  497.5 688.3 %reduce-scatter.26.cloned.1.call-start = ((), (), s32[]{:S(2)}) async-start(), calls=%async_computation.17 | async-start | bytes 7864320 | tf_op jit(solution)/shard_map/reduce_scatter | solution.py:64
  1127.8 58.0 %copy-start.9 = (f32[512,768]{1,0:T(8,128)S(1)}, f32[512,768]{1,0:T(8,128)}, u32[]{:S(2)}) copy-start(f32[512,768]{1,0:T(8,128)} %reduce-scatter.24.cloned.1.call-done) | copy-start | bytes 4718596
  1127.8 58.0 %copy-start.68 = (f32[768]{0:T(1024)S(1)}, f32[768]{0:T(1024)}, u32[]{:S(2)}) copy-start(f32[768]{0:T(1024)} %copy-done.67) | copy-start | bytes 9220
  1127.8 58.0 %copy-start.74 = (f32[512]{0:T(512)S(1)}, f32[512]{0:T(512)}, u32[]{:S(2)}) copy-start(f32[512]{0:T(512)} %copy-done.73) | copy-start | bytes 6148
  1127.9 58.0 %copy-start.79 = (f32[512]{0:T(512)S(1)}, f32[512]{0:T(512)}, u32[]{:S(2)}) copy-start(f32[512]{0:T(512)} %copy-done.78) | copy-start | bytes 6148
  1127.9 101.7 %all-gather.20.cloned.1.call-start = ((), (), s32[]{:S(2)}) async-start(), calls=%async_computation.19 | async-start | bytes 1327104 | tf_op jit(solution)/shard_map/all_gather | solution.py:207
  1129.5 58.6 %copy-start.70 = (f32[768]{0:T(1024)S(1)}, f32[768]{0:T(1024)}, u32[]{:S(2)}) copy-start(f32[768]{0:T(1024)} %get-tuple-element.606) | copy-start | bytes 9220
  1129.5 129.5 %all-gather.18.cloned.1.call-start = ((), (), s32[]{:S(2)}) async-start(), calls=%async_computation.18 | async-start | bytes 3932160 | tf_op jit(solution)/shard_map/all_gather | solution.py:60
  1190.1 112.8 %all-gather.22.cloned.1.call-start = ((), (), s32[]{:S(2)}) async-start(), calls=%async_computation.20 | async-start | bytes 1327104 | tf_op jit(solution)/shard_map/all_gather | solution.py:208
  1190.9 176.8 %reduce-scatter.28.cloned.1.call-start = ((), (), s32[]{:S(2)}) async-start(), calls=%async_computation.21 | async-start | bytes 7864320 | tf_op jit(solution)/shard_map/reduce_scatter | solution.py:64
  1310.4 57.3 %copy-start.84 = (f32[768]{0:T(1024)S(1)}, f32[768]{0:T(1024)}, u32[]{:S(2)}) copy-start(f32[768]{0:T(1024)} %get-tuple-element.605) | copy-start | bytes 9220
  1310.4 101.2 %all-gather.24.cloned.1.call-start = ((), (), s32[]{:S(2)}) async-start(), calls=%async_computation.22 | async-start | bytes 1327104 | tf_op jit(solution)/shard_map/all_gather | solution.py:209
  1312.0 142.9 %all-gather.26.cloned.1.call-start = ((), (), s32[]{:S(2)}) async-start(), calls=%async_computation.23 | async-start | bytes 3932160 | tf_op jit(solution)/shard_map/all_gather | solution.py:60
  1369.6 55.0 %copy-start.16 = (f32[512,768]{1,0:T(8,128)}, f32[512,768]{1,0:T(8,128)S(1)}, u32[]{:S(2)}) copy-start(f32[512,768]{1,0:T(8,128)S(1)} %get-tuple-element.700) | copy-start | bytes 4718596
  1369.6 55.0 %copy-start.92 = (f32[512]{0:T(512)}, f32[512]{0:T(512)S(1)}, u32[]{:S(2)}) copy-start(f32[512]{0:T(512)S(1)} %broadcast_multiply_fusion.1) | copy-start | bytes 6148
  1425.3 29.7 copy-start.129
  1427.5 101.6 %reduce-scatter.30.cloned.1.call-start = ((), (), s32[]{:S(2)}) async-start(), calls=%async_computation.24 | async-start | bytes 7864320 | tf_op jit(solution)/shard_map/reduce_scatter | solution.py:64
  1470.5 58.6 %copy-start.21 = (f32[512,768]{1,0:T(8,128)S(1)}, f32[512,768]{1,0:T(8,128)}, u32[]{:S(2)}) copy-start(f32[512,768]{1,0:T(8,128)} %copy-done.20) | copy-start | bytes 4718596
  1470.6 61.4 %copy-start.99 = (f32[512]{0:T(512)S(1)}, f32[512]{0:T(512)}, u32[]{:S(2)}) copy-start(f32[512]{0:T(512)} %copy-done.98) | copy-start | bytes 6148
  1470.6 92.9 %all-gather.28.cloned.1.call-start = ((), (), s32[]{:S(2)}) async-start(), calls=%async_computation.25 | async-start | bytes 3932160 | tf_op jit(solution)/shard_map/all_gather | solution.py:60
  1532.6 30.9 copy-start.28
  1532.6 33.9 copy-start.102
  1534.8 1197.9 %reduce-scatter.32.cloned.1.call-start = ((), (), s32[]{:S(2)}) async-start(), calls=%async_computation.26 | async-start | bytes 7864320 | tf_op jit(solution)/shard_map/reduce_scatter | solution.py:64
  2674.2 110.4 %all-reduce.23.cloned.1.call-start = ((), (), s32[]{:S(2)}) async-start(), calls=%async_computation.36 | async-start | bytes 3932160 | tf_op jit(solution)/shard_map/psum | solution.py:323
  2682.4 50.2 %copy-start.10 = (f32[512,768]{1,0:T(8,128)S(1)}, f32[512,768]{1,0:T(8,128)}, u32[]{:S(2)}) copy-start(f32[512,768]{1,0:T(8,128)} %reduce-scatter.24.cloned.1.call-done) | copy-start | bytes 4718596
  2682.5 50.2 %copy-start.19 = (f32[512,768]{1,0:T(8,128)S(1)}, f32[512,768]{1,0:T(8,128)}, u32[]{:S(2)}) copy-start(f32[512,768]{1,0:T(8,128)} %copy-done.18) | copy-start | bytes 4718596
  2682.5 50.2 %copy-start.69 = (f32[768]{0:T(1024)S(1)}, f32[768]{0:T(1024)}, u32[]{:S(2)}) copy-start(f32[768]{0:T(1024)} %copy-done.67) | copy-start | bytes 9220
  2682.5 50.2 %copy-start.75 = (f32[512]{0:T(512)S(1)}, f32[512]{0:T(512)}, u32[]{:S(2)}) copy-start(f32[512]{0:T(512)} %copy-done.73) | copy-start | bytes 6148
  2682.5 50.2 %copy-start.80 = (f32[512]{0:T(512)S(1)}, f32[512]{0:T(512)}, u32[]{:S(2)}) copy-start(f32[512]{0:T(512)} %copy-done.78) | copy-start | bytes 6148
  2682.5 50.2 %copy-start.103 = (f32[512]{0:T(512)S(1)}, f32[512]{0:T(512)}, u32[]{:S(2)}) copy-start(f32[512]{0:T(512)} %copy-done.102) | copy-start | bytes 6148
  2683.6 51.3 %copy-start.95 = (f32[512]{0:T(512)S(1)}, f32[512]{0:T(512)}, u32[]{:S(2)}) copy-start(f32[512]{0:T(512)} %copy-done.94) | copy-start | bytes 6148
  2683.6 131.3 %all-gather.30.cloned.1.call-start = ((), (), s32[]{:S(2)}) async-start(), calls=%async_computation.27 | async-start | bytes 3932160 | tf_op jit(solution)/shard_map/all_gather | solution.py:316
  2736.7 151.0 %reduce-scatter.34.cloned.1.call-start = ((), (), s32[]{:S(2)}) async-start(), calls=%async_computation.28 | async-start | bytes 2654208 | tf_op jit(solution)/shard_map/reduce_scatter | solution.py:338
  2743.8 216.4 %reduce-scatter.36.cloned.1.call-start = ((), (), s32[]{:S(2)}) async-start(), calls=%async_computation.29 | async-start | bytes 2654208 | tf_op jit(solution)/shard_map/reduce_scatter | solution.py:339
  2750.9 274.6 %reduce-scatter.44.cloned.1.call-start = ((), (), s32[]{:S(2)}) async-start(), calls=%async_computation.33 | async-start | bytes 884736
  2756.1 339.1 %reduce-scatter.42.cloned.1.call-start = ((), (), s32[]{:S(2)}) async-start(), calls=%async_computation.32 | async-start | bytes 2211840
  2763.5 399.3 %reduce-scatter.46.cloned.1.call-start = ((), (), s32[]{:S(2)}) async-start(), calls=%async_computation.34 | async-start | bytes 1769472
  2787.3 447.8 %reduce-scatter.38.cloned.1.call-start = ((), (), s32[]{:S(2)}) async-start(), calls=%async_computation.30 | async-start | bytes 2654208 | tf_op jit(solution)/shard_map/reduce_scatter | solution.py:340
  2789.0 509.9 %reduce-scatter.48.cloned.1.call-start = ((), (), s32[]{:S(2)}) async-start(), calls=%async_computation.35 | async-start | bytes 442368
  2801.6 1115.8 %reduce-scatter.40.cloned.1.call-start = ((), (), s32[]{:S(2)}) async-start(), calls=%async_computation.31 | async-start | bytes 43794432 | tf_op jit(solution)/shard_map/reduce_scatter | solution.py:319
  (161 other events, 546.1 us)
Sparse Core Ops, SparseCore 0:
  11.5 376.2 all-gather.11
  435.5 58.3 reduce-scatter.23
  496.3 55.5 all-gather.15
  554.0 26.7 all-gather.13
  1128.0 57.8 reduce-scatter.25
  1188.5 41.0 all-gather.19
  1231.7 27.2 all-gather.17
  1261.8 41.0 all-gather.21
  1310.5 57.1 reduce-scatter.27
  1370.5 41.0 all-gather.23
  1427.6 27.3 all-gather.25
  1470.7 58.3 reduce-scatter.29
  1534.9 28.5 all-gather.27
  2674.3 58.3 reduce-scatter.31
  2735.1 49.4 all-reduce.22
  2786.0 28.8 all-gather.29
  2818.7 69.0 reduce-scatter.33
  2892.1 68.0 reduce-scatter.35
  2963.9 61.5 reduce-scatter.43
  3029.3 65.8 reduce-scatter.41
  3099.0 63.7 reduce-scatter.45
  3166.9 68.1 reduce-scatter.37
  3238.4 60.4 reduce-scatter.47
  3302.6 614.7 reduce-scatter.39
where the time goes:
time: 4020 us; the launch traced here: 4000 us
  waiting for transfers between devices  1840 us (46%)
  local copies, waits for them, and re-layouts  1460 us (36%)
  matrix products  285 us (7%)
  other arithmetic  182 us (5%)
  blocking collectives  178 us (4%)
    reduce_scatter x1, waiting for transfers between devices, per_device(): lax.psum_scatter(add_rows(word_grads, flat_ids, holder, vocab_slab), 'dp'...  616 us
    rev x24, local copies, waits for them, and re-layouts, rel_skew(): table[:, :, ::-1]  427 us
    all_gather x1, waiting for transfers between devices, per_device(): lax.all_gather(embedding.astype(low_type), 'dp', axis=0, tiled=True)  375 us
    reshape x24, local copies, waits for them, and re-layouts, rel_skew(): return window.reshape(head_count, seq_len, 2 * seq_len - 1)[:, :, :seq_len]  318 us
    unnamed x28, waiting for transfers between devices  259 us
    reduce_scatter x5, waiting for transfers between devices, collect_rows(): return lax.psum_scatter(values, 'heads', scatter_dimension=0, tiled=True)  223 us
    while x172, local copies, waits for them, and re-layouts  187 us
    concatenate x24, local copies, waits for them, and re-layouts, rel_skew(): jnp.concatenate([low_end, table[:, :, ::-1], high_end, padding], 2)  110 us
  transfers between devices with their start and end apart: 24, of which 22 were waited for; matrix products, arithmetic and copies ran while one was open for 4% of the time, Pallas kernels for 0%

commit v1 on v0

v1 whole, which is shorter than its diff:
```python
import jax
import jax.numpy as jnp
from jax import lax
from jax.experimental import pallas as pl
from jax.experimental.pallas import tpu as pltpu
from jax.sharding import PartitionSpec as P

HEAD_DIM = 64
STEP = 10
BLOCK = 128
UNROLL = 8

low = jnp.bfloat16
f32 = jnp.float32

layer_eps = 1e-07
clip_level = 0.005
rate_steps = (0.1, 0.05, 0.05, 0.05, 0.05, 0.05, 0.05, 1.0)
beta_first = 0.9
beta_second = 0.999
adam_eps = 1e-08
weight_decay = 0.01

def dot_rows(a,b):
    return lax.dot_general(a,b,(((1,),(1,)),((),())),preferred_element_type=f32)
def dot_plain(a,b):
    return lax.dot_general(a,b,(((1,),(0,)),((),())),preferred_element_type=f32)
def dot_left(a,b):
    return lax.dot_general(a,b,(((0,),(0,)),((),())),preferred_element_type=f32)

def attend_kernel(length_ref, qkv_ref, table_ref, probs_ref, mixed_ref, far_ref):
    seq=qkv_ref.shape[1]; width=qkv_ref.shape[2]//3; heads=width//HEAD_DIM
    blocks=seq//BLOCK
    scale=(3*HEAD_DIM)**-0.5
    length=length_ref[0]
    live=lax.broadcasted_iota(jnp.int32,(BLOCK,seq),1)<length
    for head in range(heads):
        at=head*HEAD_DIM
        q=qkv_ref[0,:,at:at+HEAD_DIM]
        k=qkv_ref[0,:,width+at:width+at+HEAD_DIM]
        v=qkv_ref[0,:,2*width+at:2*width+at+HEAD_DIM]
        for block in range(blocks):
            rows=slice(block*BLOCK,(block+1)*BLOCK)
            start=seq-BLOCK*(block+1)
            far=dot_rows(k[rows],table_ref[0,start:start+seq+BLOCK,at:at+HEAD_DIM])
            far=pltpu.roll(far,seq,1,stride=1,stride_axis=0)[:,:seq]
            far_ref[head,:,rows]=far.T
        for block in range(blocks):
            rows=slice(block*BLOCK,(block+1)*BLOCK)
            start=seq-BLOCK*(block+1)
            near=dot_rows(q[rows],table_ref[0,start:start+seq+BLOCK,width+at:width+at+HEAD_DIM])
            near=pltpu.roll(near,seq,1,stride=1,stride_axis=0)[:,:seq]
            scores=(dot_rows(q[rows],k)+near+far_ref[head,rows,:])*scale
            scores=jnp.where(live,scores,-1e9)
            top=jnp.max(scores,-1,keepdims=True)
            expo=jnp.exp(scores-top)
            probs=(expo*(1.0/jnp.sum(expo,-1,keepdims=True))).astype(low)
            probs_ref[head,rows,:]=probs
            mixed_ref[0,rows,at:at+HEAD_DIM]=dot_plain(probs,v).astype(low)

def attend(length,qkv,table):
    groups,seq,width3=qkv.shape
    width=width3//3; heads=width//HEAD_DIM
    return pl.pallas_call(
        attend_kernel,
        grid=(groups,),
        in_specs=[pl.BlockSpec(memory_space=pltpu.SMEM),
            pl.BlockSpec((1,seq,width3),lambda g:(g,0,0)),
            pl.BlockSpec((1,2*seq,2*width),lambda g:(g,0,0))],
        out_specs=[pl.BlockSpec((heads,seq,seq),lambda g:(g,0,0)),
            pl.BlockSpec((1,seq,width),lambda g:(g,0,0))],
        out_shape=[jax.ShapeDtypeStruct((groups*heads,seq,seq),low),jax.ShapeDtypeStruct((groups,seq,width),low)],
        scratch_shapes=[pltpu.VMEM((heads,seq,seq),f32)],
        compiler_params=pltpu.CompilerParams(vmem_limit_bytes=48<<20),
        name="attend",
    )(length,qkv,table)

def attend_back_kernel(qkv_ref, table_ref, probs_ref, up_ref, grad_ref, rel_ref, low_ref, sum_ref):
    seq=qkv_ref.shape[1]; width=qkv_ref.shape[2]//3; heads=width//HEAD_DIM
    blocks=seq//BLOCK; reach=seq+BLOCK
    scale=(3*HEAD_DIM)**-0.5
    flip=(lax.broadcasted_iota(jnp.int32,(BLOCK,BLOCK),0)+lax.broadcasted_iota(jnp.int32,(BLOCK,BLOCK),1)==BLOCK-1).astype(f32).astype(low)
    edge=jnp.zeros((BLOCK,BLOCK),f32)
    def shear(rows):
        return pltpu.roll(jnp.concatenate([rows,edge],1),1,1,stride=1,stride_axis=0).astype(low)
    for head in range(heads):
        at=head*HEAD_DIM
        q=qkv_ref[0,:,at:at+HEAD_DIM]
        k=qkv_ref[0,:,width+at:width+at+HEAD_DIM]
        v=qkv_ref[0,:,2*width+at:2*width+at+HEAD_DIM]
        up=up_ref[0,:,at:at+HEAD_DIM]
        for block in range(blocks):
            rows=slice(block*BLOCK,(block+1)*BLOCK)
            probs=probs_ref[head,rows,:].astype(f32)
            pull=dot_rows(up[rows],v)
            inner=jnp.sum(probs*pull,-1,keepdims=True)
            low_ref[head,rows,:]=(probs*(pull-inner)*scale).astype(low)
        grad_ref[0,:,2*width+at:2*width+at+HEAD_DIM]=dot_left(up,probs_ref[head]).T.astype(low)
        sum_ref[2*head]=jnp.zeros(sum_ref.shape[1:],f32)
        sum_ref[2*head+1]=jnp.zeros(sum_ref.shape[1:],f32)
        for block in range(blocks):
            rows=slice(block*BLOCK,(block+1)*BLOCK)
            start=seq-BLOCK*(block+1)
            window=slice(start,start+reach)
            turned=dot_plain(flip,low_ref[head,rows,:])
            near=shear(turned)
            grad_q=dot_plain(turned.astype(low),k)+dot_plain(near,table_ref[0,window,width+at:width+at+HEAD_DIM])
            grad_ref[0,rows,at:at+HEAD_DIM]=dot_plain(flip,grad_q.astype(low)).astype(low)
            q_turned=dot_plain(flip,q[rows]).astype(low)
            sum_ref[2*head+1,:,window]+=dot_left(q_turned,near)
            turned=dot_rows(flip,low_ref[head,:,rows])
            far=shear(turned)
            grad_k=dot_plain(turned.astype(low),q)+dot_plain(far,table_ref[0,window,at:at+HEAD_DIM])
            grad_ref[0,rows,width+at:width+at+HEAD_DIM]=dot_plain(flip,grad_k.astype(low)).astype(low)
            k_turned=dot_plain(flip,k[rows]).astype(low)
            sum_ref[2*head,:,window]+=dot_left(k_turned,far)
        rel_ref[0,:,at:at+HEAD_DIM]=sum_ref[2*head].T.astype(low)
        rel_ref[0,:,width+at:width+at+HEAD_DIM]=sum_ref[2*head+1].T.astype(low)

def attend_back(qkv,table,probs,up):
    groups,seq,width3=qkv.shape
    width=width3//3; heads=width//HEAD_DIM
    return pl.pallas_call(
        attend_back_kernel,
        grid=(groups,),
        in_specs=[
            pl.BlockSpec((1,seq,width3),lambda g:(g,0,0)),
            pl.BlockSpec((1,2*seq,2*width),lambda g:(g,0,0)),
            pl.BlockSpec((heads,seq,seq),lambda g:(g,0,0)),
            pl.BlockSpec((1,seq,width),lambda g:(g,0,0))],
        out_specs=[pl.BlockSpec((1,seq,width3),lambda g:(g,0,0)),
            pl.BlockSpec((1,2*seq,2*width),lambda g:(g,0,0))],
        out_shape=[jax.ShapeDtypeStruct((groups,seq,width3),low),jax.ShapeDtypeStruct((groups,2*seq,2*width),low)],
        scratch_shapes=[pltpu.VMEM((heads,seq,seq),low),pltpu.VMEM((2*heads,HEAD_DIM,2*seq),f32)],
        compiler_params=pltpu.CompilerParams(vmem_limit_bytes=48<<20),
        name="attend_back",
    )(qkv,table,probs,up)


def lookup_kernel(lengths_ref, places_ref, table_ref, words_ref, rows_ref):
    rows_ref[...] = jnp.zeros_like(rows_ref)

    def step(index, carry):
        first = pl.multiple_of(index * UNROLL, UNROLL)
        for offset in range(UNROLL):
            place = places_ref[0, 0, first + offset]
            rows_ref[pl.ds(first + offset, 1), :] = table_ref[pl.ds(place, 1), :]
        return carry

    lax.fori_loop(0, pl.cdiv(lengths_ref[pl.program_id(0)], UNROLL), step, 0)
    words_ref[0] = rows_ref[...].astype(low)


def lookup(lengths, places, table):
    rows, seq = places.shape
    width = table.shape[1]
    return pl.pallas_call(
        lookup_kernel,
        grid=(rows,),
        in_specs=[
            pl.BlockSpec(memory_space=pltpu.SMEM),
            pl.BlockSpec((1, 1, seq), lambda row: (row, 0, 0), memory_space=pltpu.SMEM),
            pl.BlockSpec(table.shape, lambda row: (0, 0)),
        ],
        out_specs=pl.BlockSpec((1, seq, width), lambda row: (row, 0, 0)),
        out_shape=jax.ShapeDtypeStruct((rows, seq, width), low),
        scratch_shapes=[pltpu.VMEM((seq, width), f32)],
        compiler_params=pltpu.CompilerParams(vmem_limit_bytes=48 << 20),
        name="lookup",
    )(lengths, places[:, None], table)


def deposit_kernel(lengths_ref, places_ref, grads_ref, total_ref, rows_ref, *parts):
    tables = (total_ref,) + parts

    @pl.when(pl.program_id(0) == 0)
    def clear():
        for table in tables:
            table[...] = jnp.zeros_like(table)

    rows_ref[...] = grads_ref[0].astype(f32)

    def step(index, carry):
        first = pl.multiple_of(index * UNROLL, UNROLL)
        for offset in range(0, UNROLL, len(tables)):
            places = [places_ref[0, 0, first + offset + part] for part in range(len(tables))]
            sums = [
                table[pl.ds(place, 1), :] + rows_ref[pl.ds(first + offset + part, 1), :]
                for part, (place, table) in enumerate(zip(places, tables))
            ]
            for place, table, value in zip(places, tables, sums):
                table[pl.ds(place, 1), :] = value
        return carry

    lax.fori_loop(0, pl.cdiv(lengths_ref[pl.program_id(0)], UNROLL), step, 0)

    @pl.when(pl.program_id(0) == pl.num_programs(0) - 1)
    def finish():
        for part in parts:
            total_ref[...] += part[...]


def deposit(lengths, places, grads, slots):
    rows, seq = places.shape
    width = grads.shape[2]
    return pl.pallas_call(
        deposit_kernel,
        grid=(rows,),
        in_specs=[
            pl.BlockSpec(memory_space=pltpu.SMEM),
            pl.BlockSpec((1, 1, seq), lambda row: (row, 0, 0), memory_space=pltpu.SMEM),
            pl.BlockSpec((1, seq, width), lambda row: (row, 0, 0)),
        ],
        out_specs=pl.BlockSpec((slots, width), lambda row: (0, 0)),
        out_shape=jax.ShapeDtypeStruct((slots, width), f32),
        scratch_shapes=[pltpu.VMEM((seq, width), f32)] + [pltpu.VMEM((slots, width), f32)] * 3,
        compiler_params=pltpu.CompilerParams(vmem_limit_bytes=56 << 20),
        name="deposit",
    )(lengths, places[:, None], grads)


def matmul(matrix, operand):
    return jnp.dot(matrix, operand, preferred_element_type=f32)


def product(form, matrix, operand):
    return jnp.einsum(form, matrix, operand, preferred_element_type=f32)


def normalize(values, gain_row, bias_row):
    center = values - jnp.mean(values, -1, keepdims=True)
    spread_sq = jnp.mean(center * center, -1, keepdims=True)
    return center * lax.rsqrt(spread_sq + layer_eps) * gain_row + bias_row


def gelu(values):
    return jax.nn.gelu(values, approximate=False)


def norm_at(first_row):
    def apply_norm(values, gain_rows):
        return normalize(values, gain_rows[first_row], gain_rows[first_row + 1])

    return apply_norm


def split_terms(values, count):
    terms = []
    for _ in range(count):
        term = lax.reduce_precision(values, 8, 7)
        terms.append(term.astype(low))
        values = values - term
    return terms


def adamw(weight, gradient, mean, square, rate_now):
    first = beta_first * mean + (1.0 - beta_first) * gradient
    second = beta_second * square + (1.0 - beta_second) * gradient * gradient
    mean_hat = first / (1.0 - beta_first**STEP)
    square_hat = second / (1.0 - beta_second**STEP)
    master = weight - rate_now * (
        mean_hat / (jnp.sqrt(square_hat) + adam_eps) + weight_decay * weight
    )
    return (first, second, master)


def per_device(
    token_ids,
    row_lengths,
    replaced,
    embedding,
    relative,
    project,
    combine,
    expand,
    contract,
    readout,
    vectors,
    embedding_mean,
    relative_mean,
    project_mean,
    combine_mean,
    expand_mean,
    contract_mean,
    readout_mean,
    vectors_mean,
    embedding_square,
    relative_square,
    project_square,
    combine_square,
    expand_square,
    contract_square,
    readout_square,
    vectors_square,
):
    pieces = lax.axis_size("heads")
    holder = lax.axis_index("heads")
    owner = lax.axis_index("dp")
    owners = lax.axis_size("dp")
    row_count, seq_len = token_ids.shape
    width = vectors.shape[1]
    model = width * owners
    everyone = ("heads", "dp")
    head_width = project.shape[2]
    hidden = expand.shape[1]
    vocab_slab = embedding.shape[1]
    span_part = relative.shape[0] // pieces
    vector_count = vectors.shape[0]

    row_facts = lax.all_gather(
        jnp.concatenate([token_ids, row_lengths[:, None]], 1), "dp", axis=0, tiled=True
    )
    all_ids, all_lengths = row_facts[:, :seq_len], row_facts[:, seq_len]
    token_total = jnp.sum(all_lengths).astype(f32)
    local_ids = all_ids - holder * vocab_slab
    inside = (local_ids >= 0) & (local_ids < vocab_slab)
    places = jnp.where(inside, local_ids, vocab_slab)
    slots = vocab_slab + 8

    own_relative = lax.dynamic_slice_in_dim(relative, holder * span_part, span_part, 0).T
    own_readout = lax.dynamic_slice_in_dim(readout, holder * head_width, head_width, 1)
    vector_terms = jnp.concatenate(split_terms(vectors.T, 3), 1)
    first_pack = jnp.concatenate(
        [
            project.reshape(width, 3 * head_width).astype(low),
            combine.T.astype(low),
            *split_terms(own_relative, 2),
            jnp.pad(vector_terms, ((0, 0), (0, BLOCK - 3 * vector_count))),
        ],
        1,
    )
    second_pack = jnp.concatenate(
        [expand.astype(low), contract.T.astype(low), own_readout.astype(low)], 1
    )
    first_all = lax.all_gather(first_pack, everyone, axis=0, tiled=True)
    first_all = first_all.reshape(pieces, model, -1)
    second_all = lax.all_gather(second_pack, everyone, axis=0, tiled=True)
    second_all = second_all.reshape(pieces, model, -1)

    w_project = first_all[:, :, : 3 * head_width]
    w_combine = first_all[:, :, 3 * head_width : 4 * head_width]
    at = 4 * head_width
    rel_terms = first_all[:, :, at : at + 2 * span_part].astype(f32)
    rel_full = rel_terms[:, :, :span_part] + rel_terms[:, :, span_part:]
    rel_full = rel_full.transpose(0, 2, 1).reshape(pieces * span_part, model)
    at = at + 2 * span_part
    vec_terms = first_all[0, :, at : at + 3 * vector_count].astype(f32)
    vec_full = (
        vec_terms[:, :vector_count]
        + vec_terms[:, vector_count : 2 * vector_count]
        + vec_terms[:, 2 * vector_count :]
    ).T
    w_expand = second_all[:, :, :hidden]
    w_contract = second_all[:, :, hidden : 2 * hidden]
    w_readout = second_all[:, :, 2 * hidden :]

    table = jnp.pad(embedding.T, ((0, 8), (0, 0)))
    found = lookup(all_lengths, places, table).reshape(owners, row_count, seq_len, width)
    found = lax.psum_scatter(found, "heads", scatter_dimension=1, tiled=True)
    found = found.reshape(owners, seq_len, width)
    found = lax.all_to_all(found, "dp", 0, 0, tiled=True)
    word_rows = found.transpose(1, 0, 2).reshape(seq_len, model).astype(f32)

    own_length = lax.dynamic_slice_in_dim(row_lengths, holder, 1)
    own_live = jnp.arange(seq_len) < own_length
    own_flags = lax.dynamic_slice_in_dim(replaced, holder, 1)[0].astype(f32)

    hidden_in, back_in = jax.vjp(norm_at(0), word_rows, vec_full)
    hidden_low = hidden_in.astype(low)
    qkv = product("td,hdc->htc", hidden_low, w_project).astype(low)
    rel_norm, back_rel = jax.vjp(norm_at(2), rel_full, vec_full)
    rel_low = rel_norm.astype(low)
    entries = rel_full.shape[0]
    reach = jnp.clip(seq_len + entries // 2 - jnp.arange(2 * seq_len), 0, entries - 1)
    spread = (reach[:, None] == jnp.arange(entries)[None, :]).astype(low)
    rel_rows = matmul(spread, rel_low).astype(low)
    rel_table = product("ud,hdc->huc", rel_rows, w_project[:, :, : 2 * head_width]).astype(low)
    probs, mixed = attend(own_length, qkv, rel_table)
    attended = product("htc,hdc->td", mixed, w_combine)
    hidden_mid, back_mid = jax.vjp(norm_at(4), hidden_in + attended, vec_full)
    mid_low = hidden_mid.astype(low)
    gate_in = product("td,hdf->htf", mid_low, w_expand)
    gate_act, back_gate = jax.vjp(gelu, gate_in)
    gate_low = gate_act.astype(low)
    ffn_out = product("htf,hdf->td", gate_low, w_contract)
    hidden_out, back_out = jax.vjp(norm_at(6), hidden_mid + ffn_out, vec_full)
    out_low = hidden_out.astype(low)
    w_readout = w_readout.transpose(1, 0, 2).reshape(model, model)
    dense_out = matmul(out_low, w_readout)

    def head_loss(dense_rows, gain_rows):
        head_norm = normalize(gelu(dense_rows), gain_rows[8], gain_rows[9])
        logits = jnp.sum(head_norm * gain_rows[10], -1)
        losses = jax.nn.softplus(logits) - own_flags * logits
        return jnp.sum(jnp.where(own_live, losses, 0.0))

    loss_part, back_head = jax.vjp(head_loss, dense_out, vec_full)
    grad_dense, grad_vec = back_head(1.0 / token_total)
    dense_low = grad_dense.astype(low)
    grad_readout = product(
        "td,thc->hdc", out_low, dense_low.reshape(seq_len, pieces, head_width)
    ).astype(low)
    grad_sum, grad_gain = back_out(product("tc,dc->td", dense_low, w_readout))
    grad_vec = grad_vec + grad_gain
    ffn_low = grad_sum.astype(low)
    grad_contract = product("td,htf->hdf", ffn_low, gate_low).astype(low)
    gate_grad = back_gate(product("td,hdf->htf", ffn_low, w_contract))[0].astype(low)
    grad_expand = product("td,htf->hdf", mid_low, gate_grad).astype(low)
    grad_mid = grad_sum + product("htf,hdf->td", gate_grad, w_expand)
    grad_sum, grad_gain = back_mid(grad_mid)
    grad_vec = grad_vec + grad_gain
    attend_low = grad_sum.astype(low)
    grad_mixed = product("td,hdc->htc", attend_low, w_combine).astype(low)
    grad_combine = product("td,htc->hdc", attend_low, mixed).astype(low)

    early = jnp.concatenate([grad_expand, grad_contract, grad_readout, grad_combine], 2)
    early = lax.psum_scatter(
        early.reshape(pieces * model, -1), everyone, scatter_dimension=0, tiled=True
    )

    qkv_grads, rel_table_grads = attend_back(qkv, rel_table, probs, grad_mixed)
    rel_grads = product("ur,huc->hrc", spread, rel_table_grads).astype(low)
    grad_hidden = grad_sum + product("htc,hdc->td", qkv_grads, w_project)
    grad_words, grad_gain = back_in(grad_hidden)
    grad_vec = grad_vec + grad_gain
    sent = grad_words.astype(low).reshape(seq_len, owners, width).transpose(1, 0, 2)
    sent = lax.all_to_all(sent, "dp", 0, 0, tiled=True)
    sent = lax.all_gather(sent[:, None], "heads", axis=1, tiled=True)
    sent = sent.reshape(owners * row_count, seq_len, width)
    grad_project = product("td,htc->hdc", hidden_low, qkv_grads)
    grad_rel_part = product("rd,hrc->hdc", rel_low, rel_grads)
    grad_project = jnp.concatenate(
        [
            grad_project[:, :, : 2 * head_width] + grad_rel_part,
            grad_project[:, :, 2 * head_width :],
        ],
        2,
    ).astype(low)
    grad_rel_norm = product("hrc,hdc->rd", rel_grads, w_project[:, :, : 2 * head_width])
    grad_relative, grad_gain = back_rel(grad_rel_norm)
    grad_vec = grad_vec + grad_gain
    grad_relative = grad_relative.reshape(pieces, span_part, model).transpose(0, 2, 1).astype(low)
    late = jnp.concatenate([grad_project, grad_relative], 2)
    late = lax.psum_scatter(
        late.reshape(pieces * model, -1), everyone, scatter_dimension=0, tiled=True
    )
    grad_vec = lax.psum(grad_vec, everyone)
    grad_embedding = deposit(all_lengths, places, sent, slots)[:vocab_slab].T

    early = early.astype(f32)
    late = late.astype(f32)
    squares_local = sum(jnp.sum(part * part) for part in (early, late, grad_embedding))
    squares_total, loss_sum = lax.psum((squares_local, loss_part), everyone)
    grad_norm = jnp.sqrt(squares_total + jnp.sum(grad_vec * grad_vec))
    factor = jnp.minimum(1.0, clip_level / grad_norm)

    grad_expand = early[:, :hidden]
    grad_contract = early[:, hidden : 2 * hidden].T
    grad_combine = early[:, 2 * hidden + head_width :].T
    grad_project = late[:, : 3 * head_width].reshape(width, 3, head_width)
    shared = jnp.concatenate(
        [early[:, 2 * hidden : 2 * hidden + head_width], late[:, 3 * head_width :]], 1
    )
    shared = lax.all_gather(shared, "heads", axis=0, tiled=True).reshape(pieces, width, -1)
    grad_readout = shared[:, :, :head_width].transpose(1, 0, 2).reshape(width, model)
    grad_relative = shared[:, :, head_width:].transpose(0, 2, 1).reshape(entries, width)
    grad_vec = lax.dynamic_slice_in_dim(grad_vec, owner * width, width, 1)
    weights = (embedding, relative, project, combine, expand, contract, readout, vectors)
    gradients = (
        grad_embedding,
        grad_relative,
        grad_project,
        grad_combine,
        grad_expand,
        grad_contract,
        grad_readout,
        grad_vec,
    )
    means = (
        embedding_mean,
        relative_mean,
        project_mean,
        combine_mean,
        expand_mean,
        contract_mean,
        readout_mean,
        vectors_mean,
    )
    squares = (
        embedding_square,
        relative_square,
        project_square,
        combine_square,
        expand_square,
        contract_square,
        readout_square,
        vectors_square,
    )
    updates = [
        adamw(weight, gradient * factor, mean, square, rate_now)
        for weight, gradient, mean, square, rate_now in zip(
            weights, gradients, means, squares, rate_steps
        )
    ]
    return (
        loss_sum,
        token_total,
        grad_norm,
        updates[0][0],
        updates[0][1],
        updates[0][2],
        updates[1][0],
        updates[1][1],
        updates[1][2],
        updates[2][0],
        updates[2][1],
        updates[2][2],
        updates[3][0],
        updates[3][1],
        updates[3][2],
        updates[4][0],
        updates[4][1],
        updates[4][2],
        updates[5][0],
        updates[5][1],
        updates[5][2],
        updates[6][0],
        updates[6][1],
        updates[6][2],
        updates[7][0],
        updates[7][1],
        updates[7][2],
        grad_vec[3] * factor,
    )


def solution(mesh):
    placed = (
        P("dp", None),
        P("dp"),
        P("dp", None),
        P("dp", "heads"),
        P(None, "dp"),
        P("dp", None, "heads"),
        P("heads", "dp"),
        P("dp", "heads"),
        P("heads", "dp"),
        P("dp", None),
        P(None, "dp"),
        P("dp", "heads"),
        P(None, "dp"),
        P("dp", None, "heads"),
        P("heads", "dp"),
        P("dp", "heads"),
        P("heads", "dp"),
        P("dp", None),
        P(None, "dp"),
        P("dp", "heads"),
        P(None, "dp"),
        P("dp", None, "heads"),
        P("heads", "dp"),
        P("dp", "heads"),
        P("heads", "dp"),
        P("dp", None),
        P(None, "dp"),
    )
    return jax.shard_map(
        per_device,
        mesh=mesh,
        in_specs=placed,
        out_specs=(
            P(),
            P(),
            P(),
            P("dp", "heads"),
            P("dp", "heads"),
            P("dp", "heads"),
            P(None, "dp"),
            P(None, "dp"),
            P(None, "dp"),
            P("dp", None, "heads"),
            P("dp", None, "heads"),
            P("dp", None, "heads"),
            P("heads", "dp"),
            P("heads", "dp"),
            P("heads", "dp"),
            P("dp", "heads"),
            P("dp", "heads"),
            P("dp", "heads"),
            P("heads", "dp"),
            P("heads", "dp"),
            P("heads", "dp"),
            P("dp", None),
            P("dp", None),
            P("dp", None),
            P(None, "dp"),
            P(None, "dp"),
            P(None, "dp"),
            P("dp"),
        ),
        check_vma=False,
    )
```

time: 4020 us -> 789 us (0.20)
  waiting for transfers between devices: 1840 us -> 239 us
  local copies, waits for them, and re-layouts: 1460 us -> 117 us
  matrix products: 285 us -> 88 us
  Pallas kernels: 0 us -> 138 us
  other arithmetic: 182 us -> 63.4 us
  blocking collectives: 178 us -> 105 us
    reduce_scatter x9 -> x3, waiting for transfers between devices: 982 us -> 180 us  [the longest x1 110 us: per_device(): lax.psum_scatter(early.reshape(pieces * model, -1), everyone, scatter_dim...]
    all_gather x10 -> x3, waiting for transfers between devices: 578 us -> 29.4 us  [the longest x1 21.8 us: per_device(): second_all = lax.all_gather(second_pack, everyone, axis=0, tiled=True)]
    rev x24 -> x0, local copies, waits for them, and re-layouts: 427 us -> none  [rel_skew(): table[:, :, ::-1]]
    reshape x25 -> x2, local copies, waits for them, and re-layouts: 318 us -> 12.5 us  [the longest x1 6.51 us: per_device(): late.reshape(pieces * model, -1)]
    unnamed x28 -> x6, waiting for transfers between devices: 259 us -> 0.1 us
    while x179 -> x0, local copies, waits for them, and re-layouts: 195 us -> none
    dot_general x78 -> x19, matrix products: 257 us -> 88 us  [the longest x18 83.8 us: product(): return jnp.einsum(form, matrix, operand, preferred_element_type=f32)]
    pallas_call x0 -> x4, Pallas kernels: none -> 138 us  [the longest x1 57.1 us: attend_back(): pl.pallas_call(attend_back_kernel, grid=(groups,), in_specs=[pl.BlockSpec...]
  transfers between devices with their start and end apart: 24 -> 7, of which waited for: 22 -> 6; matrix products, arithmetic and copies ran while one was open for 4% -> 13% of each run, Pallas kernels for 0% -> 8%
where the time goes in v1:
time: 789 us; the launch traced here: 780 us
  waiting for transfers between devices  239 us (30%)
  Pallas kernels  138 us (17%)
  local copies, waits for them, and re-layouts  117 us (15%)
  blocking collectives  105 us (13%)
  matrix products  88 us (11%)
  other arithmetic  63.4 us (8%)
  between operations  23.6 us (3%)
    reduce_scatter x1, waiting for transfers between devices, per_device(): lax.psum_scatter(early.reshape(pieces * model, -1), everyone, scatter_dim...  110 us
    dot_general x18, matrix products, product(): return jnp.einsum(form, matrix, operand, preferred_element_type=f32)  83.8 us
    pallas_call x1, Pallas kernels, attend_back(): pl.pallas_call(attend_back_kernel, grid=(groups,), in_specs=[pl.BlockSpec...  57.1 us
    unnamed x142, local copies, waits for them, and re-layouts  53.9 us
    psum x1, blocking collectives, per_device(): squares_total, loss_sum = lax.psum((squares_local, loss_part), everyone)  40.3 us
    pallas_call x1, Pallas kernels, attend(): pl.pallas_call(attend_kernel, grid=(groups,), in_specs=[pl.BlockSpec(memo...  35 us
    reduce_scatter x1, waiting for transfers between devices, per_device(): lax.psum_scatter(late.reshape(pieces * model, -1), everyone, scatter_dime...  35 us
    reduce_scatter x1, waiting for transfers between devices, per_device(): found = lax.psum_scatter(found, 'heads', scatter_dimension=1, tiled=True)  34.3 us
  transfers between devices with their start and end apart: 7, of which 6 were waited for; matrix products, arithmetic and copies ran while one was open for 13% of the time, Pallas kernels for 8%

profile of v1, /device:TPU:0, one launch (start us, length us, event | category | flops | bytes accessed | tf_op | source)
XLA Modules:
  0.0 780.0 jit_solution(17614694664177509448)
XLA Ops:
  9.5 32.3 %all-gather.1 = s32[8,4,513]{2,1,0:T(4,128)S(1)} all-gather(s32[1,4,513]{2,1,0:T(4,128)S(1)} %add_bitcast_fusion), channel_id=1, replica_groups=mesh['dp'=8,'heads'=4] {'dp'}, dimensions={0}, use_global_device_ids=true | all-gather | bytes 73872 | tf_op jit(solution)/shard_map/all_gather | solution.py:310
  42.6 6.5 copy.266
  49.0 4.8 pad.41.table_ref
  53.9 17.4 %lookup.1 = bf16[32,512,96]{2,1,0:T(8,128)(2,1)S(1)} custom-call(s32[32]{0:T(128)S(1)} %get-tuple-element.203.lengths_ref, s32[32,1,512]{2,1,0:T(1,128)S(1)} %broadcast_in_dim.37.places_ref, f32[12680,96]{1,0:T(8,128)} %pad.41.table_ref), custom_call_target="tpu_custom_call" | custom-call | tf_op jit(solution)/shard_map/lookup/pallas_call | solution.py:157
  73.3 6.0 copy.267
  84.3 34.3 %reduce-scatter.4.cloned.1.call-done = bf16[8,1,512,96]{2,3,0,1:T(8,128)(2,1)} async-done(((bf16[8,4,512,96]{2,3,0,1:T(8,128)(2,1)}), bf16[8,1,512,96]{2,3,0,1:T(8,128)(2,1)}) %reduce-scatter.4.cloned.1.call-update) | async-done | bytes 786448 | tf_op jit(solution)/shard_map/reduce_scatter | solution.py:359
  118.6 5.5 all-to-all-start
  126.1 30.0 %all-to-all-done = bf16[8,512,96]{1,2,0:T(8,128)(2,1)S(1)} async-done(((bf16[8,512,96]{1,2,0:T(8,128)(2,1)}), bf16[8,512,96]{1,2,0:T(8,128)(2,1)S(1)}, u32[]{:S(2)}, u32[]{:S(2)}) %all-to-all-start) | async-done | bytes 786464 | tf_op jit(solution)/shard_map/all_to_all | solution.py:361
  159.0 7.6 all-gather.6.cloned.1.call-done
  170.0 6.0 fusion.48
  176.1 3.3 copy.273
  179.4 2.6 slice_convert_fusion.1
  183.3 3.0 copy.275
  188.9 7.1 convert_bitcast_fusion.2.table_ref
  196.1 35.0 %attend.1 = (bf16[12,512,512]{2,1,0:T(8,128)(2,1)}, bf16[4,512,192]{2,1,0:T(8,128)(2,1)S(1)}) custom-call(s32[1]{0:T(128)} %dynamic_slice.15.length_ref, bf16[4,512,576]{2,1,0:T(8,128)(2,1)S(1)} %bitcast.284, bf16[4,1024,384]{2,1,0:T(8,128)(2,1)} %convert_bitcast_fusion.2.table_ref), custom_call_target="tpu_custom_call" | custom-call | tf_op jit(solution)/shard_map/attend/pallas_call | solution.py:64
  231.1 3.4 fusion.152
  234.8 21.8 %all-gather.8.cloned.1.call-done = bf16[3072,1728]{1,0:T(8,128)(2,1)} async-done(((bf16[96,1728]{1,0:T(8,128)(2,1)}), bf16[3072,1728]{1,0:T(8,128)(2,1)}) %all-gather.8.cloned.1.call-update) | async-done | bytes 10616848 | tf_op jit(solution)/shard_map/all_gather | solution.py:337
  256.7 2.7 slice_bitcast_fusion
  259.3 2.5 copy.281
  261.8 20.4 %fusion.11 = (bf16[4,512,768]{1,2,0:T(8,128)(2,1)S(1)}, f32[4,512,768]{1,2,0:T(8,128)}, f32[4,768,512]{2,1,0:T(8,128)}) fusion(f32[512,768]{1,0:T(8,128)S(1)} %get-tuple-element.255, f32[768]{0:T(1024)S(1)} %get-tuple-element.196, f32[768]{0:T(1024)S(1)} %get-tuple-element.197, f32[512]{0:T(512)S(1)} %fusion.123, f32[512]{0:T(512)S(1)} %broadcast_multiply_fusion.3, ...), kind=kOutput, calls=%fused_computation.24 | convolution fusion | flops 2520121344 | bytes 22030336 | tf_op jit(solution)/shard_map/td,hdf->htf/dot_general | solution.py:227
  282.2 6.4 fusion.153
  290.5 4.2 fusion.147
  302.0 8.3 %fusion.8 = bf16[4,512,768]{1,2,0:T(8,128)(2,1)S(1)} fusion(f32[4,512,768]{1,2,0:T(8,128)} %get-tuple-element.244, f32[4,768,512]{2,1,0:T(8,128)} %get-tuple-element.256, bf16[4,768,1728]{2,1,0:T(8,128)(2,1)S(1)} %bitcast.317, f32[512,768]{1,0:T(8,128)S(1)} %get-tuple-element.239, f32[512]{0:T(512)S(1)} %negate_multiply_fusion.5), kind=kOutput, calls=%fused_computation.16 | convolution fusion | flops 2438725632 | bytes 22022144 | tf_op jit(solution)/shard_map/td,hdf->htf/dot_general | solution.py:227
  310.3 3.3 multiply_reduce_fusion.3
  315.5 4.2 convolution_convert_fusion.2
  321.1 57.1 %attend_back.1 = (bf16[4,512,576]{2,1,0:T(8,128)(2,1)S(1)}, bf16[4,1024,384]{2,1,0:T(8,128)(2,1)}) custom-call(bf16[4,512,576]{2,1,0:T(8,128)(2,1)} %bitcast.285, bf16[4,1024,384]{2,1,0:T(8,128)(2,1)} %convert_bitcast_fusion.2.table_ref, bf16[12,512,512]{2,1,0:T(8,128)(2,1)} %get-tuple-element.33.probs_ref, bf16[4,512,192]{2,1,0:T(8,128)(2,1)S(1)} %bitcast.287), custom_call_target="tpu_custom_call" | custom-call | tf_op jit(solution)/shard_map/attend_back/pallas_call | solution.py:123
  378.2 4.8 multiply_reduce_fusion.2
  387.2 3.5 fusion.59
  397.9 6.5 copy.335
  408.3 24.5 %all_to_all.10 = bf16[8,512,96]{1,2,0:T(8,128)(2,1)} all-to-all(bf16[8,512,96]{1,2,0:T(8,128)(2,1)S(1)} %bitcast.294), channel_id=1, replica_groups=mesh['dp'=8,'heads'=4] {'dp'}, dimensions={0} | all-to-all | bytes 1572864 | tf_op jit(solution)/shard_map/all_to_all | solution.py:427
  433.5 2.6 fusion.75
  437.8 3.1 convert_bitcast_fusion
  440.8 3.3 convert_bitcast_fusion.1
  444.1 5.2 pad_maximum_fusion
  449.3 15.2 %copy.287 = bf16[4,768,1920]{2,1,0:T(8,128)(2,1)} copy(bf16[4,768,1920]{1,2,0:T(8,128)(2,1)} %pad_maximum_fusion) | data formatting | bytes 23592960 | tf_op jit(solution)/shard_map/concatenate | solution.py:416
  465.7 6.5 copy.300
  472.2 6.4 copy.298
  479.4 35.0 %reduce-scatter.8.cloned.1.call-done = bf16[96,704]{1,0:T(8,128)(2,1)} async-done(((bf16[3072,704]{1,0:T(8,128)(2,1)}), bf16[96,704]{1,0:T(8,128)(2,1)}) %reduce-scatter.8.cloned.1.call-update) | async-done | bytes 135184 | tf_op jit(solution)/shard_map/reduce_scatter | solution.py:444
  517.8 6.1 copy.297
  523.9 28.4 %deposit.1 = f32[12680,96]{1,0:T(8,128)} custom-call(s32[32]{0:T(128)} %copy-done.3, s32[32,1,512]{2,1,0:T(1,128)} %copy-done.2, bf16[32,512,96]{2,1,0:T(8,128)(2,1)} %bitcast.291), custom_call_target="tpu_custom_call" | custom-call | tf_op jit(solution)/shard_map/deposit/pallas_call | solution.py:206
  552.3 4.7 multiply_reduce_fusion
  557.0 110.4 %reduce-scatter.6.cloned.1.call-done = bf16[96,1920]{1,0:T(8,128)(2,1)} async-done(((bf16[3072,1920]{1,0:T(8,128)(2,1)}), bf16[96,1920]{1,0:T(8,128)(2,1)}) %reduce-scatter.6.cloned.1.call-update) | async-done | bytes 368656 | tf_op jit(solution)/shard_map/reduce_scatter | solution.py:417
  671.1 40.3 %all-reduce.13 = (f32[]{:T(128)}, f32[]{:T(128)}, f32[11,768]{1,0:T(8,128)S(1)}) all-reduce(f32[]{:T(128)} %get-tuple-element.251, f32[]{:T(128)S(6)} %add.351, f32[11,768]{1,0:T(8,128)S(1)} %add_add_fusion.5), channel_id=1, replica_groups=mesh['dp'=8,'heads'=4] {'heads','dp'}, use_global_device_ids=true, to_apply=%region_13.14 | all-reduce | flops 8450 | bytes 67600 | tf_op jit(solution)/shard_map/psum | solution.py:453
  713.4 17.3 %multiply_subtract_fusion = (f32[96,12672]{0,1:T(8,128)}, f32[96,12672]{0,1:T(8,128)}, f32[96,12672]{0,1:T(8,128)}) fusion(f32[96,12672]{0,1:T(8,128)} %copy.266, f32[]{:T(128)S(6)} %min.15, f32[12680,96]{1,0:T(8,128)} %deposit.1, f32[96,12672]{0,1:T(8,128)} %copy.300, f32[96,12672]{0,1:T(8,128)} %copy.298), kind=kLoop, calls=%fused_computation.6 | loop fusion | flops 19464192 | bytes 34062340 | tf_op jit(solution)/shard_map/sub | solution.py:261
  730.7 6.3 copy.314
  737.0 6.3 copy.315
  743.3 6.3 copy.316
  749.7 8.3 %all_gather.19 = f32[384,320]{1,0:T(8,128)S(1)} all-gather(f32[96,320]{1,0:T(8,128)S(1)} %pad_maximum_fusion.3), channel_id=1, replica_groups=mesh['dp'=8,'heads'=4] {'heads'}, dimensions={0}, use_global_device_ids=true | all-gather | bytes 614400 | tf_op jit(solution)/shard_map/all_gather | solution.py:464
  (256 shorter events, 69.9 us)
Async XLA Ops:
  8.0 110.5 %reduce-scatter.4.cloned.1.call-start = ((), (), s32[]{:S(2)}) async-start(), calls=%async_computation.5 | async-start | bytes 3932160 | tf_op jit(solution)/shard_map/reduce_scatter | solution.py:359
  42.5 11.4 %copy-start.3 = (s32[32]{0:T(128)}, s32[32]{0:T(128)S(1)}, u32[]{:S(2)}) copy-start(s32[32]{0:T(128)S(1)} %get-tuple-element.203.lengths_ref) | copy-start | bytes 388
  42.6 11.3 %copy-start.2 = (s32[32,1,512]{2,1,0:T(1,128)}, s32[32,1,512]{2,1,0:T(1,128)S(1)}, u32[]{:S(2)}) copy-start(s32[32,1,512]{2,1,0:T(1,128)S(1)} %broadcast_in_dim.37.places_ref) | copy-start | bytes 196612
  79.3 3.1 copy-start.20
  79.3 4.1 copy-start.22
  79.3 87.2 %all-gather.6.cloned.1.call-start = ((), (), s32[]{:S(2)}) async-start(), calls=%async_computation.6 | async-start | bytes 7299072 | tf_op jit(solution)/shard_map/all_gather | solution.py:335
  82.3 174.3 %all-gather.8.cloned.1.call-start = ((), (), s32[]{:S(2)}) async-start(), calls=%async_computation.7 | async-start | bytes 11354112 | tf_op jit(solution)/shard_map/all_gather | solution.py:337
  82.4 41.7 %copy-start.51 = (s32[4]{0:T(128)S(1)}, s32[4]{0:T(128)}, u32[]{:S(2)}) copy-start(s32[4]{0:T(128)} %param.28) | copy-start | bytes 52
  118.6 37.6 %all-to-all-start = ((bf16[8,512,96]{1,2,0:T(8,128)(2,1)}), bf16[8,512,96]{1,2,0:T(8,128)(2,1)S(1)}, u32[]{:S(2)}, u32[]{:S(2)}) async-start(bf16[8,512,96]{1,2,0:T(8,128)(2,1)} %bitcast.301), calls=%async_computation.1 | async-start | bytes 1572864 | tf_op jit(solution)/shard_map/all_to_all | solution.py:361
  124.1 390.3 %reduce-scatter.8.cloned.1.call-start = ((), (), s32[]{:S(2)}) async-start(), calls=%async_computation.9 | async-start | bytes 4866048 | tf_op jit(solution)/shard_map/reduce_scatter | solution.py:444
  167.8 2.2 copy-start.9
  179.4 16.7 %copy-start = (bf16[4,576,512]{1,2,0:T(8,128)(2,1)}, bf16[4,576,512]{1,2,0:T(8,128)(2,1)S(1)}, u32[]{:S(2)}) copy-start(bf16[4,576,512]{1,2,0:T(8,128)(2,1)S(1)} %copy.273) | copy-start | bytes 7077892
  186.3 2.3 copy-start.6
  188.9 7.2 copy-start.12
  196.1 35.0 %copy-start.10 = (f32[512,768]{1,0:T(8,128)S(1)}, f32[512,768]{1,0:T(8,128)}, u32[]{:S(2)}) copy-start(f32[512,768]{1,0:T(8,128)} %copy.268) | copy-start | bytes 4718596
  231.1 3.4 copy-start.4
  282.2 6.4 copy-start.55
  288.6 12.5 %copy-start.8 = (f32[512,768]{1,0:T(8,128)}, f32[512,768]{1,0:T(8,128)S(1)}, u32[]{:S(2)}) copy-start(f32[512,768]{1,0:T(8,128)S(1)} %get-tuple-element.258) | copy-start | bytes 4718596
  294.9 6.9 slice-start
  298.7 3.1 slice-start.1
  301.8 8.5 %copy-start.15 = (f32[512,768]{1,0:T(8,128)}, f32[512,768]{1,0:T(8,128)S(1)}, u32[]{:S(2)}) copy-start(f32[512,768]{1,0:T(8,128)S(1)} %get-tuple-element.239) | copy-start | bytes 4718596
  310.3 3.3 copy-start.53
  321.1 57.1 %copy-start.11 = (f32[512,768]{1,0:T(8,128)S(1)}, f32[512,768]{1,0:T(8,128)}, u32[]{:S(2)}) copy-start(f32[512,768]{1,0:T(8,128)} %copy.268) | copy-start | bytes 4718596
  321.1 57.1 %copy-start.18 = (f32[512,768]{1,0:T(8,128)S(1)}, f32[512,768]{1,0:T(8,128)}, u32[]{:S(2)}) copy-start(f32[512,768]{1,0:T(8,128)} %copy-done.17) | copy-start | bytes 4718596
  383.0 2.2 copy-start.52
  404.4 113.4 %all-gather.10.cloned.1.call-start = ((), (), s32[]{:S(2)}) async-start(), calls=%async_computation.10 | async-start | bytes 3932160 | tf_op jit(solution)/shard_map/all_gather | solution.py:428
  432.9 234.5 %reduce-scatter.6.cloned.1.call-start = ((), (), s32[]{:S(2)}) async-start(), calls=%async_computation.8 | async-start | bytes 12165120 | tf_op jit(solution)/shard_map/reduce_scatter | solution.py:417
  433.4 2.6 copy-start.5
  433.4 2.6 copy-start.19
  433.5 3.5 copy-start.56
  437.7 3.1 copy-start.54
  472.2 6.5 copy-start.35
  472.2 6.6 copy-start.36
  472.2 6.8 copy-start.41
  472.2 6.9 copy-start.42
  743.3 6.3 copy-start.14
  761.3 2.8 copy-start.30
  761.3 2.8 copy-start.39
  761.3 2.8 copy-start.40
  764.1 2.2 copy-start.23
  764.1 2.2 copy-start.33
  764.2 2.1 copy-start.34
  765.2 2.8 copy-start.44
  765.2 2.8 copy-start.49
  765.2 2.8 copy-start.50
  766.3 2.4 copy-start.27
  766.3 2.4 copy-start.37
  766.3 2.4 copy-start.38
  (19 other events, 27.9 us)
Sparse Core Ops, SparseCore 0:
  79.4 39.0 reduce-scatter.3
  433.0 27.2 all-gather.9
Sparse Core Ops, SparseCore 1:
  83.4 83.1 all-gather.5
  170.0 86.6 all-gather.7
  404.5 109.8 reduce-scatter.7
  520.5 146.9 reduce-scatter.5

commit v2 on v1

--- a/solution.py
+++ b/solution.py
@@ -1,3 +1,5 @@
+import functools
+
 import jax
 import jax.numpy as jnp
 from jax import lax
@@ -20,6 +22,7 @@
 beta_second = 0.999
 adam_eps = 1e-08
 weight_decay = 0.01
+
 
 def dot_rows(a,b):
     return lax.dot_general(a,b,(((1,),(1,)),((),())),preferred_element_type=f32)
@@ -137,48 +140,604 @@
     )(qkv,table,probs,up)
 
 
-def lookup_kernel(lengths_ref, places_ref, table_ref, words_ref, rows_ref):
+MESH = pl.DeviceIdType.MESH
+ANYWHERE = pl.BlockSpec(memory_space=pl.ANY)
+IN_VMEM = pl.BlockSpec(memory_space=pltpu.VMEM)
+
+
+def place():
+    owner, holder = lax.axis_index("dp"), lax.axis_index("heads")
+    return owner // 2, owner % 2, holder // 2, holder % 2
+
+
+def device(z, x, y, c):
+    return (z * 2 + x, y * 2 + c)
+
+
+def signal(target):
+    pl.semaphore_signal(
+        pltpu.get_barrier_semaphore(), inc=1, device_id=target, device_id_type=MESH
+    )
+
+
+def greet(z, x, y, c, line):
+    signal(device(z, x, y, 1 - c))
+    signal(device(z, x, 1 - y, c))
+    if line:
+        signal(device(z, 1 - x, y, c))
+
+        @pl.when(z < 3)
+        def above():
+            signal(device(z + 1, x, y, c))
+
+        @pl.when(z > 0)
+        def below():
+            signal(device(z - 1, x, y, c))
+
+        pl.semaphore_wait(pltpu.get_barrier_semaphore(), jnp.where((z == 0) | (z == 3), 4, 5))
+
+
+def remote(source, target, send, recv, to):
+    return pltpu.make_async_remote_copy(
+        src_ref=source, dst_ref=target, send_sem=send, recv_sem=recv, device_id=to, device_id_type=MESH
+    )
+
+
+def scatter_sums_kernel(count, *refs):
+    grads, totals = refs[:count], refs[count : 2 * count]
+    refs = refs[2 * count :]
+    own, pair, first_a, first_b, second_a, second_b, rise, fall = [
+        refs[count * part : count * (part + 1)] for part in range(8)
+    ]
+    local_sem, send_sem, recv_sem = refs[8 * count :]
+    z, x, y, c = place()
+    greet(z, x, y, c, True)
+    half = grads[0].shape[3] // 2
+    upper, lower = pl.ds(0, half), pl.ds(half, half)
+    core_to, y_to, x_to = device(z, x, y, 1 - c), device(z, x, 1 - y, c), device(z, 1 - x, y, c)
+    up_to, down_to = device(z + 1, x, y, c), device(z - 1, x, y, c)
+
+    def link(part, slot, source, target, to):
+        return remote(source, target, send_sem.at[part, slot], recv_sem.at[part, slot], to)
+
+    def local(part, side):
+        return pltpu.make_async_copy(
+            grads[part].at[side * 2 + c], own[part].at[side], local_sem.at[part, side]
+        )
+
+    def pair_copy(part, side):
+        return link(part, side, grads[part].at[side * 2 + 1 - c], pair[part].at[side], core_to)
+
+    def first_copies(part):
+        block = own[part]
+        return (
+            link(part, 2, block.at[1 - y, :, :, upper], first_a[part], y_to),
+            link(part, 3, block.at[:, :, 1 - x, lower], first_b[part], x_to),
+        )
+
+    def second_copies(part):
+        block = own[part]
+        return (
+            link(part, 4, block.at[y, :, 1 - x, upper], second_a[part], x_to),
+            link(part, 5, block.at[1 - y, :, x, lower], second_b[part], y_to),
+        )
+
+    def rise_copy(part, turn):
+        block = own[part].at[y, lax.clamp(0, 3 + z - turn, 3), x]
+        return link(part, 6 + turn, block, rise[part].at[turn], up_to)
+
+    def fall_copy(part, turn):
+        block = own[part].at[y, lax.clamp(0, turn - 3 + z, 3), x]
+        return link(part, 9 + turn, block, fall[part].at[turn], down_to)
+
+    def add(target, source):
+        target[...] = (target[...].astype(f32) + source[...].astype(f32)).astype(low)
+
+    def start(part):
+        for side in range(2):
+            pair_copy(part, side).start()
+            local(part, side).start()
+
+    def stage_pair(part):
+        for side in range(2):
+            local(part, side).wait()
+            pair_copy(part, side).wait()
+
+        def step(index, carry):
+            side, rest = index // 8, index % 8
+            add(own[part].at[side, rest // 2, rest % 2], pair[part].at[side, rest // 2, rest % 2])
+            return carry
+
+        lax.fori_loop(0, 16, step, 0)
+        for copy in first_copies(part):
+            copy.start()
+
+    def stage_first(part):
+        for copy in first_copies(part):
+            copy.wait()
+
+        def step(index, carry):
+            add(own[part].at[y, index // 2, index % 2, upper], first_a[part].at[index // 2, index % 2])
+            add(own[part].at[index % 2, index // 2, x, lower], first_b[part].at[index % 2, index // 2])
+            return carry
+
+        lax.fori_loop(0, 8, step, 0)
+        for copy in second_copies(part):
+            copy.start()
+
+    def stage_second(part):
+        for copy in second_copies(part):
+            copy.wait()
+
+        def step(index, carry):
+            add(own[part].at[y, index, x, upper], second_a[part].at[index])
+            add(own[part].at[y, index, x, lower], second_b[part].at[index])
+            return carry
+
+        lax.fori_loop(0, 4, step, 0)
+
+    def stage_line(part, turn):
+        @pl.when((z <= turn) & (z < 3))
+        def rises():
+            if turn > 0:
+
+                @pl.when(z > 0)
+                def joined():
+                    rise_copy(part, turn - 1).wait_recv()
+                    add(own[part].at[y, 3 + z - turn, x], rise[part].at[turn - 1])
+
+            rise_copy(part, turn).start()
+
+        @pl.when((3 - z <= turn) & (z > 0))
+        def falls():
+            if turn > 0:
+
+                @pl.when(z < 3)
+                def joined():
+                    fall_copy(part, turn - 1).wait_recv()
+                    add(own[part].at[y, turn - 3 + z, x], fall[part].at[turn - 1])
+
+            fall_copy(part, turn).start()
+
+    def stage_total(part):
+        totals[part][...] = own[part][y, z, x].astype(f32)
+
+        @pl.when(z > 0)
+        def risen():
+            rise_copy(part, 2).wait_recv()
+            totals[part][...] += rise[part][2].astype(f32)
+
+        @pl.when(z < 3)
+        def fallen():
+            fall_copy(part, 2).wait_recv()
+            totals[part][...] += fall[part][2].astype(f32)
+
+        for turn in range(3):
+
+            @pl.when((z <= turn) & (z < 3))
+            def risen_out():
+                rise_copy(part, turn).wait_send()
+
+            @pl.when((3 - z <= turn) & (z > 0))
+            def fallen_out():
+                fall_copy(part, turn).wait_send()
+
+    stages = [
+        stage_pair,
+        stage_first,
+        stage_second,
+        functools.partial(stage_line, turn=0),
+        functools.partial(stage_line, turn=1),
+        functools.partial(stage_line, turn=2),
+        stage_total,
+    ]
+    for part in range(count):
+        start(part)
+    for tick in range(count + len(stages) - 1):
+        for index, stage in enumerate(stages):
+            if 0 <= tick - index < count:
+                stage(tick - index)
+
+
+def scatter_sums(grads, tag):
+    count = len(grads)
+    width = grads[0].shape[2]
+    sizes = [grad.shape[3] for grad in grads]
+    half = width // 2
+    scratch = []
+    for lead in (
+        (2, 4, 2, width),
+        (2, 4, 2, width),
+        (4, 2, half),
+        (2, 4, half),
+        (4, half),
+        (4, half),
+        (3, width),
+        (3, width),
+    ):
+        scratch += [pltpu.VMEM(lead + (size,), low) for size in sizes]
+    return pl.pallas_call(
+        functools.partial(scatter_sums_kernel, count),
+        in_specs=[ANYWHERE] * count,
+        out_specs=[IN_VMEM] * count,
+        out_shape=[jax.ShapeDtypeStruct((width, size), f32) for size in sizes],
+        scratch_shapes=scratch
+        + [
+            pltpu.SemaphoreType.DMA((count, 2)),
+            pltpu.SemaphoreType.DMA((count, 12)),
+            pltpu.SemaphoreType.DMA((count, 12)),
+        ],
+        compiler_params=pltpu.CompilerParams(
+            collective_id=tag, has_side_effects=True, vmem_limit_bytes=56 << 20
+        ),
+        name="scatter_sums",
+    )(*[grad.reshape(4, 4, 2, width, size) for grad, size in zip(grads, sizes)])
+
+
+def peers(z, x):
+    return [((z + 2 - far) % 4, x if same else 1 - x) for far, same in PEER_ORDER]
+
+
+PEER_ORDER = ((0, False), (0, True), (1, False), (1, True), (3, False), (3, True), (2, False))
+
+
+def meet_owners(z, x, y, c):
+    for peer_z, peer_x in peers(z, x):
+        signal(device(peer_z, peer_x, y, c))
+
+
+def share_facts_kernel(facts_ref, all_ref, local_sem, send_sem, recv_sem):
+    z, x, y, c = place()
+    meet_owners(z, x, y, c)
+    pl.semaphore_wait(pltpu.get_barrier_semaphore(), 7)
+    here = z * 2 + x
+    keep = pltpu.make_async_copy(facts_ref, all_ref.at[here], local_sem)
+    keep.start()
+    copies = []
+    for index, (peer_z, peer_x) in enumerate(peers(z, x)):
+        copy = remote(
+            facts_ref,
+            all_ref.at[here],
+            send_sem.at[index],
+            recv_sem.at[here],
+            device(peer_z, peer_x, y, c),
+        )
+        copy.start()
+        copies.append(copy)
+    for index, (peer_z, peer_x) in enumerate(peers(z, x)):
+        there = peer_z * 2 + peer_x
+        copies[index].wait_send()
+        remote(
+            facts_ref, all_ref.at[there], send_sem.at[index], recv_sem.at[there], device(z, x, y, c)
+        ).wait_recv()
+    keep.wait()
+
+
+def share_facts(facts, tag):
+    return pl.pallas_call(
+        share_facts_kernel,
+        in_specs=[IN_VMEM],
+        out_specs=IN_VMEM,
+        out_shape=jax.ShapeDtypeStruct((8,) + facts.shape, facts.dtype),
+        scratch_shapes=[
+            pltpu.SemaphoreType.DMA,
+            pltpu.SemaphoreType.DMA((7,)),
+            pltpu.SemaphoreType.DMA((8,)),
+        ],
+        compiler_params=pltpu.CompilerParams(collective_id=tag, has_side_effects=True),
+        name="share_facts",
+    )(facts)
+
+
+def exchange_words_kernel(found_ref, words_ref, pair, side, send_sem, recv_sem, out_sem, in_sem):
+    z, x, y, c = place()
+    meet_owners(z, x, y, c)
+    greet(z, x, y, c, False)
+    pl.semaphore_wait(pltpu.get_barrier_semaphore(), 9)
+    here = z * 2 + x
+    targets = [(z, x)] + peers(z, x)
+    targets = targets[1:] + targets[:1]
+    core_to, y_to = device(z, x, y, 1 - c), device(z, x, 1 - y, c)
+
+    def pair_copy(part, row):
+        to = targets[part][0] * 2 + targets[part][1]
+        return remote(
+            found_ref.at[row * 2 + 1 - c, to],
+            pair.at[row, to],
+            send_sem.at[part, row],
+            recv_sem.at[part, row],
+            core_to,
+        )
+
+    def side_copy(part):
+        to = targets[part][0] * 2 + targets[part][1]
+        return remote(
+            pair.at[1 - y, to], side.at[to], send_sem.at[part, 2], recv_sem.at[part, 2], y_to
+        )
+
+    def out_copy(part):
+        to = targets[part][0] * 2 + targets[part][1]
+        return remote(
+            pair.at[y, to],
+            words_ref.at[here],
+            out_sem.at[part],
+            in_sem.at[here],
+            device(targets[part][0], targets[part][1], y, c),
+        )
+
+    def at_home(part):
+        return targets[part][0] * 2 + targets[part][1]
+
+    for part in range(8):
+        for row in range(2):
+            pair_copy(part, row).start()
+    for part in range(8):
+        to = at_home(part)
+        for row in range(2):
+            pair_copy(part, row).wait_recv()
+            pair[row, to] = pair[row, to] + found_ref[row * 2 + c, to]
+        side_copy(part).start()
+    for part in range(8):
+        to = at_home(part)
+        side_copy(part).wait_recv()
+        pair[y, to] = pair[y, to] + side[to]
+        if part < 7:
+            out_copy(part).start()
+        else:
+            words_ref[here] = pair[y, to]
+    for part in range(8):
+        for row in range(2):
+            pair_copy(part, row).wait_send()
+        side_copy(part).wait_send()
+        if part < 7:
+            out_copy(part).wait_send()
+            there = at_home(part)
+            remote(
+                pair.at[y, there], words_ref.at[there], out_sem.at[part], in_sem.at[there], core_to
+            ).wait_recv()
+
+
+def exchange_words(found, tag):
+    piece = found.shape[2:]
+    return pl.pallas_call(
+        exchange_words_kernel,
+        in_specs=[IN_VMEM],
+        out_specs=IN_VMEM,
+        out_shape=jax.ShapeDtypeStruct((8,) + piece, low),
+        scratch_shapes=[
+            pltpu.VMEM((2, 8) + piece, low),
+            pltpu.VMEM((8,) + piece, low),
+            pltpu.SemaphoreType.DMA((8, 3)),
+            pltpu.SemaphoreType.DMA((8, 3)),
+            pltpu.SemaphoreType.DMA((8,)),
+            pltpu.SemaphoreType.DMA((8,)),
+        ],
+        compiler_params=pltpu.CompilerParams(
+            collective_id=tag, has_side_effects=True, vmem_limit_bytes=40 << 20
+        ),
+        name="exchange_words",
+    )(found)
+
+
+def return_words_kernel(grads_ref, sent_ref, local_sem, out_sem, in_sem, send_sem, recv_sem):
+    z, x, y, c = place()
+    meet_owners(z, x, y, c)
+    greet(z, x, y, c, False)
+    pl.semaphore_wait(pltpu.get_barrier_semaphore(), 9)
+    here = z * 2 + x
+    own = y * 2 + c
+    other = (1 - y) * 2 + c
+    core_to, y_to = device(z, x, y, 1 - c), device(z, x, 1 - y, c)
+    near_first = peers(z, x)[::-1]
+    keep = pltpu.make_async_copy(grads_ref.at[here], sent_ref.at[own, here], local_sem)
+    keep.start()
+
+    def out_copy(part, peer):
+        return remote(
+            grads_ref.at[peer[0] * 2 + peer[1]],
+            sent_ref.at[own, here],
+            out_sem.at[part],
+            in_sem.at[here],
+            device(peer[0], peer[1], y, c),
+        )
+
+    def in_copy(part, peer):
+        there = peer[0] * 2 + peer[1]
+        return remote(
+            grads_ref.at[there], sent_ref.at[own, there], out_sem.at[part], in_sem.at[there], core_to
+        )
+
+    def pass_on(slot, row, there, to):
+        block = sent_ref.at[row, there]
+        return remote(block, block, send_sem.at[slot, there], recv_sem.at[row, there], to)
+
+    for part, peer in enumerate(peers(z, x)):
+        out_copy(part, peer).start()
+    keep.wait()
+    order = [(z, x)] + near_first
+    for part, (peer_z, peer_x) in enumerate(order):
+        there = peer_z * 2 + peer_x
+        if part > 0:
+            in_copy(part - 1, (peer_z, peer_x)).wait_recv()
+        pass_on(0, own, there, y_to).start()
+        pass_on(1, own, there, core_to).start()
+    for peer_z, peer_x in order:
+        there = peer_z * 2 + peer_x
+        pass_on(0, other, there, y_to).wait_recv()
+        pass_on(2, other, there, core_to).start()
+    for part, peer in enumerate(peers(z, x)):
+        out_copy(part, peer).wait_send()
+    for peer_z, peer_x in order:
+        there = peer_z * 2 + peer_x
+        pass_on(0, own, there, y_to).wait_send()
+        pass_on(1, own, there, core_to).wait_send()
+        pass_on(2, other, there, core_to).wait_send()
+        pass_on(1, y * 2 + 1 - c, there, core_to).wait_recv()
+        pass_on(2, (1 - y) * 2 + 1 - c, there, core_to).wait_recv()
+
+
+def return_words(grads, tag):
+    piece = grads.shape[1:]
+    return pl.pallas_call(
+        return_words_kernel,
+        in_specs=[IN_VMEM],
+        out_specs=IN_VMEM,
+        out_shape=jax.ShapeDtypeStruct((4, 8) + piece, low),
+        scratch_shapes=[
+            pltpu.SemaphoreType.DMA,
+            pltpu.SemaphoreType.DMA((7,)),
+            pltpu.SemaphoreType.DMA((8,)),
+            pltpu.SemaphoreType.DMA((3, 8)),
+            pltpu.SemaphoreType.DMA((4, 8)),
+        ],
+        compiler_params=pltpu.CompilerParams(
+            collective_id=tag, has_side_effects=True, vmem_limit_bytes=40 << 20
+        ),
+        name="return_words",
+    )(grads)
+
+
+def finish_sums_kernel(facts_ref, shared_ref, total_ref, all_ref, pair, side, cross, line, local_sem, send_sem, recv_sem, line_send, line_recv):
+    z, x, y, c = place()
+    core_to, y_to, x_to = device(z, x, y, 1 - c), device(z, x, 1 - y, c), device(z, 1 - x, y, c)
+    column = [(z + step) % 4 for step in range(1, 4)]
+    for target in (core_to, y_to, x_to, *[device(other, x, y, c) for other in column]):
+        signal(target)
+    pl.semaphore_wait(pltpu.get_barrier_semaphore(), 6)
+    own, other = y * 2 + c, (1 - y) * 2 + c
+    keep = pltpu.make_async_copy(shared_ref, all_ref.at[own], local_sem)
+    keep.start()
+    swap_pair = remote(facts_ref, pair, send_sem.at[0], recv_sem.at[0], core_to)
+    swap_pair.start()
+    shared_side = remote(shared_ref, all_ref.at[own], send_sem.at[3], recv_sem.at[3], y_to)
+    shared_pair = remote(shared_ref, all_ref.at[own], send_sem.at[4], recv_sem.at[4], core_to)
+    shared_side.start()
+    shared_pair.start()
+    swap_pair.wait()
+    total_ref[...] = facts_ref[...] + pair[...]
+    swap_side = remote(total_ref, side, send_sem.at[1], recv_sem.at[1], y_to)
+    swap_side.start()
+    swap_side.wait()
+    total_ref[...] += side[...]
+    swap_cross = remote(total_ref, cross, send_sem.at[2], recv_sem.at[2], x_to)
+    swap_cross.start()
+    swap_cross.wait()
+    total_ref[...] += cross[...]
+    line[z] = total_ref[...]
+    lines = [
+        remote(line.at[z], line.at[z], line_send.at[step], line_recv.at[z], device(to, x, y, c))
+        for step, to in enumerate(column)
+    ]
+    for copy in lines:
+        copy.start()
+    shared_side.wait()
+    relay = remote(all_ref.at[other], all_ref.at[other], send_sem.at[5], recv_sem.at[5], core_to)
+    relay.start()
+    for step, to in enumerate(column):
+        lines[step].wait_send()
+        remote(line.at[to], line.at[to], line_send.at[step], line_recv.at[to], core_to).wait_recv()
+    total_ref[...] = (line[0] + line[1]) + (line[2] + line[3])
+    shared_pair.wait()
+    relay.wait()
+    keep.wait()
+
+
+def finish_sums(facts, shared, tag):
+    return pl.pallas_call(
+        finish_sums_kernel,
+        in_specs=[IN_VMEM] * 2,
+        out_specs=[IN_VMEM] * 2,
+        out_shape=[
+            jax.ShapeDtypeStruct(facts.shape, f32),
+            jax.ShapeDtypeStruct((4,) + shared.shape, f32),
+        ],
+        scratch_shapes=[pltpu.VMEM(facts.shape, f32)] * 3
+        + [
+            pltpu.VMEM((4,) + facts.shape, f32),
+            pltpu.SemaphoreType.DMA,
+            pltpu.SemaphoreType.DMA((6,)),
+            pltpu.SemaphoreType.DMA((6,)),
+            pltpu.SemaphoreType.DMA((3,)),
+            pltpu.SemaphoreType.DMA((4,)),
+        ],
+        compiler_params=pltpu.CompilerParams(collective_id=tag, has_side_effects=True),
+        name="finish_sums",
+    )(facts, shared)
+
+
+def identity(size):
+    rows = lax.broadcasted_iota(jnp.int32, (size, size), 0)
+    columns = lax.broadcasted_iota(jnp.int32, (size, size), 1)
+    return (rows == columns).astype(f32).astype(low)
+
+
+def turn(values):
+    return dot_rows(identity(values.shape[1]), values)
+
+
+def lookup_kernel(lengths_ref, places_ref, weights_ref, words_ref, table_ref, rows_ref):
+    width, slab = weights_ref.shape
+
+    @pl.when(pl.program_id(0) == 0)
+    def fill():
+        def step(index, carry):
+            first = pl.multiple_of(index * BLOCK, BLOCK)
+            table_ref[pl.ds(first, BLOCK), :] = turn(weights_ref[:, pl.ds(first, BLOCK)].astype(low))
+            return carry
+
+        lax.fori_loop(0, slab // BLOCK, step, 0)
+        table_ref[pl.ds(slab, 8), :] = jnp.zeros((8, width), f32)
+
     rows_ref[...] = jnp.zeros_like(rows_ref)
 
     def step(index, carry):
         first = pl.multiple_of(index * UNROLL, UNROLL)
         for offset in range(UNROLL):
-            place = places_ref[0, 0, first + offset]
-            rows_ref[pl.ds(first + offset, 1), :] = table_ref[pl.ds(place, 1), :]
+            spot = places_ref[0, 0, first + offset]
+            rows_ref[pl.ds(first + offset, 1), :] = table_ref[pl.ds(spot, 1), :]
         return carry
 
     lax.fori_loop(0, pl.cdiv(lengths_ref[pl.program_id(0)], UNROLL), step, 0)
-    words_ref[0] = rows_ref[...].astype(low)
-
-
-def lookup(lengths, places, table):
+    seq = rows_ref.shape[0]
+    for first in range(0, seq, BLOCK):
+        words_ref[0, 0, :, first : first + BLOCK] = turn_block(rows_ref[first : first + BLOCK, :])
+
+
+def turn_block(rows):
+    return dot_rows(identity(rows.shape[1]), rows.astype(low)).astype(low)
+
+
+def lookup(lengths, places, weights, row_count):
     rows, seq = places.shape
-    width = table.shape[1]
+    width, slab = weights.shape
     return pl.pallas_call(
         lookup_kernel,
         grid=(rows,),
         in_specs=[
             pl.BlockSpec(memory_space=pltpu.SMEM),
             pl.BlockSpec((1, 1, seq), lambda row: (row, 0, 0), memory_space=pltpu.SMEM),
-            pl.BlockSpec(table.shape, lambda row: (0, 0)),
+            pl.BlockSpec(weights.shape, lambda row: (0, 0)),
         ],
-        out_specs=pl.BlockSpec((1, seq, width), lambda row: (row, 0, 0)),
-        out_shape=jax.ShapeDtypeStruct((rows, seq, width), low),
-        scratch_shapes=[pltpu.VMEM((seq, width), f32)],
+        out_specs=pl.BlockSpec(
+            (1, 1, width, seq), lambda row: (row % row_count, row // row_count, 0, 0)
+        ),
+        out_shape=jax.ShapeDtypeStruct((row_count, rows // row_count, width, seq), low),
+        scratch_shapes=[pltpu.VMEM((slab + 8, width), f32), pltpu.VMEM((seq, width), f32)],
         compiler_params=pltpu.CompilerParams(vmem_limit_bytes=48 << 20),
         name="lookup",
-    )(lengths, places[:, None], table)
-
-
-def deposit_kernel(lengths_ref, places_ref, grads_ref, total_ref, rows_ref, *parts):
-    tables = (total_ref,) + parts
+    )(lengths, places[:, None], weights)
+
+
+def deposit_kernel(lengths_ref, places_ref, grads_ref, total_ref, squares_ref, rows_ref, *tables):
+    width, slab = total_ref.shape
 
     @pl.when(pl.program_id(0) == 0)
     def clear():
         for table in tables:
             table[...] = jnp.zeros_like(table)
 
-    rows_ref[...] = grads_ref[0].astype(f32)
+    for first in range(0, rows_ref.shape[0], BLOCK):
+        rows_ref[first : first + BLOCK, :] = turn(grads_ref[0, 0, :, first : first + BLOCK])
 
     def step(index, carry):
         first = pl.multiple_of(index * UNROLL, UNROLL)
@@ -196,24 +755,40 @@
 
     @pl.when(pl.program_id(0) == pl.num_programs(0) - 1)
     def finish():
-        for part in parts:
-            total_ref[...] += part[...]
-
-
-def deposit(lengths, places, grads, slots):
+        squares_ref[...] = jnp.zeros_like(squares_ref)
+
+        def step(index, carry):
+            first = pl.multiple_of(index * BLOCK, BLOCK)
+            block = sum(table[pl.ds(first, BLOCK), :] for table in tables).T
+            total_ref[:, pl.ds(first, BLOCK)] = block
+            squares_ref[...] += block * block
+            return carry
+
+        lax.fori_loop(0, slab // BLOCK, step, 0)
+
+
+def deposit(lengths, places, grads, slab):
     rows, seq = places.shape
-    width = grads.shape[2]
+    row_count, width = grads.shape[0], grads.shape[2]
     return pl.pallas_call(
         deposit_kernel,
         grid=(rows,),
         in_specs=[
             pl.BlockSpec(memory_space=pltpu.SMEM),
             pl.BlockSpec((1, 1, seq), lambda row: (row, 0, 0), memory_space=pltpu.SMEM),
-            pl.BlockSpec((1, seq, width), lambda row: (row, 0, 0)),
+            pl.BlockSpec(
+                (1, 1, width, seq), lambda row: (row % row_count, row // row_count, 0, 0)
+            ),
         ],
-        out_specs=pl.BlockSpec((slots, width), lambda row: (0, 0)),
-        out_shape=jax.ShapeDtypeStruct((slots, width), f32),
-        scratch_shapes=[pltpu.VMEM((seq, width), f32)] + [pltpu.VMEM((slots, width), f32)] * 3,
+        out_specs=[
+            pl.BlockSpec((width, slab), lambda row: (0, 0)),
+            pl.BlockSpec((width, BLOCK), lambda row: (0, 0)),
+        ],
+        out_shape=[
+            jax.ShapeDtypeStruct((width, slab), f32),
+            jax.ShapeDtypeStruct((width, BLOCK), f32),
+        ],
+        scratch_shapes=[pltpu.VMEM((seq, width), f32)] + [pltpu.VMEM((slab + 8, width), f32)] * 4,
         compiler_params=pltpu.CompilerParams(vmem_limit_bytes=56 << 20),
         name="deposit",
     )(lengths, places[:, None], grads)
@@ -295,7 +870,6 @@
 ):
     pieces = lax.axis_size("heads")
     holder = lax.axis_index("heads")
-    owner = lax.axis_index("dp")
     owners = lax.axis_size("dp")
     row_count, seq_len = token_ids.shape
     width = vectors.shape[1]
@@ -306,16 +880,8 @@
     vocab_slab = embedding.shape[1]
     span_part = relative.shape[0] // pieces
     vector_count = vectors.shape[0]
-
-    row_facts = lax.all_gather(
-        jnp.concatenate([token_ids, row_lengths[:, None]], 1), "dp", axis=0, tiled=True
-    )
-    all_ids, all_lengths = row_facts[:, :seq_len], row_facts[:, seq_len]
-    token_total = jnp.sum(all_lengths).astype(f32)
-    local_ids = all_ids - holder * vocab_slab
-    inside = (local_ids >= 0) & (local_ids < vocab_slab)
-    places = jnp.where(inside, local_ids, vocab_slab)
-    slots = vocab_slab + 8
+    vector_part = pl.cdiv(vector_count, pieces)
+    direct = owners == 8 and pieces == 4
 
     own_relative = lax.dynamic_slice_in_dim(relative, holder * span_part, span_part, 0).T
     own_readout = lax.dynamic_slice_in_dim(readout, holder * head_width, head_width, 1)
@@ -337,6 +903,16 @@
     second_all = lax.all_gather(second_pack, everyone, axis=0, tiled=True)
     second_all = second_all.reshape(pieces, model, -1)
 
+    length_row = jnp.pad(row_lengths[None, :], ((0, 0), (0, seq_len - row_count)))
+    facts = jnp.concatenate([token_ids, jnp.pad(length_row, ((0, 8 - 1 - row_count), (0, 0)))], 0)
+    all_facts = share_facts(facts, 1) if direct else lax.all_gather(facts, "dp")
+    all_ids = all_facts[:, :row_count].reshape(owners * row_count, seq_len)
+    all_lengths = all_facts[:, row_count, :row_count].reshape(-1)
+    token_total = jnp.sum(all_lengths).astype(f32)
+    local_ids = all_ids - holder * vocab_slab
+    inside = (local_ids >= 0) & (local_ids < vocab_slab)
+    places = jnp.where(inside, local_ids, vocab_slab)
+
     w_project = first_all[:, :, : 3 * head_width]
     w_combine = first_all[:, :, 3 * head_width : 4 * head_width]
     at = 4 * head_width
@@ -354,12 +930,13 @@
     w_contract = second_all[:, :, hidden : 2 * hidden]
     w_readout = second_all[:, :, 2 * hidden :]
 
-    table = jnp.pad(embedding.T, ((0, 8), (0, 0)))
-    found = lookup(all_lengths, places, table).reshape(owners, row_count, seq_len, width)
-    found = lax.psum_scatter(found, "heads", scatter_dimension=1, tiled=True)
-    found = found.reshape(owners, seq_len, width)
-    found = lax.all_to_all(found, "dp", 0, 0, tiled=True)
-    word_rows = found.transpose(1, 0, 2).reshape(seq_len, model).astype(f32)
+    found = lookup(all_lengths, places, embedding, row_count)
+    if direct:
+        found = exchange_words(found, 2)
+    else:
+        found = lax.psum_scatter(found, "heads", scatter_dimension=0, tiled=True)[0]
+        found = lax.all_to_all(found, "dp", 0, 0, tiled=True)
+    word_rows = found.reshape(model, seq_len).T.astype(f32)
 
     own_length = lax.dynamic_slice_in_dim(row_lengths, holder, 1)
     own_live = jnp.arange(seq_len) < own_length
@@ -413,20 +990,18 @@
     grad_mixed = product("td,hdc->htc", attend_low, w_combine).astype(low)
     grad_combine = product("td,htc->hdc", attend_low, mixed).astype(low)
 
-    early = jnp.concatenate([grad_expand, grad_contract, grad_readout, grad_combine], 2)
-    early = lax.psum_scatter(
-        early.reshape(pieces * model, -1), everyone, scatter_dimension=0, tiled=True
-    )
-
     qkv_grads, rel_table_grads = attend_back(qkv, rel_table, probs, grad_mixed)
-    rel_grads = product("ur,huc->hrc", spread, rel_table_grads).astype(low)
     grad_hidden = grad_sum + product("htc,hdc->td", qkv_grads, w_project)
     grad_words, grad_gain = back_in(grad_hidden)
     grad_vec = grad_vec + grad_gain
-    sent = grad_words.astype(low).reshape(seq_len, owners, width).transpose(1, 0, 2)
-    sent = lax.all_to_all(sent, "dp", 0, 0, tiled=True)
-    sent = lax.all_gather(sent[:, None], "heads", axis=1, tiled=True)
-    sent = sent.reshape(owners * row_count, seq_len, width)
+    sent = grad_words.astype(low).T.reshape(owners, width, seq_len)
+    if direct:
+        sent = return_words(sent, 3)
+    else:
+        sent = lax.all_to_all(sent, "dp", 0, 0, tiled=True)
+        sent = lax.all_gather(sent, "heads", axis=0)
+
+    rel_grads = product("ur,huc->hrc", spread, rel_table_grads).astype(low)
     grad_project = product("td,htc->hdc", hidden_low, qkv_grads)
     grad_rel_part = product("rd,hrc->hdc", rel_low, rel_grads)
     grad_project = jnp.concatenate(
@@ -440,31 +1015,52 @@
     grad_relative, grad_gain = back_rel(grad_rel_norm)
     grad_vec = grad_vec + grad_gain
     grad_relative = grad_relative.reshape(pieces, span_part, model).transpose(0, 2, 1).astype(low)
-    late = jnp.concatenate([grad_project, grad_relative], 2)
-    late = lax.psum_scatter(
-        late.reshape(pieces * model, -1), everyone, scatter_dimension=0, tiled=True
-    )
-    grad_vec = lax.psum(grad_vec, everyone)
-    grad_embedding = deposit(all_lengths, places, sent, slots)[:vocab_slab].T
-
-    early = early.astype(f32)
-    late = late.astype(f32)
-    squares_local = sum(jnp.sum(part * part) for part in (early, late, grad_embedding))
-    squares_total, loss_sum = lax.psum((squares_local, loss_part), everyone)
-    grad_norm = jnp.sqrt(squares_total + jnp.sum(grad_vec * grad_vec))
+    grad_vec = jnp.pad(grad_vec, ((0, pieces * vector_part - vector_count), (0, 0)))
+    grad_vec = grad_vec.reshape(pieces, vector_part, model).transpose(0, 2, 1).astype(low)
+    grad_vec = jnp.pad(grad_vec, ((0, 0), (0, 0), (0, BLOCK - vector_part)))
+
+    partial_grads = [
+        grad_contract,
+        grad_expand,
+        jnp.concatenate([grad_readout, grad_combine], 2),
+        grad_project,
+        jnp.concatenate([grad_relative, grad_vec], 2),
+    ]
+    if direct:
+        sums = scatter_sums(
+            [part.reshape(pieces, owners, width, -1) for part in partial_grads], 4
+        )
+    else:
+        sums = [
+            lax.psum_scatter(
+                part.reshape(pieces * model, -1), everyone, scatter_dimension=0, tiled=True
+            ).astype(f32)
+            for part in partial_grads
+        ]
+    grad_embedding, own_squares = deposit(all_lengths, places, sent, vocab_slab)
+
+    squares_local = sum(jnp.sum(part * part) for part in sums) + jnp.sum(own_squares)
+    shared = jnp.concatenate([sums[2][:, :head_width], sums[4]], 1)
+    if direct:
+        column = lax.broadcasted_iota(jnp.int32, (8, BLOCK), 1)
+        own_facts = jnp.where(column == 0, squares_local, jnp.where(column == 1, loss_part, 0.0))
+        all_facts, shared = finish_sums(own_facts, shared, 5)
+        squares_total, loss_sum = all_facts[0, 0], all_facts[0, 1]
+    else:
+        squares_total, loss_sum = lax.psum((squares_local, loss_part), everyone)
+        shared = lax.all_gather(shared, "heads", axis=0)
+    grad_norm = jnp.sqrt(squares_total)
     factor = jnp.minimum(1.0, clip_level / grad_norm)
 
-    grad_expand = early[:, :hidden]
-    grad_contract = early[:, hidden : 2 * hidden].T
-    grad_combine = early[:, 2 * hidden + head_width :].T
-    grad_project = late[:, : 3 * head_width].reshape(width, 3, head_width)
-    shared = jnp.concatenate(
-        [early[:, 2 * hidden : 2 * hidden + head_width], late[:, 3 * head_width :]], 1
-    )
-    shared = lax.all_gather(shared, "heads", axis=0, tiled=True).reshape(pieces, width, -1)
+    grad_contract = sums[0].T
+    grad_expand = sums[1]
+    grad_combine = sums[2][:, head_width:].T
+    grad_project = sums[3].reshape(width, 3, head_width)
     grad_readout = shared[:, :, :head_width].transpose(1, 0, 2).reshape(width, model)
-    grad_relative = shared[:, :, head_width:].transpose(0, 2, 1).reshape(entries, width)
-    grad_vec = lax.dynamic_slice_in_dim(grad_vec, owner * width, width, 1)
+    at = head_width + span_part
+    grad_relative = shared[:, :, head_width:at].transpose(0, 2, 1).reshape(entries, width)
+    grad_vec = shared[:, :, at : at + vector_part].transpose(0, 2, 1).reshape(-1, width)
+    grad_vec = grad_vec[:vector_count]
     weights = (embedding, relative, project, combine, expand, contract, readout, vectors)
     gradients = (
         grad_embedding,

time: 789 us -> 642 us (0.81)
  Pallas kernels: 138 us -> 372 us
  waiting for transfers between devices: 239 us -> 18.1 us
  blocking collectives: 105 us -> 0 us
  local copies, waits for them, and re-layouts: 117 us -> 53.2 us
  matrix products: 88 us -> 104 us
    pallas_call x0 -> x5, Pallas kernels: none -> 204 us  [the longest x1 106 us: scatter_sums(): pl.pallas_call(functools.partial(scatter_sums_kernel, count), in_specs=[A...]
    reduce_scatter x3 -> x0, waiting for transfers between devices: 180 us -> none  [the longest x1 110 us: per_device(): lax.psum_scatter(early.reshape(pieces * model, -1), everyone, scatter_dim...]
    all_gather x2 -> x0, blocking collectives: 40.6 us -> none  [the longest x1 32.3 us: per_device(): lax.all_gather(jnp.concatenate([token_ids, row_lengths[:, None]], 1), 'dp...]
    psum x1 -> x0, blocking collectives: 40.3 us -> none  [per_device(): squares_total, loss_sum = lax.psum((squares_local, loss_part), everyone)]
    unnamed x142 -> x182, local copies, waits for them, and re-layouts: 53.9 us -> 15.9 us
    all_to_all x1 -> x0, waiting for transfers between devices: 30 us -> none  [per_device(): found = lax.all_to_all(found, 'dp', 0, 0, tiled=True)]
    all_to_all x1 -> x0, blocking collectives: 24.5 us -> none  [per_device(): sent = lax.all_to_all(sent, 'dp', 0, 0, tiled=True)]
    pallas_call x1, Pallas kernels: 17.4 us -> 35.7 us  [lookup(): pl.pallas_call(lookup_kernel, grid=(rows,), in_specs=[pl.BlockSpec(memory...]
  transfers between devices with their start and end apart: 7 -> 2, of which waited for: 6 -> 1; matrix products, arithmetic and copies ran while one was open for 13% -> 7% of each run, Pallas kernels for 8% -> 19%
where the time goes in v2:
time: 642 us; the launch traced here: 632 us
  Pallas kernels  372 us (58%)
  matrix products  104 us (16%)
  other arithmetic  61.7 us (10%)
  local copies, waits for them, and re-layouts  53.2 us (8%)
  between operations  23.3 us (4%)
  waiting for transfers between devices  18.1 us (3%)
    pallas_call x1, Pallas kernels, scatter_sums(): pl.pallas_call(functools.partial(scatter_sums_kernel, count), in_specs=[A...  106 us
    dot_general x18, matrix products, product(): return jnp.einsum(form, matrix, operand, preferred_element_type=f32)  98.2 us
    pallas_call x1, Pallas kernels, attend_back(): pl.pallas_call(attend_back_kernel, grid=(groups,), in_specs=[pl.BlockSpec...  56.5 us
    pallas_call x1, Pallas kernels, deposit(): pl.pallas_call(deposit_kernel, grid=(rows,), in_specs=[pl.BlockSpec(memor...  40.4 us
    pallas_call x1, Pallas kernels, exchange_words(): pl.pallas_call(exchange_words_kernel, in_specs=[IN_VMEM], out_specs=IN_VM...  36 us
    pallas_call x1, Pallas kernels, lookup(): pl.pallas_call(lookup_kernel, grid=(rows,), in_specs=[pl.BlockSpec(memory...  35.7 us
    pallas_call x1, Pallas kernels, attend(): pl.pallas_call(attend_kernel, grid=(groups,), in_specs=[pl.BlockSpec(memo...  34.8 us
    pallas_call x1, Pallas kernels, return_words(): pl.pallas_call(return_words_kernel, in_specs=[IN_VMEM], out_specs=IN_VMEM...  25.9 us
  transfers between devices with their start and end apart: 2, of which 1 were waited for; matrix products, arithmetic and copies ran while one was open for 7% of the time, Pallas kernels for 19%

profile of v2, /device:TPU:0, one launch (start us, length us, event | category | flops | bytes accessed | tf_op | source)
XLA Modules:
  0.0 631.6 jit_solution(8253883045801958997)
XLA Ops:
  15.5 11.2 %share_facts.1 = s32[8,8,512]{2,1,0:T(8,128)} custom-call(s32[8,512]{1,0:T(8,128)} %pad_add_fusion.facts_ref), custom_call_target="tpu_custom_call" | custom-call | tf_op jit(solution)/shard_map/share_facts/pallas_call | solution.py:417
  29.7 35.7 %lookup.1.found_ref = bf16[4,8,96,512]{3,2,1,0:T(8,128)(2,1)S(1)} custom-call(s32[32]{0:T(128)S(1)} %reshape_squeeze.3.lengths_ref, s32[32,1,512]{2,1,0:T(1,128)S(1)} %and_select_fusion.places_ref, f32[96,12672]{1,0:T(8,128)} %weights_ref.1), custom_call_target="tpu_custom_call" | custom-call | tf_op jit(solution)/shard_map/lookup/pallas_call | solution.py:713
  65.5 36.0 %exchange_words.1 = bf16[8,96,512]{2,1,0:T(8,128)(2,1)S(1)} custom-call(bf16[4,8,96,512]{3,2,1,0:T(8,128)(2,1)S(1)} %lookup.1.found_ref), custom_call_target="tpu_custom_call" | custom-call | tf_op jit(solution)/shard_map/exchange_words/pallas_call | solution.py:502
  108.7 1.7 slice_convert_fusion.1
  110.6 1.6 copy.255
  113.5 2.2 slice_reduce_fusion.2
  115.7 6.0 fusion.48
  121.7 3.1 copy.253
  124.9 2.6 multiply_reduce_fusion.12
  128.0 7.1 %convert_bitcast_fusion.table_ref = bf16[4,1024,384]{2,1,0:T(8,128)(2,1)} fusion(bf16[4,768,1152]{2,1,0:T(8,128)(2,1)} %bitcast.359, bf16[512,768]{1,0:T(8,128)(2,1)S(1)} %add_convert_fusion.3, s32[1024]{0:T(1024)S(1)} %subtract_clamp_fusion), kind=kOutput, calls=%fused_computation.51 | convolution fusion | flops 3224109056 | bytes 6295552 | tf_op jit(solution)/shard_map/ud,hdc->huc/dot_general | solution.py:802
  135.2 34.8 %attend.1 = (bf16[12,512,512]{2,1,0:T(8,128)(2,1)}, bf16[4,512,192]{2,1,0:T(8,128)(2,1)S(1)}) custom-call(s32[1]{0:T(128)} %dynamic_slice.14.length_ref, bf16[4,512,576]{2,1,0:T(8,128)(2,1)S(1)} %bitcast.337, bf16[4,1024,384]{2,1,0:T(8,128)(2,1)} %convert_bitcast_fusion.table_ref), custom_call_target="tpu_custom_call" | custom-call | tf_op jit(solution)/shard_map/attend/pallas_call | solution.py:67
  170.0 4.4 fusion.162
  174.8 18.0 %all-gather.3.cloned.1.call-done = bf16[3072,1728]{1,0:T(8,128)(2,1)} async-done(((bf16[96,1728]{1,0:T(8,128)(2,1)}), bf16[3072,1728]{1,0:T(8,128)(2,1)}) %all-gather.3.cloned.1.call-update) | async-done | bytes 10616848 | tf_op jit(solution)/shard_map/all_gather | solution.py:903
  192.8 2.7 slice_bitcast_fusion
  195.5 20.7 %fusion.9 = (bf16[4,512,768]{1,2,0:T(8,128)(2,1)S(1)}, f32[4,512,768]{1,2,0:T(8,128)}, f32[4,768,512]{2,1,0:T(8,128)}) fusion(f32[512,768]{1,0:T(8,128)S(1)} %get-tuple-element.264, f32[768]{0:T(1024)S(1)} %get-tuple-element.214, f32[768]{0:T(1024)S(1)} %get-tuple-element.215, f32[512]{0:T(512)S(1)} %fusion.134, f32[512]{0:T(512)S(1)} %broadcast_multiply_fusion.4, ...), kind=kOutput, calls=%fused_computation.18 | convolution fusion | flops 2520121344 | bytes 22030336 | tf_op jit(solution)/shard_map/td,hdf->htf/dot_general | solution.py:802
  216.1 7.6 %fusion.160 = (f32[512]{0:T(512)S(1)}, f32[512,768]{1,0:T(8,128)S(1)}, f32[512,768,1]{1,0,2:T(8,128)}) fusion(f32[768]{0:T(1024)S(1)} %get-tuple-element.214, f32[768]{0:T(1024)S(1)} %get-tuple-element.215, f32[512]{0:T(512)S(1)} %fusion.134, f32[512,768]{1,0:T(8,128)S(1)} %get-tuple-element.264, f32[512]{0:T(512)S(1)} %broadcast_multiply_fusion.4, ...), kind=kOutput, calls=%fused_computation.319 | convolution fusion | flops 2418277888 | bytes 12595200 | tf_op jit(solution)/shard_map/htf,hdf->td/dot_general | solution.py:802
  224.0 2.9 copy.260
  226.9 5.6 fusion.158
  240.3 8.9 %fusion.6 = bf16[4,512,768]{1,2,0:T(8,128)(2,1)S(1)} fusion(f32[4,512,768]{1,2,0:T(8,128)} %get-tuple-element.262, f32[4,768,512]{2,1,0:T(8,128)} %get-tuple-element.277, bf16[4,768,1728]{2,1,0:T(8,128)(2,1)S(1)} %bitcast.369, f32[512,768]{1,0:T(8,128)S(1)} %get-tuple-element.255, f32[512]{0:T(512)S(1)} %negate_multiply_fusion.5), kind=kOutput, calls=%fused_computation.10 | convolution fusion | flops 2438725632 | bytes 22022144 | tf_op jit(solution)/shard_map/td,hdf->htf/dot_general | solution.py:802
  249.2 4.5 multiply_reduce_fusion.2
  255.5 3.3 convolution_convert_fusion.4
  259.3 56.5 %attend_back.1 = (bf16[4,512,576]{2,1,0:T(8,128)(2,1)S(1)}, bf16[4,1024,384]{2,1,0:T(8,128)(2,1)}) custom-call(bf16[4,512,576]{2,1,0:T(8,128)(2,1)} %bitcast.338, bf16[4,1024,384]{2,1,0:T(8,128)(2,1)} %convert_bitcast_fusion.table_ref, bf16[12,512,512]{2,1,0:T(8,128)(2,1)} %get-tuple-element.42.probs_ref, bf16[4,512,192]{2,1,0:T(8,128)(2,1)S(1)} %bitcast.340), custom_call_target="tpu_custom_call" | custom-call | tf_op jit(solution)/shard_map/attend_back/pallas_call | solution.py:126
  315.9 6.1 fusion.78
  322.0 2.2 convolution_bitcast_fusion
  324.2 2.0 fusion.51
  326.2 4.6 multiply_reduce_fusion.5
  330.8 2.8 fusion.23
  336.2 3.5 fusion.85
  339.6 6.8 %convolution_convert_fusion = bf16[4,768,768]{1,2,0:T(8,128)(2,1)} fusion(bf16[4,512,768]{1,2,0:T(8,128)(2,1)} %copy-done.78, f32[512,768]{1,0:T(8,128)S(1)} %copy-done.16, f32[768]{0:T(1024)S(1)} %get-tuple-element.214, f32[768]{0:T(1024)S(1)} %get-tuple-element.215, f32[512]{0:T(512)S(1)} %fusion.134, f32[512]{0:T(512)S(1)} %broadcast_multiply_fusion.4), kind=kOutput, calls=%fused_computation.57 | convolution fusion | flops 2420244480 | bytes 9447424 | tf_op jit(solution)/shard_map/td,htf->hdf/dot_general | solution.py:802
  346.5 4.5 convolution_convert_fusion.1
  351.0 1.6 fusion.66
  353.2 1.6 copy.279
  354.8 4.3 copy.274
  359.0 2.6 copy.275
  361.7 2.2 fusion.86
  365.4 4.4 copy.270
  369.9 4.1 pad_maximum_fusion.refs_3_
  374.0 106.5 %scatter_sums.1 = (f32[96,768]{1,0:T(8,128)}, f32[96,768]{1,0:T(8,128)}, f32[96,384]{1,0:T(8,128)}, f32[96,576]{1,0:T(8,128)}, f32[96,256]{1,0:T(8,128)}) custom-call(bf16[4,4,2,96,768]{4,3,2,1,0:T(8,128)(2,1)} %bitcast.349, bf16[4,4,2,96,768]{4,3,2,1,0:T(8,128)(2,1)} %bitcast.348, bf16[4,4,2,96,384]{4,3,2,1,0:T(8,128)(2,1)} %bitcast.345, ...), custom_call_target="tpu_custom_call" | custom-call | tf_op jit(solution)/shard_map/scatter_sums/pallas_call | solution.py:359
  484.5 1.7 pad_maximum_fusion.3.shared_ref
  486.2 4.1 fusion.84
  490.5 25.9 %return_words.1.grads_ref = bf16[4,8,96,512]{3,2,1,0:T(8,128)(2,1)S(1)} custom-call(bf16[8,96,512]{2,1,0:T(8,128)(2,1)S(1)} %bitcast.341), custom_call_target="tpu_custom_call" | custom-call | tf_op jit(solution)/shard_map/return_words/pallas_call | solution.py:581
  516.5 1.7 copy-done.1
  518.2 40.4 %deposit.1 = (f32[96,12672]{1,0:T(8,128)}, f32[96,128]{1,0:T(8,128)}) custom-call(s32[32]{0:T(128)} %copy-done.3, s32[32,1,512]{2,1,0:T(1,128)} %copy-done.2, bf16[4,8,96,512]{3,2,1,0:T(8,128)(2,1)} %copy-done.1), custom_call_target="tpu_custom_call" | custom-call | tf_op jit(solution)/shard_map/deposit/pallas_call | solution.py:773
  567.2 24.3 %finish_sums.1 = (f32[8,128]{1,0:T(8,128)}, f32[4,96,448]{2,1,0:T(8,128)}) custom-call(f32[8,128]{1,0:T(8,128)} %broadcast_select_fusion.facts_ref, f32[96,448]{1,0:T(8,128)} %pad_maximum_fusion.3.shared_ref), custom_call_target="tpu_custom_call" | custom-call | tf_op jit(solution)/shard_map/finish_sums/pallas_call | solution.py:646
  601.2 1.9 copy.293
  607.7 2.0 multiply_subtract_fusion.5
  609.7 2.0 multiply_subtract_fusion.1
  611.7 10.3 %multiply_subtract_fusion = (f32[96,12672]{1,0:T(8,128)}, f32[96,12672]{1,0:T(8,128)}, f32[96,12672]{1,0:T(8,128)}) fusion(f32[96,12672]{1,0:T(8,128)S(1)} %bitcast.343, f32[96,12672]{1,0:T(8,128)} %get-tuple-element.52, f32[]{:T(128)S(6)} %min.15, f32[96,12672]{1,0:T(8,128)} %param.46, f32[96,12672]{1,0:T(8,128)} %param.38), kind=kLoop, calls=%fused_computation.33 | loop fusion | flops 19464192 | bytes 34062340 | tf_op jit(solution)/shard_map/sub | solution.py:836
  (293 shorter events, 57.1 us)
Async XLA Ops:
  7.2 5.2 copy-start.32
  7.2 100.9 %all-gather.5.cloned.1.call-start = ((), (), s32[]{:S(2)}) async-start(), calls=%async_computation.1 | async-start | bytes 7299072 | tf_op jit(solution)/shard_map/all_gather | solution.py:901
  11.4 181.4 %all-gather.3.cloned.1.call-start = ((), (), s32[]{:S(2)}) async-start(), calls=%async_computation | async-start | bytes 11354112 | tf_op jit(solution)/shard_map/all_gather | solution.py:903
  29.7 35.7 %copy-start.2 = (s32[32,1,512]{2,1,0:T(1,128)}, s32[32,1,512]{2,1,0:T(1,128)S(1)}, u32[]{:S(2)}) copy-start(s32[32,1,512]{2,1,0:T(1,128)S(1)} %and_select_fusion.places_ref) | copy-start | bytes 196612
  101.8 13.9 %copy-start.6 = (f32[768,512]{0,1:T(8,128)}, f32[768,512]{0,1:T(8,128)S(1)}, u32[]{:S(2)}) copy-start(f32[768,512]{0,1:T(8,128)S(1)} %copy.248) | copy-start | bytes 4718596
  124.8 10.3 %copy-start = (bf16[4,576,512]{1,2,0:T(8,128)(2,1)}, bf16[4,576,512]{1,2,0:T(8,128)(2,1)S(1)}, u32[]{:S(2)}) copy-start(bf16[4,576,512]{1,2,0:T(8,128)(2,1)S(1)} %copy.253) | copy-start | bytes 7077892
  127.4 7.7 %copy-start.68 = (f32[4,128]{1,0:T(4,128)}, f32[4,128]{1,0:T(4,128)S(1)}, u32[]{:S(2)}) copy-start(f32[4,128]{1,0:T(4,128)S(1)} %multiply_reduce_fusion.12) | copy-start | bytes 6148
  128.0 7.2 %copy-start.22 = (bf16[512,768]{1,0:T(8,128)(2,1)}, bf16[512,768]{1,0:T(8,128)(2,1)S(1)}, u32[]{:S(2)}) copy-start(bf16[512,768]{1,0:T(8,128)(2,1)S(1)} %add_convert_fusion.3) | copy-start | bytes 2359300
  135.2 34.9 %copy-start.7 = (f32[768,512]{0,1:T(8,128)S(1)}, f32[768,512]{0,1:T(8,128)}, u32[]{:S(2)}) copy-start(f32[768,512]{0,1:T(8,128)} %copy-done.6) | copy-start | bytes 4718596
  170.0 4.4 copy-start.4
  174.4 79.2 %copy-start.15 = (f32[512,768]{1,0:T(8,128)}, f32[512,768]{1,0:T(8,128)S(1)}, u32[]{:S(2)}) copy-start(f32[512,768]{1,0:T(8,128)S(1)} %get-tuple-element.264) | copy-start | bytes 4718596
  216.1 7.6 %copy-start.76 = (bf16[4,512,768]{1,2,0:T(8,128)(2,1)}, bf16[4,512,768]{1,2,0:T(8,128)(2,1)S(1)}, u32[]{:S(2)}) copy-start(bf16[4,512,768]{1,2,0:T(8,128)(2,1)S(1)} %get-tuple-element.261) | copy-start | bytes 9437188
  223.7 15.3 %copy-start.13 = (f32[512,768]{1,0:T(8,128)}, f32[512,768]{1,0:T(8,128)S(1)}, u32[]{:S(2)}) copy-start(f32[512,768]{1,0:T(8,128)S(1)} %get-tuple-element.260) | copy-start | bytes 4718596
  226.9 13.3 %slice-start.2 = ((s8[11010048]{0:T(1024)(128)(4,1)}), s8[4194304]{0:T(1024)(128)(4,1)S(1)}, s32[]{:S(2)}) async-start(s8[11010048]{0:T(1024)(128)(4,1)} %bitcast.367), calls=%async_computation.4 | async-start | bytes 8388608
  226.9 13.3 %slice-start.3 = ((s8[11010048]{0:T(1024)(128)(4,1)}), s8[4194304]{0:T(1024)(128)(4,1)S(1)}, s32[]{:S(2)}) async-start(s8[11010048]{0:T(1024)(128)(4,1)} %bitcast.367), calls=%async_computation.5 | async-start | bytes 8388608
  232.8 7.4 %slice-start.4 = ((s8[11010048]{0:T(1024)(128)(4,1)}), s8[2621440]{0:T(1024)(128)(4,1)S(1)}, s32[]{:S(2)}) async-start(s8[11010048]{0:T(1024)(128)(4,1)} %bitcast.367), calls=%async_computation.6 | async-start | bytes 5242880
  240.2 8.9 %copy-start.24 = (f32[512,768]{1,0:T(8,128)}, f32[512,768]{1,0:T(8,128)S(1)}, u32[]{:S(2)}) copy-start(f32[512,768]{1,0:T(8,128)S(1)} %get-tuple-element.255) | copy-start | bytes 4718596
  249.1 4.5 copy-start.78
  259.3 56.6 %copy-start.8 = (f32[768,512]{0,1:T(8,128)S(1)}, f32[768,512]{0,1:T(8,128)}, u32[]{:S(2)}) copy-start(f32[768,512]{0,1:T(8,128)} %copy-done.6) | copy-start | bytes 4718596
  259.3 56.6 %copy-start.27 = (f32[512,768]{1,0:T(8,128)S(1)}, f32[512,768]{1,0:T(8,128)}, u32[]{:S(2)}) copy-start(f32[512,768]{1,0:T(8,128)} %copy-done.26) | copy-start | bytes 4718596
  326.2 4.6 copy-start.23
  339.6 6.8 %copy-start.25 = (f32[512,768]{1,0:T(8,128)S(1)}, f32[512,768]{1,0:T(8,128)}, u32[]{:S(2)}) copy-start(f32[512,768]{1,0:T(8,128)} %copy-done.24) | copy-start | bytes 4718596
  339.6 6.8 %copy-start.77 = (bf16[4,512,768]{1,2,0:T(8,128)(2,1)S(1)}, bf16[4,512,768]{1,2,0:T(8,128)(2,1)}, u32[]{:S(2)}) copy-start(bf16[4,512,768]{1,2,0:T(8,128)(2,1)} %copy-done.76) | copy-start | bytes 9437188
  346.4 4.5 copy-start.69
  346.4 4.5 copy-start.67
  346.4 4.5 copy-start.12
  346.5 4.5 copy-start.30
  346.5 4.5 copy-start.31
  365.4 4.4 copy-start.19
  374.0 112.2 %copy-start.18 = (f32[512,768]{1,0:T(8,128)S(1)}, f32[512,768]{1,0:T(8,128)}, u32[]{:S(2)}) copy-start(f32[512,768]{1,0:T(8,128)} %copy-done.17) | copy-start | bytes 4718596
  374.0 112.2 %copy-start.28 = (f32[512,768,1]{1,0,2:T(8,128)S(1)}, f32[512,768,1]{1,0,2:T(8,128)}, u32[]{:S(2)}) copy-start(f32[512,768,1]{1,0,2:T(8,128)} %get-tuple-element.276) | copy-start | bytes 4718596
  374.0 112.2 %copy-start.29 = (f32[512,768,1]{1,0,2:T(8,128)S(1)}, f32[512,768,1]{1,0,2:T(8,128)}, u32[]{:S(2)}) copy-start(f32[512,768,1]{1,0,2:T(8,128)} %get-tuple-element.278) | copy-start | bytes 4718596
  518.2 40.4 %copy-start.36 = (f32[96,768]{1,0:T(8,128)S(1)}, f32[96,768]{1,0:T(8,128)}, u32[]{:S(2)}) copy-start(f32[96,768]{1,0:T(8,128)} %get-tuple-element.46) | copy-start | bytes 884740
  518.2 41.1 %copy-start.37 = (f32[96,768]{1,0:T(8,128)S(1)}, f32[96,768]{1,0:T(8,128)}, u32[]{:S(2)}) copy-start(f32[96,768]{1,0:T(8,128)} %get-tuple-element.45) | copy-start | bytes 884740
  518.2 41.8 %copy-start.45 = (f32[96,576]{1,0:T(8,128)S(1)}, f32[96,576]{1,0:T(8,128)}, u32[]{:S(2)}) copy-start(f32[96,576]{1,0:T(8,128)} %get-tuple-element.48) | copy-start | bytes 663556
  518.2 48.4 %copy-start.74 = (pred[128]{0:T(512)(128)(4,1)S(1)}, pred[128]{0:T(512)(128)(4,1)}, u32[]{:S(2)}) copy-start(pred[128]{0:T(512)(128)(4,1)} %iota_compare_fusion.11) | copy-start | bytes 388
  592.6 5.1 copy-start.46
  592.6 5.0 copy-start.49
  592.6 5.0 copy-start.50
  592.6 5.0 copy-start.51
  600.0 11.7 %slice-start = ((s8[4866048]{0:T(1024)(128)(4,1)}), s8[671744]{0:T(1024)(128)(4,1)S(1)}, s32[]{:S(2)}) async-start(s8[4866048]{0:T(1024)(128)(4,1)} %bitcast.342), calls=%async_computation.2 | async-start | bytes 1343488
  600.2 4.6 copy-start.65
  600.2 4.6 copy-start.71
  600.2 4.6 copy-start.72
  600.2 5.3 copy-start.33
  601.2 4.3 copy-start.54
  601.2 6.5 %copy-start.61 = (f32[512,96]{0,1:T(8,128)S(1)}, f32[512,96]{0,1:T(8,128)}, u32[]{:S(2)}) copy-start(f32[512,96]{0,1:T(8,128)} %param.39) | copy-start | bytes 589828
  605.5 6.2 slice-start.1
  (38 other events, 102.0 us)
Sparse Core Ops, SparseCore 0:
  11.6 89.8 all-gather.4
  105.1 87.6 all-gather.2

commit v3 on v2

--- a/solution.py
+++ b/solution.py
@@ -10,7 +10,7 @@
 HEAD_DIM = 64
 STEP = 10
 BLOCK = 128
-UNROLL = 8
+UNROLL = 16
 
 low = jnp.bfloat16
 f32 = jnp.float32
@@ -442,7 +442,7 @@
     def pair_copy(part, row):
         to = targets[part][0] * 2 + targets[part][1]
         return remote(
-            found_ref.at[row * 2 + 1 - c, to],
+            found_ref.at[to, row * 2 + 1 - c],
             pair.at[row, to],
             send_sem.at[part, row],
             recv_sem.at[part, row],
@@ -475,7 +475,7 @@
         to = at_home(part)
         for row in range(2):
             pair_copy(part, row).wait_recv()
-            pair[row, to] = pair[row, to] + found_ref[row * 2 + c, to]
+            pair[row, to] = pair[row, to] + found_ref[to, row * 2 + c]
         side_copy(part).start()
     for part in range(8):
         to = at_home(part)
@@ -529,13 +529,13 @@
     other = (1 - y) * 2 + c
     core_to, y_to = device(z, x, y, 1 - c), device(z, x, 1 - y, c)
     near_first = peers(z, x)[::-1]
-    keep = pltpu.make_async_copy(grads_ref.at[here], sent_ref.at[own, here], local_sem)
+    keep = pltpu.make_async_copy(grads_ref.at[here], sent_ref.at[here, own], local_sem)
     keep.start()
 
     def out_copy(part, peer):
         return remote(
             grads_ref.at[peer[0] * 2 + peer[1]],
-            sent_ref.at[own, here],
+            sent_ref.at[here, own],
             out_sem.at[part],
             in_sem.at[here],
             device(peer[0], peer[1], y, c),
@@ -544,11 +544,11 @@
     def in_copy(part, peer):
         there = peer[0] * 2 + peer[1]
         return remote(
-            grads_ref.at[there], sent_ref.at[own, there], out_sem.at[part], in_sem.at[there], core_to
+            grads_ref.at[there], sent_ref.at[there, own], out_sem.at[part], in_sem.at[there], core_to
         )
 
     def pass_on(slot, row, there, to):
-        block = sent_ref.at[row, there]
+        block = sent_ref.at[there, row]
         return remote(block, block, send_sem.at[slot, there], recv_sem.at[row, there], to)
 
     for part, peer in enumerate(peers(z, x)):
@@ -582,7 +582,7 @@
         return_words_kernel,
         in_specs=[IN_VMEM],
         out_specs=IN_VMEM,
-        out_shape=jax.ShapeDtypeStruct((4, 8) + piece, low),
+        out_shape=jax.ShapeDtypeStruct((8, 4) + piece, low),
         scratch_shapes=[
             pltpu.SemaphoreType.DMA,
             pltpu.SemaphoreType.DMA((7,)),
@@ -675,148 +675,442 @@
     return dot_rows(identity(values.shape[1]), values)
 
 
+def row_sets(rows):
+    return 8 if rows % 8 == 0 else 1
+
+
 def lookup_kernel(lengths_ref, places_ref, weights_ref, words_ref, table_ref, rows_ref):
     width, slab = weights_ref.shape
+    count = places_ref.shape[1]
+    seq = rows_ref.shape[0]
 
     @pl.when(pl.program_id(0) == 0)
     def fill():
         def step(index, carry):
-            first = pl.multiple_of(index * BLOCK, BLOCK)
-            table_ref[pl.ds(first, BLOCK), :] = turn(weights_ref[:, pl.ds(first, BLOCK)].astype(low))
+            first = pl.multiple_of(index * 3 * BLOCK, BLOCK)
+            for part in range(3):
+                at = first + part * BLOCK
+                table_ref[pl.ds(at, BLOCK), :] = turn(weights_ref[:, pl.ds(at, BLOCK)].astype(low))
             return carry
 
-        lax.fori_loop(0, slab // BLOCK, step, 0)
+        lax.fori_loop(0, slab // (3 * BLOCK), step, 0)
         table_ref[pl.ds(slab, 8), :] = jnp.zeros((8, width), f32)
 
-    rows_ref[...] = jnp.zeros_like(rows_ref)
-
-    def step(index, carry):
-        first = pl.multiple_of(index * UNROLL, UNROLL)
-        for offset in range(UNROLL):
-            spot = places_ref[0, 0, first + offset]
-            rows_ref[pl.ds(first + offset, 1), :] = table_ref[pl.ds(spot, 1), :]
+    def one_row(row, carry):
+        rows_ref[...] = jnp.zeros_like(rows_ref)
+
+        def step(index, carry):
+            first = pl.multiple_of(index * UNROLL, UNROLL)
+            for offset in range(UNROLL):
+                spot = places_ref[0, row, first + offset]
+                rows_ref[pl.ds(first + offset, 1), :] = table_ref[pl.ds(spot, 1), :]
+            return carry
+
+        length = lengths_ref[pl.program_id(0) * count + row]
+        lax.fori_loop(0, pl.cdiv(length, UNROLL), step, 0)
+        words_ref[row] = dot_rows(identity(width), rows_ref[...].astype(low)).astype(low)
         return carry
 
-    lax.fori_loop(0, pl.cdiv(lengths_ref[pl.program_id(0)], UNROLL), step, 0)
-    seq = rows_ref.shape[0]
-    for first in range(0, seq, BLOCK):
-        words_ref[0, 0, :, first : first + BLOCK] = turn_block(rows_ref[first : first + BLOCK, :])
-
-
-def turn_block(rows):
-    return dot_rows(identity(rows.shape[1]), rows.astype(low)).astype(low)
-
-
-def lookup(lengths, places, weights, row_count):
+    lax.fori_loop(0, count, one_row, 0)
+
+
+def lookup(lengths, places, weights):
     rows, seq = places.shape
     width, slab = weights.shape
+    count = row_sets(rows)
     return pl.pallas_call(
         lookup_kernel,
-        grid=(rows,),
+        grid=(rows // count,),
         in_specs=[
             pl.BlockSpec(memory_space=pltpu.SMEM),
-            pl.BlockSpec((1, 1, seq), lambda row: (row, 0, 0), memory_space=pltpu.SMEM),
-            pl.BlockSpec(weights.shape, lambda row: (0, 0)),
-        ],
-        out_specs=pl.BlockSpec(
-            (1, 1, width, seq), lambda row: (row % row_count, row // row_count, 0, 0)
-        ),
-        out_shape=jax.ShapeDtypeStruct((row_count, rows // row_count, width, seq), low),
+            pl.BlockSpec((1, count, seq), lambda step: (step, 0, 0), memory_space=pltpu.SMEM),
+            pl.BlockSpec(weights.shape, lambda step: (0, 0)),
+        ],
+        out_specs=pl.BlockSpec((count, width, seq), lambda step: (step, 0, 0)),
+        out_shape=jax.ShapeDtypeStruct((rows, width, seq), low),
         scratch_shapes=[pltpu.VMEM((slab + 8, width), f32), pltpu.VMEM((seq, width), f32)],
         compiler_params=pltpu.CompilerParams(vmem_limit_bytes=48 << 20),
         name="lookup",
-    )(lengths, places[:, None], weights)
+    )(lengths, places.reshape(rows // count, count, seq), weights)
 
 
 def deposit_kernel(lengths_ref, places_ref, grads_ref, total_ref, squares_ref, rows_ref, *tables):
     width, slab = total_ref.shape
+    count = places_ref.shape[1]
 
     @pl.when(pl.program_id(0) == 0)
     def clear():
         for table in tables:
             table[...] = jnp.zeros_like(table)
 
-    for first in range(0, rows_ref.shape[0], BLOCK):
-        rows_ref[first : first + BLOCK, :] = turn(grads_ref[0, 0, :, first : first + BLOCK])
-
-    def step(index, carry):
-        first = pl.multiple_of(index * UNROLL, UNROLL)
-        for offset in range(0, UNROLL, len(tables)):
-            places = [places_ref[0, 0, first + offset + part] for part in range(len(tables))]
-            sums = [
-                table[pl.ds(place, 1), :] + rows_ref[pl.ds(first + offset + part, 1), :]
-                for part, (place, table) in enumerate(zip(places, tables))
-            ]
-            for place, table, value in zip(places, tables, sums):
-                table[pl.ds(place, 1), :] = value
+    def one_row(row, carry):
+        for first in range(0, rows_ref.shape[0], BLOCK):
+            rows_ref[first : first + BLOCK, :] = turn(grads_ref[row, :, first : first + BLOCK])
+
+        def step(index, carry):
+            first = pl.multiple_of(index * UNROLL, UNROLL)
+            for offset in range(0, UNROLL, len(tables)):
+                places = [places_ref[0, row, first + offset + part] for part in range(len(tables))]
+                sums = [
+                    table[pl.ds(place, 1), :] + rows_ref[pl.ds(first + offset + part, 1), :]
+                    for part, (place, table) in enumerate(zip(places, tables))
+                ]
+                for place, table, value in zip(places, tables, sums):
+                    table[pl.ds(place, 1), :] = value
+            return carry
+
+        length = lengths_ref[pl.program_id(0) * count + row]
+        lax.fori_loop(0, pl.cdiv(length, UNROLL), step, 0)
         return carry
 
-    lax.fori_loop(0, pl.cdiv(lengths_ref[pl.program_id(0)], UNROLL), step, 0)
+    lax.fori_loop(0, count, one_row, 0)
 
     @pl.when(pl.program_id(0) == pl.num_programs(0) - 1)
     def finish():
         squares_ref[...] = jnp.zeros_like(squares_ref)
 
         def step(index, carry):
-            first = pl.multiple_of(index * BLOCK, BLOCK)
-            block = sum(table[pl.ds(first, BLOCK), :] for table in tables).T
-            total_ref[:, pl.ds(first, BLOCK)] = block
-            squares_ref[...] += block * block
+            first = pl.multiple_of(index * 3 * BLOCK, BLOCK)
+            squares = jnp.zeros((width, BLOCK), f32)
+            for part in range(3):
+                at = pl.ds(first + part * BLOCK, BLOCK)
+                block = sum(table[at, :] for table in tables).T
+                total_ref[:, at] = block
+                squares += block * block
+            squares_ref[...] += squares
             return carry
 
-        lax.fori_loop(0, slab // BLOCK, step, 0)
+        lax.fori_loop(0, slab // (3 * BLOCK), step, 0)
 
 
 def deposit(lengths, places, grads, slab):
     rows, seq = places.shape
-    row_count, width = grads.shape[0], grads.shape[2]
+    width = grads.shape[1]
+    count = row_sets(rows)
     return pl.pallas_call(
         deposit_kernel,
-        grid=(rows,),
+        grid=(rows // count,),
         in_specs=[
             pl.BlockSpec(memory_space=pltpu.SMEM),
-            pl.BlockSpec((1, 1, seq), lambda row: (row, 0, 0), memory_space=pltpu.SMEM),
-            pl.BlockSpec(
-                (1, 1, width, seq), lambda row: (row % row_count, row // row_count, 0, 0)
-            ),
+            pl.BlockSpec((1, count, seq), lambda step: (step, 0, 0), memory_space=pltpu.SMEM),
+            pl.BlockSpec((count, width, seq), lambda step: (step, 0, 0)),
         ],
         out_specs=[
-            pl.BlockSpec((width, slab), lambda row: (0, 0)),
-            pl.BlockSpec((width, BLOCK), lambda row: (0, 0)),
+            pl.BlockSpec((width, slab), lambda step: (0, 0)),
+            pl.BlockSpec((width, BLOCK), lambda step: (0, 0)),
         ],
         out_shape=[
             jax.ShapeDtypeStruct((width, slab), f32),
             jax.ShapeDtypeStruct((width, BLOCK), f32),
         ],
         scratch_shapes=[pltpu.VMEM((seq, width), f32)] + [pltpu.VMEM((slab + 8, width), f32)] * 4,
+        compiler_params=pltpu.CompilerParams(vmem_limit_bytes=60 << 20),
+        name="deposit",
+    )(lengths, places.reshape(rows // count, count, seq), grads)
+
+
+def whiten(values):
+    center = values - jnp.mean(values, -1, keepdims=True)
+    rate = lax.rsqrt(jnp.mean(center * center, -1, keepdims=True) + layer_eps)
+    return center * rate, rate
+
+
+def unwhiten(upstream, gain, white, rate):
+    scaled = upstream * gain
+    inner = jnp.mean(scaled, -1, keepdims=True)
+    along = jnp.mean(scaled * white, -1, keepdims=True)
+    return (
+        rate * (scaled - inner - white * along),
+        jnp.sum(upstream * white, 0, keepdims=True),
+        jnp.sum(upstream, 0, keepdims=True),
+    )
+
+
+def selection(length, entries):
+    rows = lax.broadcasted_iota(jnp.int32, (2 * length, entries), 0)
+    columns = lax.broadcasted_iota(jnp.int32, (2 * length, entries), 1)
+    return (jnp.clip(length + entries // 2 - rows, 0, entries - 1) == columns).astype(f32).astype(low)
+
+
+def prepare_kernel(
+    weights_ref, words_ref, vec_ref, white_ref, rate_ref, qkv_ref, rel_white_ref, rel_rate_ref, table_ref, low_ref, rel_ref
+):
+    groups, model = weights_ref.shape[:2]
+    seq = words_ref.shape[1]
+    part = rel_ref.shape[0] // groups
+    width = qkv_ref.shape[2] // 3
+    terms = turn(weights_ref[0, :, 4 * BLOCK : 5 * BLOCK])
+    half = BLOCK // 2
+    vec_ref[...] = terms[half : half + 16] + terms[half + 16 : half + 32] + terms[half + 32 : half + 48]
+    for group in range(groups):
+        rows = slice(group * part, (group + 1) * part)
+        entries = turn(weights_ref[group, :, 5 * BLOCK : 6 * BLOCK]) + turn(
+            weights_ref[group, :, 8 * BLOCK : 9 * BLOCK]
+        )
+        white, rate = whiten(entries)
+        rel_white_ref[rows, :] = white
+        rel_rate_ref[rows, :] = rate
+        rel_ref[rows, :] = (white * vec_ref[2:3] + vec_ref[3:4]).astype(low)
+    for first in range(0, seq, BLOCK):
+        rows = slice(first, first + BLOCK)
+        white, rate = whiten(turn(words_ref[:, rows]))
+        white_ref[rows, :] = white
+        rate_ref[rows, :] = rate
+        low_ref[rows, :] = (white * vec_ref[0:1] + vec_ref[1:2]).astype(low)
+    chosen = selection(seq, rel_ref.shape[0])
+
+    def step(group, carry):
+        qkv_ref[group] = dot_plain(low_ref[...], weights_ref[group, :, : 3 * width]).astype(low)
+        keys = dot_plain(rel_ref[...], weights_ref[group, :, : 2 * width]).astype(low)
+        table_ref[group] = dot_plain(chosen, keys).astype(low)
+        return carry
+
+    lax.fori_loop(0, groups, step, 0)
+
+
+def prepare(weights, words, width, entries):
+    groups, model = weights.shape[:2]
+    seq = words.shape[1]
+    return pl.pallas_call(
+        prepare_kernel,
+        in_specs=[IN_VMEM] * 2,
+        out_specs=[IN_VMEM] * 7,
+        out_shape=[
+            jax.ShapeDtypeStruct((16, model), f32),
+            jax.ShapeDtypeStruct((seq, model), f32),
+            jax.ShapeDtypeStruct((seq, 1), f32),
+            jax.ShapeDtypeStruct((groups, seq, 3 * width), low),
+            jax.ShapeDtypeStruct((entries, model), f32),
+            jax.ShapeDtypeStruct((entries, 1), f32),
+            jax.ShapeDtypeStruct((groups, 2 * seq, 2 * width), low),
+        ],
+        scratch_shapes=[pltpu.VMEM((seq, model), low), pltpu.VMEM((entries, model), low)],
         compiler_params=pltpu.CompilerParams(vmem_limit_bytes=56 << 20),
-        name="deposit",
-    )(lengths, places[:, None], grads)
-
-
-def matmul(matrix, operand):
-    return jnp.dot(matrix, operand, preferred_element_type=f32)
-
-
-def product(form, matrix, operand):
-    return jnp.einsum(form, matrix, operand, preferred_element_type=f32)
-
-
-def normalize(values, gain_row, bias_row):
-    center = values - jnp.mean(values, -1, keepdims=True)
-    spread_sq = jnp.mean(center * center, -1, keepdims=True)
-    return center * lax.rsqrt(spread_sq + layer_eps) * gain_row + bias_row
-
-
-def gelu(values):
-    return jax.nn.gelu(values, approximate=False)
-
-
-def norm_at(first_row):
-    def apply_norm(values, gain_rows):
-        return normalize(values, gain_rows[first_row], gain_rows[first_row + 1])
-
-    return apply_norm
+        name="prepare",
+    )(weights, words)
+
+
+def middle_kernel(
+    combine_ref,
+    weights_ref,
+    vec_ref,
+    white_ref,
+    mixed_ref,
+    marks_ref,
+    contract_out,
+    expand_out,
+    joint_out,
+    mixed_out,
+    sum_out,
+    vec_out,
+    loss_out,
+    readout_ref,
+    slope_ref,
+    acts_ref,
+    mid_ref,
+    mid_white_ref,
+    out_white_ref,
+    gate_ref,
+):
+    groups, model = weights_ref.shape[:2]
+    seq = white_ref.shape[0]
+    width = mixed_ref.shape[2]
+    hidden = acts_ref.shape[2]
+    vec = [vec_ref[row : row + 1] for row in range(11)]
+    for group in range(groups):
+        readout_ref[:, group * width : (group + 1) * width] = weights_ref[group, :, 2 * hidden :]
+    total = white_ref[...] * vec[0] + vec[1]
+    for group in range(groups):
+        total += dot_rows(mixed_ref[group], combine_ref[group, :, :width])
+    mid_white, mid_rate = whiten(total)
+    mid_white_ref[...] = mid_white
+    hidden_mid = mid_white * vec[4] + vec[5]
+    sum_out[...] = hidden_mid
+    mid_ref[...] = hidden_mid.astype(low)
+
+    def forward(group, carry):
+        gate = dot_plain(mid_ref[...], weights_ref[group, :, :hidden])
+        share = 0.5 + 0.5 * lax.erf(gate * 0.5**0.5)
+        acts_ref[group] = (gate * share).astype(low)
+        slope_ref[group] = share + gate * jnp.exp(-0.5 * gate * gate) * (2.0 * jnp.pi) ** -0.5
+        sum_out[...] += dot_rows(acts_ref[group], weights_ref[group, :, hidden : 2 * hidden])
+        return carry
+
+    lax.fori_loop(0, groups, forward, 0)
+    out_white, out_rate = whiten(sum_out[...])
+    out_white_ref[...] = out_white
+    gate_ref[...] = (out_white * vec[6] + vec[7]).astype(low)
+    dense = dot_plain(gate_ref[...], readout_ref[...])
+    share = 0.5 + 0.5 * lax.erf(dense * 0.5**0.5)
+    slope = share + dense * jnp.exp(-0.5 * dense * dense) * (2.0 * jnp.pi) ** -0.5
+    white, rate = whiten(dense * share)
+    head = white * vec[8] + vec[9]
+    logits = jnp.sum(head * vec[10], -1, keepdims=True)
+    weight, flags = marks_ref[:, 0:1], marks_ref[:, 1:2]
+    losses = jnp.maximum(logits, 0.0) + jnp.log1p(jnp.exp(-jnp.abs(logits))) - flags * logits
+    loss_out[...] = jnp.where(weight > 0.0, losses, 0.0)
+    pull = (1.0 / (1.0 + jnp.exp(-logits)) - flags) * weight
+    vec_out[6:7, :] = jnp.sum(head * pull, 0, keepdims=True)
+    upstream, vec_out[4:5, :], vec_out[5:6, :] = unwhiten(pull * vec[10], vec[8], white, rate)
+    dense_low = (upstream * slope).astype(low)
+    turned = gate_ref[...].astype(f32).T.astype(low)
+    for group in range(groups):
+        joint_out[group, :, :width] = dot_plain(
+            turned, dense_low[:, group * width : (group + 1) * width]
+        ).astype(low)
+    upstream, vec_out[2:3, :], vec_out[3:4, :] = unwhiten(
+        dot_rows(dense_low, readout_ref[...]), vec[6], out_white_ref[...], out_rate
+    )
+    sum_out[...] = upstream
+    gate_ref[...] = upstream.astype(low)
+    upstream_turned = upstream.T.astype(low)
+    mid_turned = mid_ref[...].astype(f32).T.astype(low)
+
+    def backward(group, carry):
+        contract_out[group] = dot_plain(upstream_turned, acts_ref[group]).astype(low)
+        acts_ref[group] = (
+            dot_plain(gate_ref[...], weights_ref[group, :, hidden : 2 * hidden]) * slope_ref[group]
+        ).astype(low)
+        expand_out[group] = dot_plain(mid_turned, acts_ref[group]).astype(low)
+        sum_out[...] += dot_rows(acts_ref[group], weights_ref[group, :, :hidden])
+        return carry
+
+    lax.fori_loop(0, groups, backward, 0)
+    upstream, vec_out[0:1, :], vec_out[1:2, :] = unwhiten(
+        sum_out[...], vec[4], mid_white_ref[...], mid_rate
+    )
+    vec_out[7:8, :] = jnp.zeros((1, model), f32)
+    sum_out[...] = upstream
+    gate_ref[...] = upstream.astype(low)
+    turned = upstream.T.astype(low)
+    for group in range(groups):
+        mixed_out[group] = dot_plain(gate_ref[...], combine_ref[group, :, :width]).astype(low)
+        joint_out[group, :, width:] = dot_plain(turned, mixed_ref[group]).astype(low)
+
+
+def middle(first_weights, weights, vec, white, mixed, marks):
+    groups, model = weights.shape[:2]
+    seq, width = mixed.shape[1:]
+    hidden = (weights.shape[2] - width) // 2
+    wide = pltpu.VMEM((seq, model), f32)
+    outputs = [
+        ((groups, model, hidden), low),
+        ((groups, model, hidden), low),
+        ((groups, model, 2 * width), low),
+        ((groups, seq, width), low),
+        ((seq, model), f32),
+        ((8, model), f32),
+        ((seq, 1), f32),
+    ]
+    return pl.pallas_call(
+        middle_kernel,
+        grid=(1,),
+        in_specs=[
+            pl.BlockSpec(
+                (groups, model, 2 * BLOCK), lambda step: (0, 0, 3), pipeline_mode=pl.Buffered(1)
+            )
+        ]
+        + [
+            pl.BlockSpec(
+                array.shape,
+                functools.partial(lambda rank, step: (0,) * rank, array.ndim),
+                pipeline_mode=pl.Buffered(1),
+            )
+            for array in (weights, vec, white, mixed, marks)
+        ],
+        out_specs=[
+            pl.BlockSpec(
+                shape,
+                functools.partial(lambda rank, step: (0,) * rank, len(shape)),
+                pipeline_mode=pl.Buffered(1),
+            )
+            for shape, _ in outputs
+        ],
+        out_shape=[jax.ShapeDtypeStruct(*output) for output in outputs],
+        scratch_shapes=[
+            pltpu.VMEM((model, model), low),
+            pltpu.VMEM((groups, seq, hidden), f32),
+            pltpu.VMEM((groups, seq, hidden), low),
+            pltpu.VMEM((seq, model), low),
+            wide,
+            wide,
+            pltpu.VMEM((seq, model), low),
+        ],
+        compiler_params=pltpu.CompilerParams(vmem_limit_bytes=60 << 20),
+        name="middle",
+    )(first_weights, weights, vec, white, mixed, marks)
+
+
+def project_back_kernel(
+    weights_ref,
+    vec_ref,
+    white_ref,
+    rate_ref,
+    rel_white_ref,
+    rel_rate_ref,
+    sum_ref,
+    grads_ref,
+    tables_ref,
+    vec_grads_ref,
+    words_out,
+    project_out,
+    total_ref,
+    fold_ref,
+):
+    groups, model = weights_ref.shape[:2]
+    seq = white_ref.shape[0]
+    width = grads_ref.shape[2] // 3
+    entries = rel_white_ref.shape[0]
+    part = entries // groups
+    vec = [vec_ref[row : row + 1] for row in range(4)]
+    turned = (white_ref[...] * vec[0] + vec[1]).T.astype(low)
+    rel_turned = (rel_white_ref[...] * vec[2] + vec[3]).T.astype(low)
+    chosen = selection(seq, entries)
+    total_ref[...] = sum_ref[...]
+    rel_total = jnp.zeros((entries, model), f32)
+    for group in range(groups):
+        fold_ref[...] = dot_left(chosen, tables_ref[group]).astype(low)
+        total_ref[...] += dot_rows(grads_ref[group], weights_ref[group, :, : 3 * width])
+        rel_total += dot_rows(fold_ref[...], weights_ref[group, :, : 2 * width])
+        project_out[group, :, : 2 * width] = (
+            dot_plain(turned, grads_ref[group, :, : 2 * width]) + dot_plain(rel_turned, fold_ref[...])
+        ).astype(low)
+        project_out[group, :, 2 * width : 3 * width] = dot_plain(
+            turned, grads_ref[group, :, 2 * width :]
+        ).astype(low)
+    upstream, gain_grad, bias_grad = unwhiten(total_ref[...], vec[0], white_ref[...], rate_ref[...])
+    words_out[...] = upstream.T.astype(low)
+    rel_up, rel_gain_grad, rel_bias_grad = unwhiten(
+        rel_total, vec[2], rel_white_ref[...], rel_rate_ref[...]
+    )
+    turned = rel_up.T.astype(low)
+    for group in range(groups):
+        project_out[group, :, 3 * width + BLOCK // 2 :] = turned[:, group * part : (group + 1) * part]
+    rows = [gain_grad, bias_grad, rel_gain_grad, rel_bias_grad]
+    rows += [vec_grads_ref[row : row + 1] for row in range(7)]
+    rows += [jnp.zeros((1, model), f32)]
+    for group in range(groups):
+        three = jnp.concatenate(rows[3 * group : 3 * group + 3] + [jnp.zeros((BLOCK - 3, model), f32)], 0)
+        project_out[group, :, 3 * width : 3 * width + BLOCK // 2] = three.T.astype(low)[:, : BLOCK // 2]
+
+
+def project_back(weights, vec, white, rate, rel_white, rel_rate, total, grads, tables, vec_grads):
+    groups, model = weights.shape[:2]
+    seq = white.shape[0]
+    width = grads.shape[2] // 3
+    entries = rel_white.shape[0]
+    return pl.pallas_call(
+        project_back_kernel,
+        in_specs=[IN_VMEM] * 10,
+        out_specs=[IN_VMEM] * 2,
+        out_shape=[
+            jax.ShapeDtypeStruct((model, seq), low),
+            jax.ShapeDtypeStruct((groups, model, 3 * width + BLOCK // 2 + entries // groups), low),
+        ],
+        scratch_shapes=[pltpu.VMEM((seq, model), f32), pltpu.VMEM((entries, 2 * width), low)],
+        compiler_params=pltpu.CompilerParams(vmem_limit_bytes=56 << 20),
+        name="project_back",
+    )(weights, vec, white, rate, rel_white, rel_rate, total, grads, tables, vec_grads)
 
 
 def split_terms(values, count):
@@ -880,18 +1174,24 @@
     vocab_slab = embedding.shape[1]
     span_part = relative.shape[0] // pieces
     vector_count = vectors.shape[0]
-    vector_part = pl.cdiv(vector_count, pieces)
     direct = owners == 8 and pieces == 4
 
     own_relative = lax.dynamic_slice_in_dim(relative, holder * span_part, span_part, 0).T
     own_readout = lax.dynamic_slice_in_dim(readout, holder * head_width, head_width, 1)
-    vector_terms = jnp.concatenate(split_terms(vectors.T, 3), 1)
+    vector_terms = [
+        jnp.pad(term, ((0, 0), (0, 16 - vector_count))) for term in split_terms(vectors.T, 3)
+    ]
+    high, rest = split_terms(own_relative, 2)
+    blank = jnp.zeros((width, 16), low)
     first_pack = jnp.concatenate(
         [
             project.reshape(width, 3 * head_width).astype(low),
+            *vector_terms,
+            blank,
+            high,
             combine.T.astype(low),
-            *split_terms(own_relative, 2),
-            jnp.pad(vector_terms, ((0, 0), (0, BLOCK - 3 * vector_count))),
+            jnp.pad(blank, ((0, 0), (0, 48))),
+            rest,
         ],
         1,
     )
@@ -913,119 +1213,50 @@
     inside = (local_ids >= 0) & (local_ids < vocab_slab)
     places = jnp.where(inside, local_ids, vocab_slab)
 
-    w_project = first_all[:, :, : 3 * head_width]
-    w_combine = first_all[:, :, 3 * head_width : 4 * head_width]
-    at = 4 * head_width
-    rel_terms = first_all[:, :, at : at + 2 * span_part].astype(f32)
-    rel_full = rel_terms[:, :, :span_part] + rel_terms[:, :, span_part:]
-    rel_full = rel_full.transpose(0, 2, 1).reshape(pieces * span_part, model)
-    at = at + 2 * span_part
-    vec_terms = first_all[0, :, at : at + 3 * vector_count].astype(f32)
-    vec_full = (
-        vec_terms[:, :vector_count]
-        + vec_terms[:, vector_count : 2 * vector_count]
-        + vec_terms[:, 2 * vector_count :]
-    ).T
-    w_expand = second_all[:, :, :hidden]
-    w_contract = second_all[:, :, hidden : 2 * hidden]
-    w_readout = second_all[:, :, 2 * hidden :]
-
-    found = lookup(all_lengths, places, embedding, row_count)
+    found = lookup(all_lengths, places, embedding)
+    found = found.reshape(owners, row_count, width, seq_len)
     if direct:
         found = exchange_words(found, 2)
     else:
-        found = lax.psum_scatter(found, "heads", scatter_dimension=0, tiled=True)[0]
+        found = lax.psum_scatter(found, "heads", scatter_dimension=1, tiled=True)[:, 0]
         found = lax.all_to_all(found, "dp", 0, 0, tiled=True)
-    word_rows = found.reshape(model, seq_len).T.astype(f32)
-
     own_length = lax.dynamic_slice_in_dim(row_lengths, holder, 1)
     own_live = jnp.arange(seq_len) < own_length
     own_flags = lax.dynamic_slice_in_dim(replaced, holder, 1)[0].astype(f32)
-
-    hidden_in, back_in = jax.vjp(norm_at(0), word_rows, vec_full)
-    hidden_low = hidden_in.astype(low)
-    qkv = product("td,hdc->htc", hidden_low, w_project).astype(low)
-    rel_norm, back_rel = jax.vjp(norm_at(2), rel_full, vec_full)
-    rel_low = rel_norm.astype(low)
-    entries = rel_full.shape[0]
-    reach = jnp.clip(seq_len + entries // 2 - jnp.arange(2 * seq_len), 0, entries - 1)
-    spread = (reach[:, None] == jnp.arange(entries)[None, :]).astype(low)
-    rel_rows = matmul(spread, rel_low).astype(low)
-    rel_table = product("ud,hdc->huc", rel_rows, w_project[:, :, : 2 * head_width]).astype(low)
+    marks = jnp.stack([jnp.where(own_live, 1.0 / token_total, 0.0), own_flags], 1)
+
+    entries = relative.shape[0]
+    vec_full, white, rate, qkv, rel_white, rel_rate, rel_table = prepare(
+        first_all, found.reshape(model, seq_len), head_width, entries
+    )
     probs, mixed = attend(own_length, qkv, rel_table)
-    attended = product("htc,hdc->td", mixed, w_combine)
-    hidden_mid, back_mid = jax.vjp(norm_at(4), hidden_in + attended, vec_full)
-    mid_low = hidden_mid.astype(low)
-    gate_in = product("td,hdf->htf", mid_low, w_expand)
-    gate_act, back_gate = jax.vjp(gelu, gate_in)
-    gate_low = gate_act.astype(low)
-    ffn_out = product("htf,hdf->td", gate_low, w_contract)
-    hidden_out, back_out = jax.vjp(norm_at(6), hidden_mid + ffn_out, vec_full)
-    out_low = hidden_out.astype(low)
-    w_readout = w_readout.transpose(1, 0, 2).reshape(model, model)
-    dense_out = matmul(out_low, w_readout)
-
-    def head_loss(dense_rows, gain_rows):
-        head_norm = normalize(gelu(dense_rows), gain_rows[8], gain_rows[9])
-        logits = jnp.sum(head_norm * gain_rows[10], -1)
-        losses = jax.nn.softplus(logits) - own_flags * logits
-        return jnp.sum(jnp.where(own_live, losses, 0.0))
-
-    loss_part, back_head = jax.vjp(head_loss, dense_out, vec_full)
-    grad_dense, grad_vec = back_head(1.0 / token_total)
-    dense_low = grad_dense.astype(low)
-    grad_readout = product(
-        "td,thc->hdc", out_low, dense_low.reshape(seq_len, pieces, head_width)
-    ).astype(low)
-    grad_sum, grad_gain = back_out(product("tc,dc->td", dense_low, w_readout))
-    grad_vec = grad_vec + grad_gain
-    ffn_low = grad_sum.astype(low)
-    grad_contract = product("td,htf->hdf", ffn_low, gate_low).astype(low)
-    gate_grad = back_gate(product("td,hdf->htf", ffn_low, w_contract))[0].astype(low)
-    grad_expand = product("td,htf->hdf", mid_low, gate_grad).astype(low)
-    grad_mid = grad_sum + product("htf,hdf->td", gate_grad, w_expand)
-    grad_sum, grad_gain = back_mid(grad_mid)
-    grad_vec = grad_vec + grad_gain
-    attend_low = grad_sum.astype(low)
-    grad_mixed = product("td,hdc->htc", attend_low, w_combine).astype(low)
-    grad_combine = product("td,htc->hdc", attend_low, mixed).astype(low)
-
+    grad_contract, grad_expand, grad_joint, grad_mixed, grad_sum, grad_vec, losses = middle(
+        first_all, second_all, vec_full, white, mixed, marks
+    )
+    loss_part = jnp.sum(losses)
     qkv_grads, rel_table_grads = attend_back(qkv, rel_table, probs, grad_mixed)
-    grad_hidden = grad_sum + product("htc,hdc->td", qkv_grads, w_project)
-    grad_words, grad_gain = back_in(grad_hidden)
-    grad_vec = grad_vec + grad_gain
-    sent = grad_words.astype(low).T.reshape(owners, width, seq_len)
+    sent, grad_project = project_back(
+        first_all,
+        vec_full,
+        white,
+        rate,
+        rel_white,
+        rel_rate,
+        grad_sum,
+        qkv_grads,
+        rel_table_grads,
+        grad_vec,
+    )
+    sent = sent.reshape(owners, width, seq_len)
     if direct:
         sent = return_words(sent, 3)
     else:
         sent = lax.all_to_all(sent, "dp", 0, 0, tiled=True)
         sent = lax.all_gather(sent, "heads", axis=0)
-
-    rel_grads = product("ur,huc->hrc", spread, rel_table_grads).astype(low)
-    grad_project = product("td,htc->hdc", hidden_low, qkv_grads)
-    grad_rel_part = product("rd,hrc->hdc", rel_low, rel_grads)
-    grad_project = jnp.concatenate(
-        [
-            grad_project[:, :, : 2 * head_width] + grad_rel_part,
-            grad_project[:, :, 2 * head_width :],
-        ],
-        2,
-    ).astype(low)
-    grad_rel_norm = product("hrc,hdc->rd", rel_grads, w_project[:, :, : 2 * head_width])
-    grad_relative, grad_gain = back_rel(grad_rel_norm)
-    grad_vec = grad_vec + grad_gain
-    grad_relative = grad_relative.reshape(pieces, span_part, model).transpose(0, 2, 1).astype(low)
-    grad_vec = jnp.pad(grad_vec, ((0, pieces * vector_part - vector_count), (0, 0)))
-    grad_vec = grad_vec.reshape(pieces, vector_part, model).transpose(0, 2, 1).astype(low)
-    grad_vec = jnp.pad(grad_vec, ((0, 0), (0, 0), (0, BLOCK - vector_part)))
-
-    partial_grads = [
-        grad_contract,
-        grad_expand,
-        jnp.concatenate([grad_readout, grad_combine], 2),
-        grad_project,
-        jnp.concatenate([grad_relative, grad_vec], 2),
-    ]
+        sent = sent.transpose(1, 0, 2, 3)
+    sent = sent.reshape(owners * row_count, width, seq_len)
+
+    partial_grads = [grad_contract, grad_expand, grad_joint, grad_project]
     if direct:
         sums = scatter_sums(
             [part.reshape(pieces, owners, width, -1) for part in partial_grads], 4
@@ -1040,7 +1271,7 @@
     grad_embedding, own_squares = deposit(all_lengths, places, sent, vocab_slab)
 
     squares_local = sum(jnp.sum(part * part) for part in sums) + jnp.sum(own_squares)
-    shared = jnp.concatenate([sums[2][:, :head_width], sums[4]], 1)
+    shared = jnp.concatenate([sums[2][:, :head_width], sums[3][:, 3 * head_width :]], 1)
     if direct:
         column = lax.broadcasted_iota(jnp.int32, (8, BLOCK), 1)
         own_facts = jnp.where(column == 0, squares_local, jnp.where(column == 1, loss_part, 0.0))
@@ -1055,11 +1286,11 @@
     grad_contract = sums[0].T
     grad_expand = sums[1]
     grad_combine = sums[2][:, head_width:].T
-    grad_project = sums[3].reshape(width, 3, head_width)
+    grad_project = sums[3][:, : 3 * head_width].reshape(width, 3, head_width)
     grad_readout = shared[:, :, :head_width].transpose(1, 0, 2).reshape(width, model)
-    at = head_width + span_part
-    grad_relative = shared[:, :, head_width:at].transpose(0, 2, 1).reshape(entries, width)
-    grad_vec = shared[:, :, at : at + vector_part].transpose(0, 2, 1).reshape(-1, width)
+    at = head_width + BLOCK // 2
+    grad_relative = shared[:, :, at:].transpose(0, 2, 1).reshape(entries, width)
+    grad_vec = shared[:, :, head_width : head_width + 3].transpose(0, 2, 1).reshape(-1, width)
     grad_vec = grad_vec[:vector_count]
     weights = (embedding, relative, project, combine, expand, contract, readout, vectors)
     gradients = (

time: 642 us -> 568 us (0.88)
  matrix products: 104 us -> 0 us
  Pallas kernels: 372 us -> 434 us
  local copies, waits for them, and re-layouts: 53.2 us -> 28.8 us
  other arithmetic: 61.7 us -> 41.7 us
  waiting for transfers between devices: 18.1 us -> 31.7 us
    dot_general x19 -> x0, matrix products: 104 us -> none  [the longest x18 98.2 us: product(): return jnp.einsum(form, matrix, operand, preferred_element_type=f32)]
    pallas_call x2 -> x5, Pallas kernels: 76.2 us -> 142 us  [the longest x1 38.2 us: middle(): pl.pallas_call(middle_kernel, grid=(1,), in_specs=[pl.BlockSpec((groups,...]
    all_gather x1, waiting for transfers between devices: 18 us -> 31.7 us  [per_device(): second_all = lax.all_gather(second_pack, everyone, axis=0, tiled=True)]
    reduce_sum x13 -> x1, other arithmetic: 9.2 us -> 0.67 us  [per_device(): loss_part = jnp.sum(losses)]
    convert_element_type x6 -> x0, other arithmetic: 8.47 us -> none  [the longest x1 4.08 us: per_device(): sent = grad_words.astype(low).T.reshape(owners, width, seq_len)]
    transpose x5 -> x2, local copies, waits for them, and re-layouts: 8.32 us -> 1.13 us  [per_device(): shared[:, :, head_width:head_width + 3].transpose(0, 2, 1)]
    concatenate x5 -> x2, other arithmetic: 7.5 us -> 0.78 us  [the longest x1 0.76 us: per_device(): jnp.concatenate([sums[2][:, :head_width], sums[3][:, 3 * head_width:]], 1)]
    unnamed x182 -> x69, local copies, waits for them, and re-layouts: 15.9 us -> 17.9 us
  transfers between devices with their start and end apart: 2 -> 2, of which waited for: 1 -> 1; matrix products, arithmetic and copies ran while one was open for 7% -> 2% of each run, Pallas kernels for 19% -> 23%
where the time goes in v3:
time: 568 us; the launch traced here: 558 us
  Pallas kernels  434 us (76%)
  other arithmetic  41.7 us (7%)
  waiting for transfers between devices  31.7 us (6%)
  local copies, waits for them, and re-layouts  28.8 us (5%)
  between operations  21.9 us (4%)
    pallas_call x1, Pallas kernels, scatter_sums(): pl.pallas_call(functools.partial(scatter_sums_kernel, count), in_specs=[A...  104 us
    pallas_call x1, Pallas kernels, attend_back(): pl.pallas_call(attend_back_kernel, grid=(groups,), in_specs=[pl.BlockSpec...  56.4 us
    pallas_call x1, Pallas kernels, middle(): pl.pallas_call(middle_kernel, grid=(1,), in_specs=[pl.BlockSpec((groups,...  38.2 us
    pallas_call x1, Pallas kernels, deposit(): pl.pallas_call(deposit_kernel, grid=(rows // count,), in_specs=[pl.BlockS...  35.8 us
    pallas_call x1, Pallas kernels, exchange_words(): pl.pallas_call(exchange_words_kernel, in_specs=[IN_VMEM], out_specs=IN_VM...  35.2 us
    pallas_call x1, Pallas kernels, attend(): pl.pallas_call(attend_kernel, grid=(groups,), in_specs=[pl.BlockSpec(memo...  34.9 us
    pallas_call x1, Pallas kernels, lookup(): pl.pallas_call(lookup_kernel, grid=(rows // count,), in_specs=[pl.BlockSp...  34 us
    all_gather x1, waiting for transfers between devices, per_device(): second_all = lax.all_gather(second_pack, everyone, axis=0, tiled=True)  31.7 us
  transfers between devices with their start and end apart: 2, of which 1 were waited for; matrix products, arithmetic and copies ran while one was open for 2% of the time, Pallas kernels for 23%

profile of v3, /device:TPU:0, one launch (start us, length us, event | category | flops | bytes accessed | tf_op | source)
XLA Modules:
  0.0 557.9 jit_solution(13341288046774880935)
XLA Ops:
  8.9 1.0 convert_element_type.61
  10.1 0.9 bitcast_dynamic-update-slice_fusion
  12.0 1.0 convert_element_type.70
  13.0 1.0 dynamic-slice_convert_fusion
  14.0 1.0 convert_bitcast_fusion
  15.8 1.0 copy.104
  16.8 1.1 copy.100
  18.5 12.4 %share_facts.1 = s32[8,8,512]{2,1,0:T(8,128)} custom-call(s32[8,512]{1,0:T(8,128)} %pad_add_fusion.facts_ref), custom_call_target="tpu_custom_call" | custom-call | tf_op jit(solution)/shard_map/share_facts/pallas_call | solution.py:417
  30.9 0.9 slice_subtract_fusion
  31.8 1.4 slice_reduce_fusion
  33.4 34.0 %lookup.1 = bf16[32,96,512]{2,1,0:T(8,128)(2,1)S(1)} custom-call(s32[32]{0:T(128)S(1)} %reshape_squeeze.3.lengths_ref, s32[4,8,512]{2,1,0:T(8,128)S(1)} %and_select_fusion.places_ref, f32[96,12672]{1,0:T(8,128)} %weights_ref.1), custom_call_target="tpu_custom_call" | custom-call | tf_op jit(solution)/shard_map/lookup/pallas_call | solution.py:721
  67.4 35.2 %exchange_words.1 = bf16[8,96,512]{2,1,0:T(8,128)(2,1)S(1)} custom-call(bf16[8,4,96,512]{3,2,1,0:T(8,128)(2,1)S(1)} %bitcast.68), custom_call_target="tpu_custom_call" | custom-call | tf_op jit(solution)/shard_map/exchange_words/pallas_call | solution.py:502
  102.6 0.9 copy-done.2
  108.8 14.3 %prepare.1 = (f32[16,768]{1,0:T(8,128)}, f32[512,768]{1,0:T(8,128)}, f32[512,1]{1,0:T(8,128)}, bf16[4,512,576]{2,1,0:T(8,128)(2,1)}, f32[512,768]{1,0:T(8,128)},...) custom-call(bf16[4,768,1152]{2,1,0:T(8,128)(2,1)} %bitcast.71, bf16[768,512]{1,0:T(8,128)(2,1)} %bitcast.69), custom_call_target="tpu_custom_call" | custom-call | tf_op jit(solution)/shard_map/prepare/pallas_call | solution.py:874
  123.1 1.7 copy-done.1
  124.8 34.9 %attend.1 = (bf16[12,512,512]{2,1,0:T(8,128)(2,1)}, bf16[4,512,192]{2,1,0:T(8,128)(2,1)S(1)}) custom-call(s32[1]{0:T(128)} %dynamic_slice.14.length_ref, bf16[4,512,576]{2,1,0:T(8,128)(2,1)S(1)} %copy-done.1, bf16[4,1024,384]{2,1,0:T(8,128)(2,1)} %get-tuple-element.59.table_ref), custom_call_target="tpu_custom_call" | custom-call | tf_op jit(solution)/shard_map/attend/pallas_call | solution.py:67
  159.8 1.0 copy-done.4
  160.8 31.7 %all-gather.5.cloned.1.call-done = bf16[3072,1728]{1,0:T(8,128)(2,1)} async-done(((bf16[96,1728]{1,0:T(8,128)(2,1)}), bf16[3072,1728]{1,0:T(8,128)(2,1)}) %all-gather.5.cloned.1.call-update) | async-done | bytes 10616848 | tf_op jit(solution)/shard_map/all_gather | solution.py:1203
  192.4 38.2 %middle.1 = (bf16[4,768,768]{2,1,0:T(8,128)(2,1)}, bf16[4,768,768]{2,1,0:T(8,128)(2,1)}, bf16[4,768,384]{2,1,0:T(8,128)(2,1)}, bf16[4,512,192]{2,1,0:T(8,128)(2,...) custom-call(bf16[4,768,1152]{2,1,0:T(8,128)(2,1)} %bitcast.72, bf16[4,768,1728]{2,1,0:T(8,128)(2,1)} %bitcast.76, ...), custom_call_target="tpu_custom_call" | custom-call | tf_op jit(solution)/shard_map/middle/pallas_call | solution.py:1005
  230.6 1.2 copy-done.5
  231.8 56.4 %attend_back.1 = (bf16[4,512,576]{2,1,0:T(8,128)(2,1)S(1)}, bf16[4,1024,384]{2,1,0:T(8,128)(2,1)}) custom-call(bf16[4,512,576]{2,1,0:T(8,128)(2,1)} %get-tuple-element.58.qkv_ref, bf16[4,1024,384]{2,1,0:T(8,128)(2,1)} %get-tuple-element.59.table_ref, bf16[12,512,512]{2,1,0:T(8,128)(2,1)} %get-tuple-element.68.probs_ref, bf16[4,512,192]{2,1,0:T(8,128)(2,1)S(1)} %copy-done.5), custom_call_target="tpu_custom_call" | custom-call | tf_op jit(solution)/shard_map/attend_back/pallas_call | solution.py:126
  288.3 1.5 copy-done.3
  289.7 19.9 %project_back.1 = (bf16[768,512]{1,0:T(8,128)(2,1)}, bf16[4,768,768]{2,1,0:T(8,128)(2,1)}) custom-call(bf16[4,768,1152]{2,1,0:T(8,128)(2,1)} %bitcast.73, f32[16,768]{1,0:T(8,128)} %get-tuple-element.56.vec_ref, f32[512,768]{1,0:T(8,128)} %get-tuple-element.57.white_ref, f32[512,1]{1,0:T(8,128)} %get-tuple-element.64.rate_ref, ...), custom_call_target="tpu_custom_call" | custom-call | tf_op jit(solution)/shard_map/project_back/pallas_call | solution.py:1102
  309.6 103.6 %scatter_sums.1 = (f32[96,768]{1,0:T(8,128)}, f32[96,768]{1,0:T(8,128)}, f32[96,384]{1,0:T(8,128)}, f32[96,768]{1,0:T(8,128)}) custom-call(bf16[4,4,2,96,768]{4,3,2,1,0:T(8,128)(2,1)} %bitcast.77, bf16[4,4,2,96,768]{4,3,2,1,0:T(8,128)(2,1)} %bitcast.78, bf16[4,4,2,96,384]{4,3,2,1,0:T(8,128)(2,1)} %bitcast.80, bf16[4,4,2,96,768]{4,3,2,1,0:T(8,128)(2,1)} %bitcast.79), custom_call_target="tpu_custom_call" | custom-call | tf_op jit(solution)/shard_map/scatter_sums/pallas_call | solution.py:359
  413.3 1.0 slice.42
  414.3 1.6 multiply_reduce_fusion.3
  415.8 1.0 slice.43
  416.8 26.5 %return_words.1 = bf16[8,4,96,512]{3,2,1,0:T(8,128)(2,1)S(1)} custom-call(bf16[8,96,512]{2,1,0:T(8,128)(2,1)S(1)} %bitcast.70), custom_call_target="tpu_custom_call" | custom-call | tf_op jit(solution)/shard_map/return_words/pallas_call | solution.py:581
  443.3 1.7 copy-done
  445.0 35.8 %deposit.1 = (f32[96,12672]{1,0:T(8,128)}, f32[96,128]{1,0:T(8,128)}) custom-call(s32[32]{0:T(128)} %copy-done.8, s32[4,8,512]{2,1,0:T(8,128)} %copy-done.7, bf16[32,96,512]{2,1,0:T(8,128)(2,1)} %bitcast.67), custom_call_target="tpu_custom_call" | custom-call | tf_op jit(solution)/shard_map/deposit/pallas_call | solution.py:790
  482.1 1.4 reduce_sum.68
  489.5 22.6 %finish_sums.1 = (f32[8,128]{1,0:T(8,128)}, f32[4,96,384]{2,1,0:T(8,128)}) custom-call(f32[8,128]{1,0:T(8,128)} %broadcast_select_fusion.facts_ref, f32[96,384]{1,0:T(8,128)} %pad_maximum_fusion.1.shared_ref), custom_call_target="tpu_custom_call" | custom-call | tf_op jit(solution)/shard_map/finish_sums/pallas_call | solution.py:646
  512.1 1.0 slice_bitcast_fusion
  513.2 1.3 fusion.29
  515.2 1.0 multiply_bitcast_fusion
  517.2 1.0 mul.458
  518.2 1.1 multiply_subtract_fusion.6
  521.5 0.9 copy.97
  522.4 2.0 multiply_subtract_fusion.4
  524.3 1.8 copy.107
  526.2 0.9 copy.108
  527.0 0.9 copy.109
  527.9 1.3 add_subtract_fusion
  529.3 2.2 multiply_subtract_fusion.2
  531.5 2.1 multiply_subtract_fusion.3
  533.6 2.1 multiply_subtract_fusion.5
  535.7 2.3 multiply_subtract_fusion.1
  538.0 10.3 %multiply_subtract_fusion = (f32[96,12672]{1,0:T(8,128)}, f32[96,12672]{1,0:T(8,128)}, f32[96,12672]{1,0:T(8,128)}) fusion(f32[96,12672]{1,0:T(8,128)S(1)} %bitcast.75, f32[96,12672]{1,0:T(8,128)} %get-tuple-element.82, f32[]{:T(128)S(6)} %min.3, f32[96,12672]{1,0:T(8,128)} %param.46, f32[96,12672]{1,0:T(8,128)} %param.38), kind=kLoop, calls=%fused_computation.2 | loop fusion | flops 19464192 | bytes 34062340 | tf_op jit(solution)/shard_map/sub | solution.py:1130
  (93 shorter events, 16.2 us)
Async XLA Ops:
  7.2 10.7 %copy-start.22 = (s32[4]{0:T(128)S(1)}, s32[4]{0:T(128)}, u32[]{:S(2)}) copy-start(s32[4]{0:T(128)} %param.28) | copy-start | bytes 52
  7.2 10.7 %copy-start.21 = (s32[4,512]{1,0:T(4,128)S(1)}, s32[4,512]{1,0:T(4,128)}, u32[]{:S(2)}) copy-start(s32[4,512]{1,0:T(4,128)} %param.27) | copy-start | bytes 24580
  7.2 101.6 %all-gather.3.cloned.1.call-start = ((), (), s32[]{:S(2)}) async-start(), calls=%async_computation | async-start | bytes 7299072 | tf_op jit(solution)/shard_map/all_gather | solution.py:1201
  12.0 180.5 %all-gather.5.cloned.1.call-start = ((), (), s32[]{:S(2)}) async-start(), calls=%async_computation.1 | async-start | bytes 11354112 | tf_op jit(solution)/shard_map/all_gather | solution.py:1203
  33.3 69.2 %copy-start.8 = (s32[32]{0:T(128)}, s32[32]{0:T(128)S(1)}, u32[]{:S(2)}) copy-start(s32[32]{0:T(128)S(1)} %reshape_squeeze.3.lengths_ref) | copy-start | bytes 388
  33.4 69.2 %copy-start.7 = (s32[4,8,512]{2,1,0:T(8,128)}, s32[4,8,512]{2,1,0:T(8,128)S(1)}, u32[]{:S(2)}) copy-start(s32[4,8,512]{2,1,0:T(8,128)S(1)} %and_select_fusion.places_ref) | copy-start | bytes 196612
  33.4 73.6 %copy-start.18 = (f32[192,96]{1,0:T(8,128)S(1)}, f32[192,96]{1,0:T(8,128)}, u32[]{:S(2)}) copy-start(f32[192,96]{1,0:T(8,128)} %param.41) | copy-start | bytes 221188
  33.4 74.3 %copy-start.19 = (f32[192,96]{1,0:T(8,128)S(1)}, f32[192,96]{1,0:T(8,128)}, u32[]{:S(2)}) copy-start(f32[192,96]{1,0:T(8,128)} %param.49) | copy-start | bytes 221188
  33.4 75.0 %copy-start.15 = (f32[96,3,192]{2,0,1:T(8,128)S(1)}, f32[96,3,192]{2,0,1:T(8,128)}, u32[]{:S(2)}) copy-start(f32[96,3,192]{2,0,1:T(8,128)} %param.40) | copy-start | bytes 663556
  33.4 75.2 %copy-start.16 = (f32[96,3,192]{2,0,1:T(8,128)S(1)}, f32[96,3,192]{2,0,1:T(8,128)}, u32[]{:S(2)}) copy-start(f32[96,3,192]{2,0,1:T(8,128)} %param.48) | copy-start | bytes 663556
  102.6 0.9 copy-start.2
  123.1 1.7 copy-start.1
  159.8 1.0 copy-start.4
  230.6 1.2 copy-start.5
  288.2 1.5 copy-start.3
  309.6 107.2 %copy-start.6 = (bf16[768,512]{1,0:T(8,128)(2,1)S(1)}, bf16[768,512]{1,0:T(8,128)(2,1)}, u32[]{:S(2)}) copy-start(bf16[768,512]{1,0:T(8,128)(2,1)} %get-tuple-element.78) | copy-start | bytes 2359300
  413.2 67.5 %copy-start.9 = (f32[96,768]{1,0:T(8,128)S(1)}, f32[96,768]{1,0:T(8,128)}, u32[]{:S(2)}) copy-start(f32[96,768]{1,0:T(8,128)} %get-tuple-element.77) | copy-start | bytes 884740
  413.2 67.5 %copy-start.12 = (f32[96,768]{1,0:T(8,128)S(1)}, f32[96,768]{1,0:T(8,128)}, u32[]{:S(2)}) copy-start(f32[96,768]{1,0:T(8,128)} %get-tuple-element.75) | copy-start | bytes 884740
  413.3 68.2 %copy-start.13 = (f32[96,768]{1,0:T(8,128)S(1)}, f32[96,768]{1,0:T(8,128)}, u32[]{:S(2)}) copy-start(f32[96,768]{1,0:T(8,128)} %get-tuple-element.74) | copy-start | bytes 884740
  413.3 70.3 %copy-start.17 = (f32[512,1]{1,0:T(8,128)S(1)}, f32[512,1]{1,0:T(8,128)}, u32[]{:S(2)}) copy-start(f32[512,1]{1,0:T(8,128)} %get-tuple-element.80) | copy-start | bytes 6148
  443.3 1.7 copy-start
  445.0 73.2 %copy-start.14 = (f32[96,384]{1,0:T(8,128)S(1)}, f32[96,384]{1,0:T(8,128)}, u32[]{:S(2)}) copy-start(f32[96,384]{1,0:T(8,128)} %get-tuple-element.76) | copy-start | bytes 442372
  483.5 44.4 %copy-start.20 = (f32[11,96]{1,0:T(8,128)S(1)}, f32[11,96]{1,0:T(8,128)}, u32[]{:S(2)}) copy-start(f32[11,96]{1,0:T(8,128)} %param.37) | copy-start | bytes 12676
  484.2 45.0 %copy-start.10 = (f32[768,96]{0,1:T(8,128)S(1)}, f32[768,96]{0,1:T(8,128)}, u32[]{:S(2)}) copy-start(f32[768,96]{0,1:T(8,128)} %param.35) | copy-start | bytes 884740
  516.3 15.2 %copy-start.11 = (f32[96,768]{1,0:T(8,128)S(1)}, f32[96,768]{1,0:T(8,128)}, u32[]{:S(2)}) copy-start(f32[96,768]{1,0:T(8,128)} %param.34) | copy-start | bytes 884740
  522.4 15.6 %slice-start = ((s8[4866048]{0:T(1024)(128)(4,1)}), s8[671744]{0:T(1024)(128)(4,1)S(1)}, s32[]{:S(2)}) async-start(s8[4866048]{0:T(1024)(128)(4,1)} %bitcast.74), calls=%async_computation.2 | async-start | bytes 1343488
  529.3 8.7 %slice-start.1 = ((s8[4866048]{0:T(1024)(128)(4,1)}), s8[4194304]{0:T(1024)(128)(4,1)S(1)}, s32[]{:S(2)}) async-start(s8[4866048]{0:T(1024)(128)(4,1)} %bitcast.74), calls=%async_computation.3 | async-start | bytes 8388608
Sparse Core Ops, SparseCore 0:
  12.1 90.1 all-gather.2
  105.9 86.4 all-gather.4

commit v4 on v3

v4 whole, which is shorter than its diff:
```python
import functools

import jax
import jax.numpy as jnp
from jax import lax
from jax.experimental import pallas as pl
from jax.experimental.pallas import tpu as pltpu
from jax.sharding import PartitionSpec as P

HEAD_DIM = 64
STEP = 10
BLOCK = 128
UNROLL = 16
ROW_SET = 8

low = jnp.bfloat16
f32 = jnp.float32

layer_eps = 1e-07
clip_level = 0.005
rate_steps = (0.1, 0.05, 0.05, 0.05, 0.05, 0.05, 0.05, 1.0)
beta_first = 0.9
beta_second = 0.999
adam_eps = 1e-08
weight_decay = 0.01


def dot_rows(a,b):
    return lax.dot_general(a,b,(((1,),(1,)),((),())),preferred_element_type=f32)
def dot_plain(a,b):
    return lax.dot_general(a,b,(((1,),(0,)),((),())),preferred_element_type=f32)
def dot_left(a,b):
    return lax.dot_general(a,b,(((0,),(0,)),((),())),preferred_element_type=f32)

def attend_head(group, head, length, qkv_ref, table_ref, probs_ref, mixed_ref, far_ref):
    seq = qkv_ref.shape[1]
    width = qkv_ref.shape[2] // 3
    heads = width // HEAD_DIM
    scale = (3 * HEAD_DIM) ** -0.5
    live = lax.broadcasted_iota(jnp.int32, (BLOCK, seq), 1) < length
    at = head * HEAD_DIM
    q = qkv_ref[group, :, at : at + HEAD_DIM]
    k = qkv_ref[group, :, width + at : width + at + HEAD_DIM]
    v = qkv_ref[group, :, 2 * width + at : 2 * width + at + HEAD_DIM]
    for block in range(seq // BLOCK):
        rows = slice(block * BLOCK, (block + 1) * BLOCK)
        window = slice(seq - BLOCK * (block + 1), 2 * seq - BLOCK * block)
        far = dot_rows(k[rows], table_ref[group, window, at : at + HEAD_DIM])
        far = pltpu.roll(far, seq, 1, stride=1, stride_axis=0)[:, :seq]
        far_ref[head, :, rows] = far.T
    for block in range(seq // BLOCK):
        rows = slice(block * BLOCK, (block + 1) * BLOCK)
        window = slice(seq - BLOCK * (block + 1), 2 * seq - BLOCK * block)
        near = dot_rows(q[rows], table_ref[group, window, width + at : width + at + HEAD_DIM])
        near = pltpu.roll(near, seq, 1, stride=1, stride_axis=0)[:, :seq]
        scores = (dot_rows(q[rows], k) + near + far_ref[head, rows, :]) * scale
        scores = jnp.where(live, scores, -1e9)
        top = jnp.max(scores, -1, keepdims=True)
        expo = jnp.exp(scores - top)
        probs = (expo * (1.0 / jnp.sum(expo, -1, keepdims=True))).astype(low)
        probs_ref[group * heads + head, rows, :] = probs
        mixed_ref[group, rows, at : at + HEAD_DIM] = dot_plain(probs, v).astype(low)


def attend_kernel(length_ref, qkv_ref, table_ref, probs_ref, mixed_ref, far_ref):
    for head in range(far_ref.shape[0]):
        attend_head(0, head, length_ref[0], qkv_ref, table_ref, probs_ref, mixed_ref, far_ref)


def attend(length, qkv, table):
    groups, seq, width3 = qkv.shape
    width = width3 // 3
    heads = width // HEAD_DIM
    return pl.pallas_call(
        attend_kernel,
        grid=(groups,),
        in_specs=[
            pl.BlockSpec(memory_space=pltpu.SMEM),
            pl.BlockSpec((1, seq, width3), lambda g: (g, 0, 0)),
            pl.BlockSpec((1, 2 * seq, 2 * width), lambda g: (g, 0, 0)),
        ],
        out_specs=[
            pl.BlockSpec((heads, seq, seq), lambda g: (g, 0, 0)),
            pl.BlockSpec((1, seq, width), lambda g: (g, 0, 0)),
        ],
        out_shape=[
            jax.ShapeDtypeStruct((groups * heads, seq, seq), low),
            jax.ShapeDtypeStruct((groups, seq, width), low),
        ],
        scratch_shapes=[pltpu.VMEM((heads, seq, seq), f32)],
        compiler_params=pltpu.CompilerParams(vmem_limit_bytes=48 << 20),
        name="attend",
    )(length, qkv, table)


def attend_back_head(
    group, head, qkv_ref, table_ref, probs_ref, up_ref, grad_ref, rel_ref, low_ref, sum_ref
):
    seq = qkv_ref.shape[1]
    width = qkv_ref.shape[2] // 3
    heads = width // HEAD_DIM
    scale = (3 * HEAD_DIM) ** -0.5
    row = lax.broadcasted_iota(jnp.int32, (BLOCK, BLOCK), 0)
    flip = row + lax.broadcasted_iota(jnp.int32, (BLOCK, BLOCK), 1) == BLOCK - 1
    flip = flip.astype(f32).astype(low)
    edge = jnp.zeros((BLOCK, BLOCK), f32)

    def shear(rows):
        return pltpu.roll(jnp.concatenate([rows, edge], 1), 1, 1, stride=1, stride_axis=0).astype(low)

    at = head * HEAD_DIM
    q = qkv_ref[group, :, at : at + HEAD_DIM]
    k = qkv_ref[group, :, width + at : width + at + HEAD_DIM]
    v = qkv_ref[group, :, 2 * width + at : 2 * width + at + HEAD_DIM]
    up = up_ref[group, :, at : at + HEAD_DIM]
    source = group * heads + head
    for block in range(seq // BLOCK):
        rows = slice(block * BLOCK, (block + 1) * BLOCK)
        probs = probs_ref[source, rows, :].astype(f32)
        pull = dot_rows(up[rows], v)
        inner = jnp.sum(probs * pull, -1, keepdims=True)
        low_ref[head, rows, :] = (probs * (pull - inner) * scale).astype(low)
    grad_v = dot_left(up, probs_ref[source]).T.astype(low)
    grad_ref[group, :, 2 * width + at : 2 * width + at + HEAD_DIM] = grad_v
    sum_ref[2 * head] = jnp.zeros(sum_ref.shape[1:], f32)
    sum_ref[2 * head + 1] = jnp.zeros(sum_ref.shape[1:], f32)
    for block in range(seq // BLOCK):
        rows = slice(block * BLOCK, (block + 1) * BLOCK)
        window = slice(seq - BLOCK * (block + 1), 2 * seq - BLOCK * block)
        turned = dot_plain(flip, low_ref[head, rows, :])
        near = shear(turned)
        grad_q = dot_plain(turned.astype(low), k) + dot_plain(
            near, table_ref[group, window, width + at : width + at + HEAD_DIM]
        )
        grad_ref[group, rows, at : at + HEAD_DIM] = dot_plain(flip, grad_q.astype(low)).astype(low)
        q_turned = dot_plain(flip, q[rows]).astype(low)
        sum_ref[2 * head + 1, :, window] += dot_left(q_turned, near)
        turned = dot_rows(flip, low_ref[head, :, rows])
        far = shear(turned)
        grad_k = dot_plain(turned.astype(low), q) + dot_plain(
            far, table_ref[group, window, at : at + HEAD_DIM]
        )
        grad_ref[group, rows, width + at : width + at + HEAD_DIM] = dot_plain(
            flip, grad_k.astype(low)
        ).astype(low)
        k_turned = dot_plain(flip, k[rows]).astype(low)
        sum_ref[2 * head, :, window] += dot_left(k_turned, far)
    rel_ref[group, :, at : at + HEAD_DIM] = sum_ref[2 * head].T.astype(low)
    rel_ref[group, :, width + at : width + at + HEAD_DIM] = sum_ref[2 * head + 1].T.astype(low)


def attend_back_kernel(*refs):
    for head in range(refs[-2].shape[0]):
        attend_back_head(0, head, *refs)


def attend_back(qkv, table, probs, up):
    groups, seq, width3 = qkv.shape
    width = width3 // 3
    heads = width // HEAD_DIM
    block = lambda *shape: pl.BlockSpec(shape, lambda g: (g, 0, 0))
    return pl.pallas_call(
        attend_back_kernel,
        grid=(groups,),
        in_specs=[
            block(1, seq, width3),
            block(1, 2 * seq, 2 * width),
            block(heads, seq, seq),
            block(1, seq, width),
        ],
        out_specs=[block(1, seq, width3), block(1, 2 * seq, 2 * width)],
        out_shape=[
            jax.ShapeDtypeStruct((groups, seq, width3), low),
            jax.ShapeDtypeStruct((groups, 2 * seq, 2 * width), low),
        ],
        scratch_shapes=[
            pltpu.VMEM((heads, seq, seq), low),
            pltpu.VMEM((2 * heads, HEAD_DIM, 2 * seq), f32),
        ],
        compiler_params=pltpu.CompilerParams(vmem_limit_bytes=48 << 20),
        name="attend_back",
    )(qkv, table, probs, up)


MESH = pl.DeviceIdType.MESH
ANYWHERE = pl.BlockSpec(memory_space=pl.ANY)
IN_VMEM = pl.BlockSpec(memory_space=pltpu.VMEM)


def place():
    owner, holder = lax.axis_index("dp"), lax.axis_index("heads")
    return owner // 2, owner % 2, holder // 2, holder % 2


def device(z, x, y, c):
    return (z * 2 + x, y * 2 + c)


def signal(target):
    pl.semaphore_signal(
        pltpu.get_barrier_semaphore(), inc=1, device_id=target, device_id_type=MESH
    )


def greet(z, x, y, c, line):
    signal(device(z, x, y, 1 - c))
    signal(device(z, x, 1 - y, c))
    if line:
        signal(device(z, 1 - x, y, c))

        @pl.when(z < 3)
        def above():
            signal(device(z + 1, x, y, c))

        @pl.when(z > 0)
        def below():
            signal(device(z - 1, x, y, c))

        pl.semaphore_wait(pltpu.get_barrier_semaphore(), jnp.where((z == 0) | (z == 3), 4, 5))


def remote(source, target, send, recv, to):
    return pltpu.make_async_remote_copy(
        src_ref=source, dst_ref=target, send_sem=send, recv_sem=recv, device_id=to, device_id_type=MESH
    )


def sum_scratch(width, sizes):
    half = width // 2
    leads = (
        (2, 4, 2, width),
        (2, 4, 2, width),
        (4, 2, half),
        (2, 4, half),
        (4, half),
        (4, half),
        (3, width),
        (3, width),
    )
    shapes = [pltpu.VMEM(lead + (size,), low) for lead in leads for size in sizes]
    count = len(sizes)
    return shapes + [
        pltpu.SemaphoreType.DMA((count, 2)),
        pltpu.SemaphoreType.DMA((count, 12)),
        pltpu.SemaphoreType.DMA((count, 12)),
    ]


def sum_stages(spot, grads, totals, chunks, refs):
    count = len(chunks)
    pair, own, first_a, first_b, second_a, second_b, rise, fall = [
        refs[count * part : count * (part + 1)] for part in range(8)
    ]
    local_sem, send_sem, recv_sem = refs[8 * count :]
    z, x, y, c = spot
    half = grads[0].shape[3] // 2
    upper, lower = pl.ds(0, half), pl.ds(half, half)
    core_to, y_to, x_to = device(z, x, y, 1 - c), device(z, x, 1 - y, c), device(z, 1 - x, y, c)
    up_to, down_to = device(z + 1, x, y, c), device(z - 1, x, y, c)

    def columns(part):
        return pl.ds(chunks[part][1], chunks[part][2])

    def source(part, row):
        return grads[chunks[part][0]].at[row, :, :, :, columns(part)]

    def link(part, slot, source, target, to):
        return remote(source, target, send_sem.at[part, slot], recv_sem.at[part, slot], to)

    def local(part, side):
        return pltpu.make_async_copy(
            source(part, side * 2 + c), own[part].at[side], local_sem.at[part, side]
        )

    def pair_copy(part, side):
        return link(part, side, source(part, side * 2 + 1 - c), pair[part].at[side], core_to)

    def first_copies(part):
        block = own[part]
        return (
            link(part, 2, block.at[1 - y, :, :, upper], first_a[part], y_to),
            link(part, 3, block.at[:, :, 1 - x, lower], first_b[part], x_to),
        )

    def second_copies(part):
        block = own[part]
        return (
            link(part, 4, block.at[y, :, 1 - x, upper], second_a[part], x_to),
            link(part, 5, block.at[1 - y, :, x, lower], second_b[part], y_to),
        )

    def rise_copy(part, turn):
        block = own[part].at[y, lax.clamp(0, 3 + z - turn, 3), x]
        return link(part, 6 + turn, block, rise[part].at[turn], up_to)

    def fall_copy(part, turn):
        block = own[part].at[y, lax.clamp(0, turn - 3 + z, 3), x]
        return link(part, 9 + turn, block, fall[part].at[turn], down_to)

    def add(target, source):
        target[...] = (target[...].astype(f32) + source[...].astype(f32)).astype(low)

    def start_pair(part):
        for side in range(2):
            pair_copy(part, side).start()
            local(part, side).start()

    def start():
        for part in range(min(2, count)):
            start_pair(part)

    def stage_pair(part):
        for side in range(2):
            local(part, side).wait()
            pair_copy(part, side).wait()
        if part + 2 < count:
            start_pair(part + 2)

        def step(index, carry):
            side, rest = index // 8, index % 8
            add(own[part].at[side, rest // 2, rest % 2], pair[part].at[side, rest // 2, rest % 2])
            return carry

        lax.fori_loop(0, 16, step, 0)
        for copy in first_copies(part):
            copy.start()

    def stage_first(part):
        for copy in first_copies(part):
            copy.wait()

        def step(index, carry):
            add(own[part].at[y, index // 2, index % 2, upper], first_a[part].at[index // 2, index % 2])
            add(own[part].at[index % 2, index // 2, x, lower], first_b[part].at[index % 2, index // 2])
            return carry

        lax.fori_loop(0, 8, step, 0)
        for copy in second_copies(part):
            copy.start()

    def stage_second(part):
        for copy in second_copies(part):
            copy.wait()

        def step(index, carry):
            add(own[part].at[y, index, x, upper], second_a[part].at[index])
            add(own[part].at[y, index, x, lower], second_b[part].at[index])
            return carry

        lax.fori_loop(0, 4, step, 0)

    def stage_line(part, turn):
        @pl.when((z <= turn) & (z < 3))
        def rises():
            if turn > 0:

                @pl.when(z > 0)
                def joined():
                    rise_copy(part, turn - 1).wait_recv()
                    add(own[part].at[y, 3 + z - turn, x], rise[part].at[turn - 1])

            rise_copy(part, turn).start()

        @pl.when((3 - z <= turn) & (z > 0))
        def falls():
            if turn > 0:

                @pl.when(z < 3)
                def joined():
                    fall_copy(part, turn - 1).wait_recv()
                    add(own[part].at[y, turn - 3 + z, x], fall[part].at[turn - 1])

            fall_copy(part, turn).start()

    def stage_total(part):
        total = totals[chunks[part][0]].at[:, columns(part)]
        total[...] = own[part][y, z, x].astype(f32)

        @pl.when(z > 0)
        def risen():
            rise_copy(part, 2).wait_recv()
            total[...] += rise[part][2].astype(f32)

        @pl.when(z < 3)
        def fallen():
            fall_copy(part, 2).wait_recv()
            total[...] += fall[part][2].astype(f32)

        for turn in range(3):

            @pl.when((z <= turn) & (z < 3))
            def risen_out():
                rise_copy(part, turn).wait_send()

            @pl.when((3 - z <= turn) & (z > 0))
            def fallen_out():
                fall_copy(part, turn).wait_send()

    return start, {
        "pair": stage_pair,
        "first": stage_first,
        "second": stage_second,
        "line0": functools.partial(stage_line, turn=0),
        "line1": functools.partial(stage_line, turn=1),
        "line2": functools.partial(stage_line, turn=2),
        "total": stage_total,
    }


def chunked(sizes, most=3 * BLOCK):
    return [
        (array, first, min(most, size - first))
        for array, size in enumerate(sizes)
        for first in range(0, size, most)
    ]


BACK_START = (("pair", 0),)
BACK_SLOTS = {
    0: (("pair", 1),),
    2: (("first", 0), ("pair", 2)),
    3: (("first", 1),),
    4: (("pair", 3), ("second", 0), ("line0", 0)),
    5: (("first", 2), ("second", 1), ("line0", 1), ("line1", 0)),
    6: (("line1", 1), ("line2", 0)),
    7: (("first", 3), ("second", 2), ("line0", 2), ("line2", 1), ("total", 0)),
    8: (("line1", 2), ("total", 1)),
    9: (("second", 3), ("line0", 3), ("line2", 2)),
    10: (("line1", 3), ("total", 2)),
    11: (("line2", 3),),
}
BACK_END = (("total", 3),)


def run_all(stages, steps):
    for name, chunk in steps:
        stages[name](chunk)


def attend_back_sums_kernel(count, chunks, *refs):
    inputs, grads = refs[:4], refs[4 : 4 + count]
    outputs, totals = refs[4 + count : 6 + count], refs[6 + count : 6 + 2 * count]
    work, rest = refs[6 + 2 * count : 8 + 2 * count], refs[8 + 2 * count :]
    groups, heads = inputs[0].shape[0], work[0].shape[0]
    spot = place()
    greet(*spot, True)
    start, stages = sum_stages(spot, grads, totals, chunks, rest)
    start()
    run_all(stages, BACK_START)

    def step(group, carry):
        for head in range(heads):
            attend_back_head(group, head, *inputs, *outputs, *work)
            for slot, steps in BACK_SLOTS.items():
                if slot % heads == head:
                    pl.when(group == slot // heads)(functools.partial(run_all, stages, steps))
        return carry

    lax.fori_loop(0, groups, step, 0)
    run_all(stages, BACK_END)


def attend_back_sums(qkv, table, probs, up, grads, tag):
    groups, seq, width3 = qkv.shape
    width = width3 // 3
    heads = width // HEAD_DIM
    part = grads[0].shape[1] // 8
    sizes = [grad.shape[2] for grad in grads]
    chunks = chunked(sizes)
    return pl.pallas_call(
        functools.partial(attend_back_sums_kernel, len(grads), chunks),
        in_specs=[IN_VMEM] * 4 + [ANYWHERE] * len(grads),
        out_specs=[IN_VMEM] * (2 + len(grads)),
        out_shape=[
            jax.ShapeDtypeStruct((groups, seq, width3), low),
            jax.ShapeDtypeStruct((groups, 2 * seq, 2 * width), low),
        ]
        + [jax.ShapeDtypeStruct((part, size), f32) for size in sizes],
        scratch_shapes=[
            pltpu.VMEM((heads, seq, seq), low),
            pltpu.VMEM((2 * heads, HEAD_DIM, 2 * seq), f32),
        ]
        + sum_scratch(part, [chunk[2] for chunk in chunks]),
        compiler_params=pltpu.CompilerParams(
            collective_id=tag, has_side_effects=True, vmem_limit_bytes=60 << 20
        ),
        name="attend_back_sums",
    )(qkv, table, probs, up, *[grad.reshape(4, 4, 2, part, -1) for grad in grads])


def peers(z, x):
    return [((z + 2 - far) % 4, x if same else 1 - x) for far, same in PEER_ORDER]


PEER_ORDER = ((0, False), (0, True), (1, False), (1, True), (3, False), (3, True), (2, False))


def meet_owners(z, x, y, c):
    for peer_z, peer_x in peers(z, x):
        signal(device(peer_z, peer_x, y, c))


def share_facts_kernel(facts_ref, all_ref, local_sem, send_sem, recv_sem):
    z, x, y, c = place()
    meet_owners(z, x, y, c)
    pl.semaphore_wait(pltpu.get_barrier_semaphore(), 7)
    here = z * 2 + x
    keep = pltpu.make_async_copy(facts_ref, all_ref.at[here], local_sem)
    keep.start()
    copies = []
    for index, (peer_z, peer_x) in enumerate(peers(z, x)):
        copy = remote(
            facts_ref,
            all_ref.at[here],
            send_sem.at[index],
            recv_sem.at[here],
            device(peer_z, peer_x, y, c),
        )
        copy.start()
        copies.append(copy)
    for index, (peer_z, peer_x) in enumerate(peers(z, x)):
        there = peer_z * 2 + peer_x
        copies[index].wait_send()
        remote(
            facts_ref, all_ref.at[there], send_sem.at[index], recv_sem.at[there], device(z, x, y, c)
        ).wait_recv()
    keep.wait()


def share_facts(facts, tag):
    return pl.pallas_call(
        share_facts_kernel,
        in_specs=[IN_VMEM],
        out_specs=IN_VMEM,
        out_shape=jax.ShapeDtypeStruct((8,) + facts.shape, facts.dtype),
        scratch_shapes=[
            pltpu.SemaphoreType.DMA,
            pltpu.SemaphoreType.DMA((7,)),
            pltpu.SemaphoreType.DMA((8,)),
        ],
        compiler_params=pltpu.CompilerParams(collective_id=tag, has_side_effects=True),
        name="share_facts",
    )(facts)


def word_stages(spot, found_ref, words_ref, pair, side, send_sem, recv_sem, out_sem, in_sem):
    z, x, y, c = spot
    here = z * 2 + x
    targets = peers(z, x) + [(z, x)]
    core_to, y_to = device(z, x, y, 1 - c), device(z, x, 1 - y, c)

    def at_home(part):
        return targets[part][0] * 2 + targets[part][1]

    def pair_copy(part, row):
        to = at_home(part)
        return remote(
            found_ref.at[to, row * 2 + 1 - c],
            pair.at[row, to],
            send_sem.at[part, row],
            recv_sem.at[part, row],
            core_to,
        )

    def side_copy(part):
        to = at_home(part)
        return remote(
            pair.at[1 - y, to], side.at[to], send_sem.at[part, 2], recv_sem.at[part, 2], y_to
        )

    def out_copy(part):
        return remote(
            pair.at[y, at_home(part)],
            words_ref.at[here],
            out_sem.at[part],
            in_sem.at[here],
            device(targets[part][0], targets[part][1], y, c),
        )

    def start():
        for part in range(8):
            for row in range(2):
                pair_copy(part, row).start()

    def sideways(first, last):
        for part in range(first, last):
            to = at_home(part)
            for row in range(2):
                pair_copy(part, row).wait_recv()
                pair[row, to] = pair[row, to] + found_ref[to, row * 2 + c]
            side_copy(part).start()

    def outward(first, last):
        for part in range(first, last):
            to = at_home(part)
            side_copy(part).wait_recv()
            pair[y, to] = pair[y, to] + side[to]
            if part < 7:
                out_copy(part).start()
            else:
                words_ref[here] = pair[y, to]

    def finish():
        for part in range(8):
            for row in range(2):
                pair_copy(part, row).wait_send()
            side_copy(part).wait_send()
            if part < 7:
                out_copy(part).wait_send()
                there = at_home(part)
                remote(
                    pair.at[y, there], words_ref.at[there], out_sem.at[part], in_sem.at[there], core_to
                ).wait_recv()

    return start, sideways, outward, finish


def exchange_words_kernel(found_ref, words_ref, *refs):
    spot = place()
    meet_owners(*spot)
    greet(*spot, False)
    pl.semaphore_wait(pltpu.get_barrier_semaphore(), 9)
    start, sideways, outward, finish = word_stages(spot, found_ref, words_ref, *refs)
    start()
    sideways(0, 8)
    outward(0, 8)
    finish()


def exchange_words(found, tag):
    piece = found.shape[2:]
    return pl.pallas_call(
        exchange_words_kernel,
        in_specs=[IN_VMEM],
        out_specs=IN_VMEM,
        out_shape=jax.ShapeDtypeStruct((8,) + piece, low),
        scratch_shapes=[
            pltpu.VMEM((2, 8) + piece, low),
            pltpu.VMEM((8,) + piece, low),
            pltpu.SemaphoreType.DMA((8, 3)),
            pltpu.SemaphoreType.DMA((8, 3)),
            pltpu.SemaphoreType.DMA((8,)),
            pltpu.SemaphoreType.DMA((8,)),
        ],
        compiler_params=pltpu.CompilerParams(
            collective_id=tag, has_side_effects=True, vmem_limit_bytes=40 << 20
        ),
        name="exchange_words",
    )(found)


def return_stages(spot, grads_ref, sent_ref, refs):
    local_sem, out_sem, in_sem, send_sem, recv_sem = refs
    z, x, y, c = spot
    here = z * 2 + x
    own = y * 2 + c
    other = (1 - y) * 2 + c
    core_to, y_to = device(z, x, y, 1 - c), device(z, x, 1 - y, c)
    order = [(z, x)] + peers(z, x)[::-1]
    keep = pltpu.make_async_copy(grads_ref.at[here], sent_ref.at[here, own], local_sem)

    def out_copy(part, peer):
        return remote(
            grads_ref.at[peer[0] * 2 + peer[1]],
            sent_ref.at[here, own],
            out_sem.at[part],
            in_sem.at[here],
            device(peer[0], peer[1], y, c),
        )

    def in_copy(part, peer):
        there = peer[0] * 2 + peer[1]
        return remote(
            grads_ref.at[there], sent_ref.at[there, own], out_sem.at[part], in_sem.at[there], core_to
        )

    def pass_on(slot, row, there, to):
        block = sent_ref.at[there, row]
        return remote(block, block, send_sem.at[slot, there], recv_sem.at[row, there], to)

    def start():
        keep.start()
        for part, peer in enumerate(peers(z, x)):
            out_copy(part, peer).start()

    def forward(first, last):
        for part in range(first, last):
            there = order[part][0] * 2 + order[part][1]
            if part == 0:
                keep.wait()
            else:
                in_copy(part - 1, order[part]).wait_recv()
            pass_on(0, own, there, y_to).start()
            pass_on(1, own, there, core_to).start()

    def relay(first, last):
        for part in range(first, last):
            there = order[part][0] * 2 + order[part][1]
            pass_on(0, other, there, y_to).wait_recv()
            pass_on(2, other, there, core_to).start()

    def finish():
        for part, peer in enumerate(peers(z, x)):
            out_copy(part, peer).wait_send()
        for peer_z, peer_x in order:
            there = peer_z * 2 + peer_x
            pass_on(0, own, there, y_to).wait_send()
            pass_on(1, own, there, core_to).wait_send()
            pass_on(2, other, there, core_to).wait_send()
            pass_on(1, y * 2 + 1 - c, there, core_to).wait_recv()
            pass_on(2, (1 - y) * 2 + 1 - c, there, core_to).wait_recv()

    return start, forward, relay, finish


def return_sums_kernel(chunks, words_ref, grads_ref, sent_ref, total_ref, *refs):
    spot = place()
    z, x, y, c = spot
    meet_owners(*spot)
    greet(*spot, False)
    pl.semaphore_wait(pltpu.get_barrier_semaphore(), 9)
    start_words, forward, relay, finish = return_stages(spot, words_ref, sent_ref, refs[:5])
    start_sums, stages = sum_stages(spot, [grads_ref], [total_ref], chunks, refs[5:])
    start_words()
    start_sums()
    forward(0, 1)
    run_all(stages, (("pair", 0), ("pair", 1)))
    forward(1, 8)
    run_all(stages, (("first", 0),))
    relay(0, 4)
    run_all(stages, (("first", 1), ("second", 0), ("line0", 0)))
    relay(4, 8)
    run_all(stages, (("second", 1), ("line0", 1)))
    for turn in ("line1", "line2", "total"):
        run_all(stages, ((turn, 0), (turn, 1)))
    finish()


def return_sums(words, grads, tag):
    piece = words.shape[1:]
    size = grads.shape[2]
    part = grads.shape[1] // 8
    chunks = chunked([size])
    return pl.pallas_call(
        functools.partial(return_sums_kernel, chunks),
        in_specs=[IN_VMEM, ANYWHERE],
        out_specs=[IN_VMEM] * 2,
        out_shape=[
            jax.ShapeDtypeStruct((8, 4) + piece, low),
            jax.ShapeDtypeStruct((part, size), f32),
        ],
        scratch_shapes=[
            pltpu.SemaphoreType.DMA,
            pltpu.SemaphoreType.DMA((7,)),
            pltpu.SemaphoreType.DMA((8,)),
            pltpu.SemaphoreType.DMA((3, 8)),
            pltpu.SemaphoreType.DMA((4, 8)),
        ]
        + sum_scratch(part, [chunk[2] for chunk in chunks]),
        compiler_params=pltpu.CompilerParams(
            collective_id=tag, has_side_effects=True, vmem_limit_bytes=48 << 20
        ),
        name="return_sums",
    )(words, grads.reshape(4, 4, 2, part, size))


def gather_stages(spot, pack_ref, all_ref, local_sem, send_sem, recv_sem):
    z, x, y, c = spot
    half = pack_ref.shape[0] // 2
    core_to, y_to, x_to = device(z, x, y, 1 - c), device(z, x, 1 - y, c), device(z, 1 - x, y, c)
    up_to, down_to = device(z + 1, x, y, c), device(z - 1, x, y, c)
    keep = pltpu.make_async_copy(pack_ref, all_ref.at[y * 2 + c, z * 2 + x], local_sem)
    UP, DOWN, CROSS, SIDE, CORE = range(5)
    targets = (up_to, down_to, x_to, y_to, core_to)

    def copy(kind, part, zz, xx, yy, column=c):
        zz = lax.clamp(0, zz, 3)
        block = all_ref.at[yy * 2 + column, zz * 2 + xx, pl.ds(part * half, half)]
        return remote(
            block,
            block,
            send_sem.at[kind, part, yy, zz * 2 + xx],
            recv_sem.at[column, part, yy, zz * 2 + xx],
            targets[kind],
        )

    def distances(far):
        if far == 0:
            return [(z, z >= 0, None)]
        return [(z - far, z >= far, UP), (z + far, z <= 3 - far, DOWN)]

    def spread_block(zz):
        for part in range(2):
            copy(CROSS if part == 0 else SIDE, part, zz, x, y).start()
        for part in range(2):
            copy(SIDE if part == 0 else CROSS, part, zz, x, y).start()
            copy(CORE, part, zz, x, y).start()

    def along(zz, way):
        if way is None:
            return [(UP, z < 3), (DOWN, z > 0)]
        return [(way, z < 3 if way == UP else z > 0)]

    def line(far):
        for zz, exists, way in distances(far):

            @pl.when(exists)
            def arrived():
                if way is None:
                    keep.wait()
                else:
                    for part in range(2):
                        copy(way, part, zz, x, y).wait_recv()
                for on, possible in along(zz, way):

                    @pl.when(possible)
                    def onward():
                        for part in range(2):
                            copy(on, part, zz, x, y).start()

                spread_block(zz)

    def sides(far):
        for zz, exists, way in distances(far):

            @pl.when(exists)
            def arrived():
                copy(CROSS, 0, zz, 1 - x, y).wait_recv()
                copy(SIDE, 0, zz, 1 - x, y).start()
                copy(CORE, 0, zz, 1 - x, y).start()
                copy(SIDE, 1, zz, x, 1 - y).wait_recv()
                copy(CROSS, 1, zz, x, 1 - y).start()
                copy(CORE, 1, zz, x, 1 - y).start()

    def corners(far):
        for zz, exists, way in distances(far):

            @pl.when(exists)
            def arrived():
                for part, xx, yy in ((0, x, 1 - y), (1, 1 - x, y), (0, 1 - x, 1 - y), (1, 1 - x, 1 - y)):
                    copy(CORE, part, zz, xx, yy).wait_recv()
                    copy(CORE, part, zz, xx, yy).start()

    def finish():
        for far in range(4):
            for zz, exists, way in distances(far):

                @pl.when(exists)
                def drained():
                    for on, possible in along(zz, way):

                        @pl.when(possible)
                        def onward():
                            for part in range(2):
                                copy(on, part, zz, x, y).wait_send()

                    for part in range(2):
                        copy(CROSS, part, zz, x, y).wait_send()
                        copy(SIDE, part, zz, x, y).wait_send()
                        for xx in range(2):
                            for yy in range(2):
                                copy(CORE, part, zz, xx, yy).wait_send()
                                copy(CORE, part, zz, xx, yy, 1 - c).wait_recv()
                    copy(SIDE, 0, zz, 1 - x, y).wait_send()
                    copy(CROSS, 1, zz, x, 1 - y).wait_send()

    return keep.start, {"line": line, "sides": sides, "corners": corners, "finish": lambda far: finish()}


def gather_scratch():
    return [
        pltpu.SemaphoreType.DMA,
        pltpu.SemaphoreType.DMA((5, 2, 2, 8)),
        pltpu.SemaphoreType.DMA((2, 2, 2, 8)),
    ]


def finish_sums_kernel(
    width,
    losses_ref,
    squares_ref,
    *refs,
):
    sums, refs = refs[:4], refs[4:]
    total_ref, all_ref, facts, pair, side, cross, line, local_sem, send_sem, recv_sem, line_send, line_recv = refs
    z, x, y, c = place()
    core_to, y_to, x_to = device(z, x, y, 1 - c), device(z, x, 1 - y, c), device(z, 1 - x, y, c)
    column = [(z + step) % 4 for step in range(1, 4)]
    for target in (core_to, y_to, x_to, *[device(other, x, y, c) for other in column]):
        signal(target)
    own, other = y * 2 + c, (1 - y) * 2 + c
    all_ref[own, :, :width] = sums[2][:, :width]
    all_ref[own, :, width:] = sums[3][:, 3 * width :]
    squares = jnp.sum(squares_ref[...], 0, keepdims=True)
    for part in sums:
        for first in range(0, part.shape[1], BLOCK):
            values = part[:, first : first + BLOCK]
            squares += jnp.sum(values * values, 0, keepdims=True)
    facts[0:1] = squares
    facts[1:2] = jnp.broadcast_to(jnp.sum(losses_ref[...], 0, keepdims=True), squares.shape)
    facts[2:8] = jnp.zeros((6, BLOCK), f32)
    pl.semaphore_wait(pltpu.get_barrier_semaphore(), 6)
    swap_pair = remote(facts, pair, send_sem.at[0], recv_sem.at[0], core_to)
    swap_pair.start()
    block = all_ref.at[own]
    shared_side = remote(block, block, send_sem.at[3], recv_sem.at[3], y_to)
    shared_pair = remote(block, block, send_sem.at[4], recv_sem.at[4], core_to)
    swap_pair.wait()
    total_ref[...] = facts[...] + pair[...]
    swap_side = remote(total_ref, side, send_sem.at[1], recv_sem.at[1], y_to)
    swap_side.start()
    shared_side.start()
    shared_pair.start()
    swap_side.wait()
    total_ref[...] += side[...]
    swap_cross = remote(total_ref, cross, send_sem.at[2], recv_sem.at[2], x_to)
    swap_cross.start()
    swap_cross.wait()
    total_ref[...] += cross[...]
    line[z] = total_ref[...]
    lines = [
        remote(line.at[z], line.at[z], line_send.at[step], line_recv.at[z], device(to, x, y, c))
        for step, to in enumerate(column)
    ]
    for copy in lines:
        copy.start()
    shared_side.wait()
    relay = remote(all_ref.at[other], all_ref.at[other], send_sem.at[5], recv_sem.at[5], core_to)
    relay.start()
    for step, to in enumerate(column):
        lines[step].wait_send()
        remote(line.at[to], line.at[to], line_send.at[step], line_recv.at[to], core_to).wait_recv()
    total_ref[...] = (line[0] + line[1]) + (line[2] + line[3])
    shared_pair.wait()
    relay.wait()


def finish_sums(losses, squares, sums, width, tag):
    small = (8, BLOCK)
    return pl.pallas_call(
        functools.partial(finish_sums_kernel, width),
        in_specs=[IN_VMEM] * 6,
        out_specs=[IN_VMEM] * 2,
        out_shape=[
            jax.ShapeDtypeStruct(small, f32),
            jax.ShapeDtypeStruct((4, squares.shape[0], 2 * width), f32),
        ],
        scratch_shapes=[pltpu.VMEM(small, f32)] * 4
        + [
            pltpu.VMEM((4,) + small, f32),
            pltpu.SemaphoreType.DMA,
            pltpu.SemaphoreType.DMA((6,)),
            pltpu.SemaphoreType.DMA((6,)),
            pltpu.SemaphoreType.DMA((3,)),
            pltpu.SemaphoreType.DMA((4,)),
        ],
        compiler_params=pltpu.CompilerParams(collective_id=tag, has_side_effects=True),
        name="finish_sums",
    )(losses, squares, *sums)


def identity(size):
    rows = lax.broadcasted_iota(jnp.int32, (size, size), 0)
    columns = lax.broadcasted_iota(jnp.int32, (size, size), 1)
    return (rows == columns).astype(f32).astype(low)


def turn(values):
    return dot_rows(identity(values.shape[1]), values)


TABLES = 2


def lookup_kernel(counts_ref, keys_ref, weights_ref, words_ref, table_ref, rows_ref):
    width, slab = weights_ref.shape
    rows, _, seq = words_ref.shape
    shift = slab.bit_length()

    @pl.when(pl.program_id(0) == 0)
    def fill():
        def step(index, carry):
            first = pl.multiple_of(index * 9 * BLOCK, BLOCK)
            for part in range(9):
                at = first + part * BLOCK
                table_ref[pl.ds(at, BLOCK), :] = turn(weights_ref[:, pl.ds(at, BLOCK)].astype(low))
            return carry

        lax.fori_loop(0, slab // (9 * BLOCK), step, 0)
        table_ref[pl.ds(slab, 8), :] = jnp.zeros((8, width), f32)

    rows_ref[...] = jnp.zeros_like(rows_ref)

    def step(index, carry):
        for offset in range(UNROLL):
            key = keys_ref[0, 0, index * UNROLL + offset]
            spot, token = key & ((1 << shift) - 1), key >> shift
            rows_ref[pl.ds(token, 1), :] = table_ref[pl.ds(spot, 1), :]
        return carry

    lax.fori_loop(0, pl.cdiv(counts_ref[pl.program_id(0)], UNROLL), step, 0)
    for row in range(rows):
        values = rows_ref[row * seq : (row + 1) * seq, :].astype(low)
        words_ref[row] = dot_rows(identity(width), values).astype(low)


def lookup(counts, keys, weights, seq):
    steps, tokens = keys.shape
    width, slab = weights.shape
    rows = tokens // seq
    return pl.pallas_call(
        lookup_kernel,
        grid=(steps,),
        in_specs=[
            pl.BlockSpec(memory_space=pltpu.SMEM),
            pl.BlockSpec((1, 1, tokens), lambda step: (step, 0, 0), memory_space=pltpu.SMEM),
            pl.BlockSpec(weights.shape, lambda step: (0, 0)),
        ],
        out_specs=pl.BlockSpec((rows, width, seq), lambda step: (step, 0, 0)),
        out_shape=jax.ShapeDtypeStruct((steps * rows, width, seq), low),
        scratch_shapes=[pltpu.VMEM((slab + 8, width), f32), pltpu.VMEM((tokens + 8, width), f32)],
        compiler_params=pltpu.CompilerParams(vmem_limit_bytes=48 << 20),
        name="lookup",
    )(counts, keys[:, None], weights)


def deposit_kernel(counts_ref, keys_ref, grads_ref, total_ref, squares_ref, rows_ref, *tables):
    width, slab = total_ref.shape
    rows, _, seq = grads_ref.shape
    shift = slab.bit_length()

    @pl.when(pl.program_id(0) == 0)
    def clear():
        for table in tables:
            table[...] = jnp.zeros_like(table)
        rows_ref[pl.ds(rows * seq, 8), :] = jnp.zeros((8, width), f32)

    for row in range(rows):
        for first in range(0, seq, BLOCK):
            at = row * seq + first
            rows_ref[at : at + BLOCK, :] = turn(grads_ref[row, :, first : first + BLOCK])

    def step(index, carry):
        for offset in range(0, UNROLL, len(tables)):
            keys = [keys_ref[0, 0, index * UNROLL + offset + part] for part in range(len(tables))]
            spots = [key & ((1 << shift) - 1) for key in keys]
            sums = [
                table[pl.ds(spot, 1), :] + rows_ref[pl.ds(key >> shift, 1), :]
                for key, spot, table in zip(keys, spots, tables)
            ]
            for spot, table, value in zip(spots, tables, sums):
                table[pl.ds(spot, 1), :] = value
        return carry

    lax.fori_loop(0, pl.cdiv(counts_ref[pl.program_id(0)], UNROLL), step, 0)

    @pl.when(pl.program_id(0) == pl.num_programs(0) - 1)
    def finish():
        squares_ref[...] = jnp.zeros_like(squares_ref)

        def step(index, carry):
            first = pl.multiple_of(index * 9 * BLOCK, BLOCK)
            squares = jnp.zeros((width, BLOCK), f32)
            for part in range(9):
                at = pl.ds(first + part * BLOCK, BLOCK)
                block = sum(table[at, :] for table in tables).T
                total_ref[:, at] = block
                squares += block * block
            squares_ref[...] += squares
            return carry

        lax.fori_loop(0, slab // (9 * BLOCK), step, 0)


def deposit(counts, keys, grads, slab):
    steps, tokens = keys.shape
    _, width, seq = grads.shape
    rows = tokens // seq
    return pl.pallas_call(
        deposit_kernel,
        grid=(steps,),
        in_specs=[
            pl.BlockSpec(memory_space=pltpu.SMEM),
            pl.BlockSpec((1, 1, tokens), lambda step: (step, 0, 0), memory_space=pltpu.SMEM),
            pl.BlockSpec((rows, width, seq), lambda step: (step, 0, 0)),
        ],
        out_specs=[
            pl.BlockSpec((width, slab), lambda step: (0, 0)),
            pl.BlockSpec((width, BLOCK), lambda step: (0, 0)),
        ],
        out_shape=[
            jax.ShapeDtypeStruct((width, slab), f32),
            jax.ShapeDtypeStruct((width, BLOCK), f32),
        ],
        scratch_shapes=[pltpu.VMEM((tokens + 8, width), f32)]
        + [pltpu.VMEM((slab + 8, width), f32)] * TABLES,
        compiler_params=pltpu.CompilerParams(vmem_limit_bytes=60 << 20),
        name="deposit",
    )(counts, keys[:, None], grads)


def whiten(values):
    center = values - jnp.mean(values, -1, keepdims=True)
    rate = lax.rsqrt(jnp.mean(center * center, -1, keepdims=True) + layer_eps)
    return center * rate, rate


def unwhiten(upstream, gain, white, rate):
    scaled = upstream * gain
    inner = jnp.mean(scaled, -1, keepdims=True)
    along = jnp.mean(scaled * white, -1, keepdims=True)
    return (
        rate * (scaled - inner - white * along),
        jnp.sum(upstream * white, 0, keepdims=True),
        jnp.sum(upstream, 0, keepdims=True),
    )


def selection(length, entries):
    rows = lax.broadcasted_iota(jnp.int32, (2 * length, entries), 0)
    columns = lax.broadcasted_iota(jnp.int32, (2 * length, entries), 1)
    return (jnp.clip(length + entries // 2 - rows, 0, entries - 1) == columns).astype(f32).astype(low)


def prepare_kernel(*refs, between=lambda group: None):
    weights_ref, words_ref, vec_ref, white_ref, rate_ref, qkv_ref = refs[:6]
    rel_white_ref, rel_rate_ref, table_ref, low_ref, rel_ref = refs[6:]
    groups, model = weights_ref.shape[:2]
    seq = words_ref.shape[1]
    part = rel_ref.shape[0] // groups
    width = qkv_ref.shape[2] // 3
    terms = turn(weights_ref[0, :, 4 * BLOCK : 5 * BLOCK])
    half = BLOCK // 2
    vec_ref[...] = terms[half : half + 16] + terms[half + 16 : half + 32] + terms[half + 32 : half + 48]
    for group in range(groups):
        rows = slice(group * part, (group + 1) * part)
        entries = turn(weights_ref[group, :, 5 * BLOCK : 6 * BLOCK]) + turn(
            weights_ref[group, :, 6 * BLOCK : 7 * BLOCK]
        )
        white, rate = whiten(entries)
        rel_white_ref[rows, :] = white
        rel_rate_ref[rows, :] = rate
        rel_ref[rows, :] = (white * vec_ref[2:3] + vec_ref[3:4]).astype(low)
    for first in range(0, seq, BLOCK):
        rows = slice(first, first + BLOCK)
        white, rate = whiten(turn(words_ref[:, rows]))
        white_ref[rows, :] = white
        rate_ref[rows, :] = rate
        low_ref[rows, :] = (white * vec_ref[0:1] + vec_ref[1:2]).astype(low)
    chosen = selection(seq, rel_ref.shape[0])

    def step(group, carry):
        between(group)
        qkv_ref[group] = dot_plain(low_ref[...], weights_ref[group, :, : 3 * width]).astype(low)
        keys = dot_plain(rel_ref[...], weights_ref[group, :, : 2 * width]).astype(low)
        table_ref[group] = dot_plain(chosen, keys).astype(low)
        return carry

    lax.fori_loop(0, groups, step, 0)


def prepared(weights, seq, width, entries):
    groups, model = weights.shape[:2]
    outputs = [
        jax.ShapeDtypeStruct((16, model), f32),
        jax.ShapeDtypeStruct((seq, model), f32),
        jax.ShapeDtypeStruct((seq, 1), f32),
        jax.ShapeDtypeStruct((groups, seq, 3 * width), low),
        jax.ShapeDtypeStruct((entries, model), f32),
        jax.ShapeDtypeStruct((entries, 1), f32),
        jax.ShapeDtypeStruct((groups, 2 * seq, 2 * width), low),
    ]
    return outputs, [pltpu.VMEM((seq, model), low), pltpu.VMEM((entries, model), low)]


def prepare(weights, words, width, entries):
    outputs, scratch = prepared(weights, words.shape[1], width, entries)
    return pl.pallas_call(
        prepare_kernel,
        in_specs=[IN_VMEM] * 2,
        out_specs=[IN_VMEM] * 7,
        out_shape=outputs,
        scratch_shapes=scratch,
        compiler_params=pltpu.CompilerParams(vmem_limit_bytes=56 << 20),
        name="prepare",
    )(weights, words)


GATHER_SLOTS = {
    1: (("line", 2),),
    4: (("line", 3), ("sides", 1)),
    8: (("sides", 2),),
    9: (("sides", 3), ("corners", 0)),
    11: (("corners", 1),),
}
GATHER_END = (("corners", 2), ("corners", 3), ("finish", 0))


def attend_gather_kernel(length_ref, weights_ref, words_ref, pack_ref, *refs):
    outputs, probs_ref, mixed_ref, all_ref = refs[:7], refs[7], refs[8], refs[9]
    low_ref, rel_ref, far_ref, *sems = refs[10:]
    qkv_ref, table_ref = outputs[3], outputs[6]
    groups, heads = qkv_ref.shape[0], far_ref.shape[0]
    spot = place()
    greet(*spot, True)
    start, steps = gather_stages(spot, pack_ref, all_ref, *sems)
    start()
    run_all(steps, (("line", 0),))

    def between(group):
        pl.when(group == 2)(lambda: run_all(steps, (("line", 1), ("sides", 0))))

    prepare_kernel(weights_ref, words_ref, *outputs, low_ref, rel_ref, between=between)

    def step(group, carry):
        for head in range(heads):
            attend_head(group, head, length_ref[0], qkv_ref, table_ref, probs_ref, mixed_ref, far_ref)
            for slot, timed in GATHER_SLOTS.items():
                if slot % heads == head:
                    pl.when(group == slot // heads)(functools.partial(run_all, steps, timed))
        return carry

    lax.fori_loop(0, groups, step, 0)
    run_all(steps, GATHER_END)


def attend_gather(length, weights, words, pack, width, entries, tag):
    groups = weights.shape[0]
    seq = words.shape[1]
    heads = width // HEAD_DIM
    outputs, scratch = prepared(weights, seq, width, entries)
    return pl.pallas_call(
        attend_gather_kernel,
        in_specs=[pl.BlockSpec(memory_space=pltpu.SMEM), IN_VMEM, IN_VMEM, ANYWHERE],
        out_specs=[IN_VMEM] * 9 + [ANYWHERE],
        out_shape=outputs
        + [
            jax.ShapeDtypeStruct((groups * heads, seq, seq), low),
            jax.ShapeDtypeStruct((groups, seq, width), low),
            jax.ShapeDtypeStruct((4, 8) + pack.shape, low),
        ],
        scratch_shapes=scratch + [pltpu.VMEM((heads, seq, seq), f32)] + gather_scratch(),
        compiler_params=pltpu.CompilerParams(
            collective_id=tag, has_side_effects=True, vmem_limit_bytes=56 << 20
        ),
        name="attend_gather",
    )(length, weights, words, pack)


def middle_kernel(
    weights_ref,
    vec_ref,
    white_ref,
    mixed_ref,
    marks_ref,
    contract_out,
    expand_out,
    joint_out,
    mixed_out,
    sum_out,
    vec_out,
    loss_out,
    combine_ref,
    readout_ref,
    slope_ref,
    acts_ref,
    mid_ref,
    mid_white_ref,
    out_white_ref,
    gate_ref,
):
    groups, model = weights_ref.shape[:2]
    seq = white_ref.shape[0]
    width = mixed_ref.shape[2]
    hidden = acts_ref.shape[2]
    vec = [vec_ref[row : row + 1] for row in range(11)]
    for group in range(groups):
        joint = weights_ref[group, :, 2 * hidden :]
        readout_ref[:, group * width : (group + 1) * width] = joint[:, :width]
        combine_ref[group] = joint[:, width:]
    total = white_ref[...] * vec[0] + vec[1]
    for group in range(groups):
        total += dot_rows(mixed_ref[group], combine_ref[group])
    mid_white, mid_rate = whiten(total)
    mid_white_ref[...] = mid_white
    hidden_mid = mid_white * vec[4] + vec[5]
    sum_out[...] = hidden_mid
    mid_ref[...] = hidden_mid.astype(low)

    def forward(group, carry):
        gate = dot_plain(mid_ref[...], weights_ref[group, :, :hidden])
        share = 0.5 + 0.5 * lax.erf(gate * 0.5**0.5)
        acts_ref[group] = (gate * share).astype(low)
        slope_ref[group] = share + gate * jnp.exp(-0.5 * gate * gate) * (2.0 * jnp.pi) ** -0.5
        sum_out[...] += dot_rows(acts_ref[group], weights_ref[group, :, hidden : 2 * hidden])
        return carry

    lax.fori_loop(0, groups, forward, 0)
    out_white, out_rate = whiten(sum_out[...])
    out_white_ref[...] = out_white
    gate_ref[...] = (out_white * vec[6] + vec[7]).astype(low)
    dense = dot_plain(gate_ref[...], readout_ref[...])
    share = 0.5 + 0.5 * lax.erf(dense * 0.5**0.5)
    slope = share + dense * jnp.exp(-0.5 * dense * dense) * (2.0 * jnp.pi) ** -0.5
    white, rate = whiten(dense * share)
    head = white * vec[8] + vec[9]
    logits = jnp.sum(head * vec[10], -1, keepdims=True)
    weight, flags = marks_ref[:, 0:1], marks_ref[:, 1:2]
    losses = jnp.maximum(logits, 0.0) + jnp.log1p(jnp.exp(-jnp.abs(logits))) - flags * logits
    loss_out[...] = jnp.where(weight > 0.0, losses, 0.0)
    pull = (1.0 / (1.0 + jnp.exp(-logits)) - flags) * weight
    vec_out[6:7, :] = jnp.sum(head * pull, 0, keepdims=True)
    upstream, vec_out[4:5, :], vec_out[5:6, :] = unwhiten(pull * vec[10], vec[8], white, rate)
    dense_low = (upstream * slope).astype(low)
    turned = gate_ref[...].astype(f32).T.astype(low)
    for group in range(groups):
        joint_out[group, :, :width] = dot_plain(
            turned, dense_low[:, group * width : (group + 1) * width]
        ).astype(low)
    upstream, vec_out[2:3, :], vec_out[3:4, :] = unwhiten(
        dot_rows(dense_low, readout_ref[...]), vec[6], out_white_ref[...], out_rate
    )
    sum_out[...] = upstream
    gate_ref[...] = upstream.astype(low)
    upstream_turned = upstream.T.astype(low)
    mid_turned = mid_ref[...].astype(f32).T.astype(low)

    def backward(group, carry):
        contract_out[group] = dot_plain(upstream_turned, acts_ref[group]).astype(low)
        acts_ref[group] = (
            dot_plain(gate_ref[...], weights_ref[group, :, hidden : 2 * hidden]) * slope_ref[group]
        ).astype(low)
        expand_out[group] = dot_plain(mid_turned, acts_ref[group]).astype(low)
        sum_out[...] += dot_rows(acts_ref[group], weights_ref[group, :, :hidden])
        return carry

    lax.fori_loop(0, groups, backward, 0)
    upstream, vec_out[0:1, :], vec_out[1:2, :] = unwhiten(
        sum_out[...], vec[4], mid_white_ref[...], mid_rate
    )
    vec_out[7:8, :] = jnp.zeros((1, model), f32)
    sum_out[...] = upstream
    gate_ref[...] = upstream.astype(low)
    turned = upstream.T.astype(low)
    for group in range(groups):
        mixed_out[group] = dot_plain(gate_ref[...], combine_ref[group]).astype(low)
        joint_out[group, :, width:] = dot_plain(turned, mixed_ref[group]).astype(low)


def middle(weights, vec, white, mixed, marks):
    groups, model = weights.shape[:2]
    seq, width = mixed.shape[1:]
    hidden = weights.shape[2] // 2 - width
    wide = pltpu.VMEM((seq, model), f32)
    outputs = [
        ((groups, model, hidden), low),
        ((groups, model, hidden), low),
        ((groups, model, 2 * width), low),
        ((groups, seq, width), low),
        ((seq, model), f32),
        ((8, model), f32),
        ((seq, 1), f32),
    ]
    return pl.pallas_call(
        middle_kernel,
        grid=(1,),
        in_specs=[
            pl.BlockSpec(
                array.shape,
                functools.partial(lambda rank, step: (0,) * rank, array.ndim),
                pipeline_mode=pl.Buffered(1),
            )
            for array in (weights, vec, white, mixed, marks)
        ],
        out_specs=[
            pl.BlockSpec(
                shape,
                functools.partial(lambda rank, step: (0,) * rank, len(shape)),
                pipeline_mode=pl.Buffered(1),
            )
            for shape, _ in outputs
        ],
        out_shape=[jax.ShapeDtypeStruct(*output) for output in outputs],
        scratch_shapes=[
            pltpu.VMEM((groups, model, width), low),
            pltpu.VMEM((model, model), low),
            pltpu.VMEM((groups, seq, hidden), f32),
            pltpu.VMEM((groups, seq, hidden), low),
            pltpu.VMEM((seq, model), low),
            wide,
            wide,
            pltpu.VMEM((seq, model), low),
        ],
        compiler_params=pltpu.CompilerParams(vmem_limit_bytes=60 << 20),
        name="middle",
    )(weights, vec, white, mixed, marks)


def project_back_kernel(
    weights_ref,
    vec_ref,
    white_ref,
    rate_ref,
    rel_white_ref,
    rel_rate_ref,
    sum_ref,
    grads_ref,
    tables_ref,
    vec_grads_ref,
    words_out,
    project_out,
    total_ref,
    fold_ref,
    between=lambda point: None,
):
    groups, model = weights_ref.shape[:2]
    seq = white_ref.shape[0]
    width = grads_ref.shape[2] // 3
    entries = rel_white_ref.shape[0]
    part = entries // groups
    vec = [vec_ref[row : row + 1] for row in range(4)]
    turned = (white_ref[...] * vec[0] + vec[1]).T.astype(low)
    rel_turned = (rel_white_ref[...] * vec[2] + vec[3]).T.astype(low)
    chosen = selection(seq, entries)
    total_ref[...] = sum_ref[...]
    between(-1)
    rel_total = jnp.zeros((entries, model), f32)
    for group in range(groups):
        fold_ref[...] = dot_left(chosen, tables_ref[group]).astype(low)
        total_ref[...] += dot_rows(grads_ref[group], weights_ref[group, :, : 3 * width])
        rel_total += dot_rows(fold_ref[...], weights_ref[group, :, : 2 * width])
        project_out[group, :, : 2 * width] = (
            dot_plain(turned, grads_ref[group, :, : 2 * width]) + dot_plain(rel_turned, fold_ref[...])
        ).astype(low)
        project_out[group, :, 2 * width : 3 * width] = dot_plain(
            turned, grads_ref[group, :, 2 * width :]
        ).astype(low)
        between(group)
    upstream, gain_grad, bias_grad = unwhiten(total_ref[...], vec[0], white_ref[...], rate_ref[...])
    words_out[...] = upstream.T.astype(low)
    between(groups)
    rel_up, rel_gain_grad, rel_bias_grad = unwhiten(
        rel_total, vec[2], rel_white_ref[...], rel_rate_ref[...]
    )
    turned = rel_up.T.astype(low)
    for group in range(groups):
        project_out[group, :, 3 * width + BLOCK // 2 :] = turned[:, group * part : (group + 1) * part]
    rows = [gain_grad, bias_grad, rel_gain_grad, rel_bias_grad]
    rows += [vec_grads_ref[row : row + 1] for row in range(7)]
    rows += [jnp.zeros((1, model), f32)]
    for group in range(groups):
        three = jnp.concatenate(rows[3 * group : 3 * group + 3] + [jnp.zeros((BLOCK - 3, model), f32)], 0)
        project_out[group, :, 3 * width : 3 * width + BLOCK // 2] = three.T.astype(low)[:, : BLOCK // 2]


def projected_back(weights, white, grads, rel_white):
    groups, model = weights.shape[:2]
    seq = white.shape[0]
    width = grads.shape[2] // 3
    entries = rel_white.shape[0]
    outputs = [
        jax.ShapeDtypeStruct((model, seq), low),
        jax.ShapeDtypeStruct((groups, model, 3 * width + BLOCK // 2 + entries // groups), low),
    ]
    return outputs, [pltpu.VMEM((seq, model), f32), pltpu.VMEM((entries, 2 * width), low)]


def project_back(weights, vec, white, rate, rel_white, rel_rate, total, grads, tables, vec_grads):
    outputs, scratch = projected_back(weights, white, grads, rel_white)
    return pl.pallas_call(
        project_back_kernel,
        in_specs=[IN_VMEM] * 10,
        out_specs=[IN_VMEM] * 2,
        out_shape=outputs,
        scratch_shapes=scratch,
        compiler_params=pltpu.CompilerParams(vmem_limit_bytes=56 << 20),
        name="project_back",
    )(weights, vec, white, rate, rel_white, rel_rate, total, grads, tables, vec_grads)


PROJECT_STEPS = {
    -1: ("pair",),
    1: ("first",),
    2: ("second", "line0"),
    3: ("line1",),
    4: ("line2",),
}


def project_back_sums_kernel(count, chunks, *refs):
    inputs, grads = refs[:10], refs[10 : 10 + count]
    outputs, totals = refs[10 + count : 12 + count], refs[12 + count : 12 + 2 * count]
    work, rest = refs[12 + 2 * count : 14 + 2 * count], refs[14 + 2 * count :]
    spot = place()
    greet(*spot, True)
    start, stages = sum_stages(spot, grads, totals, chunks, rest)
    start()

    def between(point):
        for name in PROJECT_STEPS.get(point, ()):
            run_all(stages, [(name, chunk) for chunk in range(len(chunks))])

    project_back_kernel(*inputs, *outputs, *work, between=between)
    run_all(stages, [("total", chunk) for chunk in range(len(chunks))])


def project_back_sums(*inputs, grads, tag):
    weights, white, rel_white, upstream = inputs[0], inputs[2], inputs[4], inputs[7]
    outputs, scratch = projected_back(weights, white, upstream, rel_white)
    part = grads[0].shape[1] // 8
    sizes = [grad.shape[2] for grad in grads]
    chunks = chunked(sizes)
    return pl.pallas_call(
        functools.partial(project_back_sums_kernel, len(grads), chunks),
        in_specs=[IN_VMEM] * 10 + [ANYWHERE] * len(grads),
        out_specs=[IN_VMEM] * (2 + len(grads)),
        out_shape=outputs + [jax.ShapeDtypeStruct((part, size), f32) for size in sizes],
        scratch_shapes=scratch + sum_scratch(part, [chunk[2] for chunk in chunks]),
        compiler_params=pltpu.CompilerParams(
            collective_id=tag, has_side_effects=True, vmem_limit_bytes=56 << 20
        ),
        name="project_back_sums",
    )(*inputs, *[grad.reshape(4, 4, 2, part, -1) for grad in grads])


def split_terms(values, count):
    terms = []
    for _ in range(count):
        term = lax.reduce_precision(values, 8, 7)
        terms.append(term.astype(low))
        values = values - term
    return terms


def adamw(weight, gradient, mean, square, rate_now):
    first = beta_first * mean + (1.0 - beta_first) * gradient
    second = beta_second * square + (1.0 - beta_second) * gradient * gradient
    mean_hat = first / (1.0 - beta_first**STEP)
    square_hat = second / (1.0 - beta_second**STEP)
    master = weight - rate_now * (
        mean_hat / (jnp.sqrt(square_hat) + adam_eps) + weight_decay * weight
    )
    return (first, second, master)


def update_kernel(width, *refs):
    facts_ref, shared_ref, *grads = refs[:7]
    weights, refs = refs[7:31], refs[31:]
    outputs, (factor_ref, bias_ref) = refs[:24], refs[24:26]
    squares = jnp.sum(facts_ref[0:1, :], 1, keepdims=True)
    factor = jnp.minimum(1.0, clip_level / jnp.sqrt(squares))

    def update(index, spot, gradient):
        weight, mean, square = [part.at[spot] for part in weights[3 * index : 3 * index + 3]]
        results = adamw(
            weight[...], gradient * factor, mean[...], square[...], rate_steps[index]
        )
        for part, value in zip(outputs[3 * index : 3 * index + 3], results):
            part.at[spot][...] = value

    everything = slice(None)
    update(0, (everything, everything), grads[0][...])

    @pl.when(pl.program_id(0) == 0)
    def small():
        contract, expand, joint, project = grads[1:]
        factor_ref[...] = jnp.broadcast_to(jnp.sqrt(squares), factor_ref.shape)
        for group in range(4):
            part = slice(group * BLOCK, (group + 1) * BLOCK)
            update(1, (everything, part), shared_ref[group, :, width + BLOCK // 2 :])
            part = slice(group * width, (group + 1) * width)
            update(6, (everything, part), shared_ref[group, :, :width])
        for kind in range(3):
            part = slice(kind * width, (kind + 1) * width)
            update(2, (kind,), project[:, part])
        update(3, (everything, everything), joint[:, width:].T)
        update(4, (everything, everything), expand[...])
        update(5, (everything, everything), contract[...])
        count = weights[21].shape[0]
        for group in range(4):
            rows = shared_ref[group, :, BLOCK : 2 * BLOCK].T[BLOCK // 2 :]
            first = 3 * group
            last = min(first + 3, count)
            update(7, (slice(first, last), everything), rows[: last - first])
            if group == 1:
                bias_ref[...] = rows[0:1] * factor


def update_all(facts, shared, grads, weights, width):
    rows, slab = grads[0].shape
    columns = 11 * BLOCK
    stripe = pl.BlockSpec((rows, columns), lambda step: (0, step))

    def full(array):
        return pl.BlockSpec(array.shape, functools.partial(lambda rank, step: (0,) * rank, array.ndim))

    in_specs = [full(facts), full(shared), stripe] + [full(grad) for grad in grads[1:]]
    in_specs += [stripe] * 3 + [full(weight) for weight in weights[3:]]
    results = [jax.ShapeDtypeStruct(weight.shape, f32) for weight in weights]
    results += [jax.ShapeDtypeStruct((1, BLOCK), f32), jax.ShapeDtypeStruct((1, rows), f32)]
    return pl.pallas_call(
        functools.partial(update_kernel, width),
        grid=(slab // columns,),
        in_specs=in_specs,
        out_specs=[stripe] * 3 + [full(result) for result in results[3:]],
        out_shape=results,
        compiler_params=pltpu.CompilerParams(vmem_limit_bytes=62 << 20),
        name="update_all",
    )(facts, shared, *grads, *weights)


def per_device(
    token_ids,
    row_lengths,
    replaced,
    embedding,
    relative,
    project,
    combine,
    expand,
    contract,
    readout,
    vectors,
    embedding_mean,
    relative_mean,
    project_mean,
    combine_mean,
    expand_mean,
    contract_mean,
    readout_mean,
    vectors_mean,
    embedding_square,
    relative_square,
    project_square,
    combine_square,
    expand_square,
    contract_square,
    readout_square,
    vectors_square,
):
    pieces = lax.axis_size("heads")
    holder = lax.axis_index("heads")
    owners = lax.axis_size("dp")
    row_count, seq_len = token_ids.shape
    width = vectors.shape[1]
    model = width * owners
    everyone = ("heads", "dp")
    head_width = project.shape[2]
    hidden = expand.shape[1]
    vocab_slab = embedding.shape[1]
    span_part = relative.shape[0] // pieces
    vector_count = vectors.shape[0]
    direct = owners == 8 and pieces == 4

    own_relative = lax.dynamic_slice_in_dim(relative, holder * span_part, span_part, 0).T
    own_readout = lax.dynamic_slice_in_dim(readout, holder * head_width, head_width, 1)
    vector_terms = [
        jnp.pad(term, ((0, 0), (0, 16 - vector_count))) for term in split_terms(vectors.T, 3)
    ]
    high, rest = split_terms(own_relative, 2)
    first_pack = jnp.concatenate(
        [
            project.reshape(width, 3 * head_width).astype(low),
            *vector_terms,
            jnp.zeros((width, 16), low),
            high,
            rest,
        ],
        1,
    )
    second_pack = jnp.concatenate(
        [
            expand.astype(low),
            contract.T.astype(low),
            own_readout.astype(low),
            combine.T.astype(low),
        ],
        1,
    )
    first_all = lax.all_gather(first_pack, everyone, axis=0, tiled=True)
    first_all = first_all.reshape(pieces, model, -1)

    length_row = jnp.pad(row_lengths[None, :], ((0, 0), (0, seq_len - row_count)))
    facts = jnp.concatenate([token_ids, jnp.pad(length_row, ((0, 8 - 1 - row_count), (0, 0)))], 0)
    all_facts = share_facts(facts, 1) if direct else lax.all_gather(facts, "dp")
    all_ids = all_facts[:, :row_count].reshape(owners * row_count, seq_len)
    all_lengths = all_facts[:, row_count, :row_count].reshape(-1)
    token_total = jnp.sum(all_lengths).astype(f32)
    local_ids = all_ids - holder * vocab_slab
    inside = (local_ids >= 0) & (local_ids < vocab_slab)
    inside = inside & (jnp.arange(seq_len)[None] < all_lengths[:, None])
    inside = inside.reshape(-1, ROW_SET * seq_len)
    counts = jnp.sum(inside.astype(jnp.int32), 1)
    shift = vocab_slab.bit_length()
    keys = jnp.arange(ROW_SET * seq_len, dtype=jnp.int32)[None] << shift
    keys = jnp.where(
        inside,
        keys + local_ids.reshape(inside.shape),
        ((ROW_SET * seq_len) << shift) + vocab_slab,
    )
    keys = lax.sort(keys.T, dimension=0, is_stable=False).T

    found = lookup(counts, keys, embedding, seq_len)
    found = found.reshape(owners, row_count, width, seq_len)
    if direct:
        found = exchange_words(found, 2)
    else:
        found = lax.psum_scatter(found, "heads", scatter_dimension=1, tiled=True)[:, 0]
        found = lax.all_to_all(found, "dp", 0, 0, tiled=True)
    own_length = lax.dynamic_slice_in_dim(row_lengths, holder, 1)
    own_live = jnp.arange(seq_len) < own_length
    own_flags = lax.dynamic_slice_in_dim(replaced, holder, 1)[0].astype(f32)
    marks = jnp.stack([jnp.where(own_live, 1.0 / token_total, 0.0), own_flags], 1)

    entries = relative.shape[0]
    words = found.reshape(model, seq_len)
    if direct:
        *ready, probs, mixed, second_all = attend_gather(
            own_length, first_all, words, second_pack, head_width, entries, 3
        )
    else:
        ready = prepare(first_all, words, head_width, entries)
        probs, mixed = attend(own_length, ready[3], ready[6])
        second_all = lax.all_gather(second_pack, everyone, axis=0, tiled=True)
    vec_full, white, rate, qkv, rel_white, rel_rate, rel_table = ready
    second_all = second_all.reshape(pieces, model, -1)
    grad_contract, grad_expand, grad_joint, grad_mixed, grad_sum, grad_vec, losses = middle(
        second_all, vec_full, white, mixed, marks
    )
    back = (first_all, vec_full, white, rate, rel_white, rel_rate, grad_sum)
    if direct:
        qkv_grads, rel_table_grads, *sums = attend_back_sums(
            qkv, rel_table, probs, grad_mixed, [grad_contract, grad_expand], 4
        )
        sent, grad_project, joint_sum = project_back_sums(
            *back, qkv_grads, rel_table_grads, grad_vec, grads=[grad_joint], tag=7
        )
        sums.append(joint_sum)
    else:
        qkv_grads, rel_table_grads = attend_back(qkv, rel_table, probs, grad_mixed)
        sent, grad_project = project_back(*back, qkv_grads, rel_table_grads, grad_vec)
    sent = sent.reshape(owners, width, seq_len)
    if direct:
        sent, late_sum = return_sums(sent, grad_project, 5)
        sums.append(late_sum)
    else:
        sent = lax.all_to_all(sent, "dp", 0, 0, tiled=True)
        sent = lax.all_gather(sent, "heads", axis=0)
        sent = sent.transpose(1, 0, 2, 3)
        sums = [
            lax.psum_scatter(
                part.reshape(pieces * model, -1), everyone, scatter_dimension=0, tiled=True
            ).astype(f32)
            for part in (grad_contract, grad_expand, grad_joint, grad_project)
        ]
    sent = sent.reshape(owners * row_count, width, seq_len)
    grad_embedding, own_squares = deposit(counts, keys, sent, vocab_slab)

    weights = (embedding, relative, project, combine, expand, contract, readout, vectors)
    means = (
        embedding_mean,
        relative_mean,
        project_mean,
        combine_mean,
        expand_mean,
        contract_mean,
        readout_mean,
        vectors_mean,
    )
    squares = (
        embedding_square,
        relative_square,
        project_square,
        combine_square,
        expand_square,
        contract_square,
        readout_square,
        vectors_square,
    )
    if direct:
        turns = {1: (1, 0), 2: (1, 0, 2), 5: (1, 0)}
        flat = [
            part.transpose(turns[index]) if index in turns else part
            for index, parts in enumerate(zip(weights, means, squares))
            for part in parts
        ]
        all_facts, shared = finish_sums(losses, own_squares, sums, head_width, 6)
        *flat, norm_row, bias_row = update_all(
            all_facts, shared, [grad_embedding, *sums], flat, head_width
        )
        flat = [
            part.transpose(turns[index // 3]) if index // 3 in turns else part
            for index, part in enumerate(flat)
        ]
        return (all_facts[1, 0], token_total, norm_row[0, 0], *flat, bias_row[0])

    squares_local = sum(jnp.sum(part * part) for part in sums) + jnp.sum(own_squares)
    shared = jnp.concatenate([sums[2][:, :head_width], sums[3][:, 3 * head_width :]], 1)
    squares_total, loss_sum = lax.psum((squares_local, jnp.sum(losses)), everyone)
    shared = lax.all_gather(shared, "heads", axis=0)
    grad_norm = jnp.sqrt(squares_total)
    factor = jnp.minimum(1.0, clip_level / grad_norm)
    grad_readout = shared[:, :, :head_width].transpose(1, 0, 2).reshape(width, model)
    at = head_width + BLOCK // 2
    grad_relative = shared[:, :, at:].transpose(0, 2, 1).reshape(entries, width)
    grad_vec = shared[:, :, head_width : head_width + 3].transpose(0, 2, 1).reshape(-1, width)
    grad_vec = grad_vec[:vector_count]
    gradients = (
        grad_embedding,
        grad_relative,
        sums[3][:, : 3 * head_width].reshape(width, 3, head_width),
        sums[2][:, head_width:].T,
        sums[1],
        sums[0].T,
        grad_readout,
        grad_vec,
    )
    updates = [
        adamw(weight, gradient * factor, mean, square, rate_now)
        for weight, gradient, mean, square, rate_now in zip(
            weights, gradients, means, squares, rate_steps
        )
    ]
    flat = [part for parts in updates for part in parts]
    return (loss_sum, token_total, grad_norm, *flat, grad_vec[3] * factor)


def solution(mesh):
    placed = (
        P("dp", None),
        P("dp"),
        P("dp", None),
        P("dp", "heads"),
        P(None, "dp"),
        P("dp", None, "heads"),
        P("heads", "dp"),
        P("dp", "heads"),
        P("heads", "dp"),
        P("dp", None),
        P(None, "dp"),
        P("dp", "heads"),
        P(None, "dp"),
        P("dp", None, "heads"),
        P("heads", "dp"),
        P("dp", "heads"),
        P("heads", "dp"),
        P("dp", None),
        P(None, "dp"),
        P("dp", "heads"),
        P(None, "dp"),
        P("dp", None, "heads"),
        P("heads", "dp"),
        P("dp", "heads"),
        P("heads", "dp"),
        P("dp", None),
        P(None, "dp"),
    )
    return jax.shard_map(
        per_device,
        mesh=mesh,
        in_specs=placed,
        out_specs=(
            P(),
            P(),
            P(),
            P("dp", "heads"),
            P("dp", "heads"),
            P("dp", "heads"),
            P(None, "dp"),
            P(None, "dp"),
            P(None, "dp"),
            P("dp", None, "heads"),
            P("dp", None, "heads"),
            P("dp", None, "heads"),
            P("heads", "dp"),
            P("heads", "dp"),
            P("heads", "dp"),
            P("dp", "heads"),
            P("dp", "heads"),
            P("dp", "heads"),
            P("heads", "dp"),
            P("heads", "dp"),
            P("heads", "dp"),
            P("dp", None),
            P("dp", None),
            P("dp", None),
            P(None, "dp"),
            P(None, "dp"),
            P(None, "dp"),
            P("dp"),
        ),
        check_vma=False,
    )
```

time: 568 us -> 448 us (0.79)
  Pallas kernels: 434 us -> 396 us
  waiting for transfers between devices: 31.7 us -> 2.48 us
  other arithmetic: 41.7 us -> 13.5 us
  local copies, waits for them, and re-layouts: 28.8 us -> 12.8 us
    pallas_call x10 -> x9, Pallas kernels: 386 us -> 345 us  [the longest x1 77.6 us: attend_back_sums(): pl.pallas_call(functools.partial(attend_back_sums_kernel, len(grads), chu...]
    all_gather x1 -> x0, waiting for transfers between devices: 31.7 us -> none  [per_device(): second_all = lax.all_gather(second_pack, everyone, axis=0, tiled=True)]
    sub x9 -> x0, other arithmetic: 24.4 us -> none  [the longest x8 23.5 us: adamw(): weight - rate_now * (mean_hat / (jnp.sqrt(square_hat) + adam_eps) + weigh...]
    unnamed x69 -> x25, local copies, waits for them, and re-layouts: 17.9 us -> 5.66 us
  transfers between devices with their start and end apart: 2 -> 1, of which waited for: 1 -> 1; matrix products, arithmetic and copies ran while one was open for 2% -> 4% of each run, Pallas kernels for 23% -> 14%
where the time goes in v4:
time: 448 us; the launch traced here: 441 us
  Pallas kernels  396 us (88%)
  between operations  16.6 us (4%)
  other arithmetic  13.5 us (3%)
  local copies, waits for them, and re-layouts  12.8 us (3%)
    pallas_call x1, Pallas kernels, attend_back_sums(): pl.pallas_call(functools.partial(attend_back_sums_kernel, len(grads), chu...  77.6 us
    pallas_call x1, Pallas kernels, attend_gather(): pl.pallas_call(attend_gather_kernel, in_specs=[pl.BlockSpec(memory_space=...  76.8 us
    pallas_call x1, Pallas kernels, return_sums(): pl.pallas_call(functools.partial(return_sums_kernel, chunks), in_specs=[I...  54 us
    pallas_call x1, Pallas kernels, exchange_words(): pl.pallas_call(exchange_words_kernel, in_specs=[IN_VMEM], out_specs=IN_VM...  39.9 us
    pallas_call x1, Pallas kernels, middle(): pl.pallas_call(middle_kernel, grid=(1,), in_specs=[pl.BlockSpec(array.sha...  38.6 us
    pallas_call x1, Pallas kernels, project_back_sums(): pl.pallas_call(functools.partial(project_back_sums_kernel, len(grads), ch...  36.7 us
    pallas_call x1, Pallas kernels, update_all(): pl.pallas_call(functools.partial(update_kernel, width), grid=(slab // col...  22.5 us
    pallas_call x1, Pallas kernels, finish_sums(): pl.pallas_call(functools.partial(finish_sums_kernel, width), in_specs=[IN...  14.2 us
  transfers between devices with their start and end apart: 1, of which 1 were waited for; matrix products, arithmetic and copies ran while one was open for 4% of the time, Pallas kernels for 14%

profile of v4, /device:TPU:0, one launch (start us, length us, event | category | flops | bytes accessed | tf_op | source)
XLA Modules:
  0.0 440.9 jit_solution(13641435220031727857)
XLA Ops:
  7.2 0.0 all-gather.2.cloned.1.call-start
  7.3 0.7 fusion.6
  8.0 0.8 constant_dynamic-slice_fusion
  8.8 0.1 copy.76
  8.9 1.0 convert_element_type.60
  9.8 0.2 copy.68
  10.1 0.8 copy.70
  10.9 0.0 all-gather.2.cloned.1.call-update
  11.0 1.0 copy.73
  12.0 1.2 dynamic_slice.12.length_ref
  13.2 1.3 pad_add_fusion.facts_ref
  14.5 10.9 %share_facts.1 = s32[8,8,512]{2,1,0:T(8,128)} custom-call(s32[8,512]{1,0:T(8,128)} %pad_add_fusion.facts_ref), custom_call_target="tpu_custom_call" | custom-call | tf_op jit(solution)/shard_map/share_facts/pallas_call | solution.py:531
  25.5 1.4 slice_reduce_fusion
  27.5 0.1 lt.83
  27.6 1.2 convert_reduce_fusion
  28.8 0.1 reduce_sum.26
  28.9 0.1 reduce_sum.27.counts_ref
  29.1 0.1 broadcast_bitcast_fusion
  29.2 0.1 sub.26
  29.3 0.1 select_bitcast_fusion
  29.3 5.2 %sort.7 = s32[4096,4]{0,1:T(4,128)S(1)} sort(s32[4096,4]{0,1:T(4,128)S(1)} %select_bitcast_fusion), dimensions={0}, to_apply=%region_2.3 | sort | flops 229376 | bytes 131072 | tf_op jit(solution)/shard_map/sort | solution.py:1701
  34.6 0.0 copy-start.4
  34.6 1.0 convert_element_type.68
  35.6 0.7 convert_bitcast_fusion.1
  36.4 0.6 compare_select_fusion
  37.0 0.9 copy.74.marks_ref
  37.9 10.8 %lookup.1 = bf16[32,96,512]{2,1,0:T(8,128)(2,1)S(1)} custom-call(s32[4]{0:T(128)S(1)} %reduce_sum.27.counts_ref, s32[4,1,4096]{2,1,0:T(1,128)S(1)} %broadcast_in_dim.27.keys_ref, f32[96,12672]{1,0:T(8,128)} %refs_7_.1), custom_call_target="tpu_custom_call" | custom-call | tf_op jit(solution)/shard_map/lookup/pallas_call | solution.py:1011
  48.8 0.0 copy-done.5
  48.8 39.9 %exchange_words.1 = bf16[8,96,512]{2,1,0:T(8,128)(2,1)S(1)} custom-call(bf16[8,4,96,512]{3,2,1,0:T(8,128)(2,1)S(1)} %bitcast.65), custom_call_target="tpu_custom_call" | custom-call | tf_op jit(solution)/shard_map/exchange_words/pallas_call | solution.py:632
  88.7 0.0 copy-start.1
  88.7 0.9 copy-done.1
  89.6 1.0 dynamic-slice_convert_fusion
  90.6 0.0 copy-done.6
  90.6 0.8 concatenate.11.pack_ref
  91.5 2.5 all-gather.2.cloned.1.call-done
  93.9 76.8 %attend_gather.1 = (f32[16,768]{1,0:T(8,128)}, f32[512,768]{1,0:T(8,128)}, f32[512,1]{1,0:T(8,128)}, bf16[4,512,576]{2,1,0:T(8,128)(2,1)}, f32[512,768]{1,0:T(8,...) custom-call(s32[1]{0:T(128)} %dynamic_slice.12.length_ref, ...), custom_call_target="tpu_custom_call" | custom-call | tf_op jit(solution)/shard_map/attend_gather/pallas_call | solution.py:1232
  170.8 38.6 %middle.1 = (bf16[4,768,768]{2,1,0:T(8,128)(2,1)}, bf16[4,768,768]{2,1,0:T(8,128)(2,1)}, bf16[4,768,384]{2,1,0:T(8,128)(2,1)}, bf16[4,512,192]{2,1,0:T(8,128)(2,...) custom-call(bf16[4,768,1920]{2,1,0:T(8,128)(2,1)} %bitcast.71, ...), custom_call_target="tpu_custom_call" | custom-call | tf_op jit(solution)/shard_map/middle/pallas_call | solution.py:1364
  209.3 77.6 %attend_back_sums.1 = (bf16[4,512,576]{2,1,0:T(8,128)(2,1)}, bf16[4,1024,384]{2,1,0:T(8,128)(2,1)}, f32[96,768]{1,0:T(8,128)}, f32[96,768]{1,0:T(8,128)}) custom-call(bf16[4,512,576]{2,1,0:T(8,128)(2,1)} %get-tuple-element.93.refs_0_, bf16[4,1024,384]{2,1,0:T(8,128)(2,1)} %get-tuple-element.94.refs_1_, bf16[12,512,512]{2,1,0:T(8,128)(2,1)} %get-tuple-element.95.refs_2_, ...), custom_call_target="tpu_custom_call" | custom-call | tf_op jit(solution)/shard_map/attend_back_sums/pallas_call | solution.py:470
  287.0 36.7 %project_back_sums.1 = (bf16[768,512]{1,0:T(8,128)(2,1)}, bf16[4,768,768]{2,1,0:T(8,128)(2,1)}, f32[96,384]{1,0:T(8,128)}) custom-call(bf16[4,768,896]{2,1,0:T(8,128)(2,1)} %bitcast.70, f32[16,768]{1,0:T(8,128)} %get-tuple-element.85.vec_ref.refs_1_, f32[512,768]{1,0:T(8,128)} %get-tuple-element.86.white_ref.refs_2_, f32[512,1]{1,0:T(8,128)} %get-tuple-element.89.refs_3_, ...), custom_call_target="tpu_custom_call" | custom-call | tf_op jit(solution)/shard_map/project_back_sums/pallas_call | solution.py:1513
  323.7 1.1 copy-done.3
  324.9 54.0 %return_sums.1 = (bf16[8,4,96,512]{3,2,1,0:T(8,128)(2,1)S(1)}, f32[96,768]{1,0:T(8,128)S(1)}) custom-call(bf16[8,96,512]{2,1,0:T(8,128)(2,1)S(1)} %bitcast.68, bf16[4,4,2,96,768]{4,3,2,1,0:T(8,128)(2,1)} %bitcast.72), custom_call_target="tpu_custom_call" | custom-call | tf_op jit(solution)/shard_map/return_sums/pallas_call | solution.py:744
  378.9 0.0 copy-start
  378.9 1.7 copy-done
  380.5 0.7 copy-done.2
  381.3 13.4 %deposit.1 = (f32[96,12672]{1,0:T(8,128)}, f32[96,128]{1,0:T(8,128)}) custom-call(s32[4]{0:T(128)} %copy-done.5, s32[4,1,4096]{2,1,0:T(1,128)} %copy-done.4, bf16[32,96,512]{2,1,0:T(8,128)(2,1)} %bitcast.66), custom_call_target="tpu_custom_call" | custom-call | tf_op jit(solution)/shard_map/deposit/pallas_call | solution.py:1079
  394.6 14.2 %finish_sums.1 = (f32[8,128]{1,0:T(8,128)}, f32[4,96,384]{2,1,0:T(8,128)}) custom-call(f32[512,1]{1,0:T(8,128)} %get-tuple-element.88.losses_ref, f32[96,128]{1,0:T(8,128)} %get-tuple-element.106.squares_ref, f32[96,768]{1,0:T(8,128)} %get-tuple-element.107.refs_0_.refs_3_, f32[96,768]{1,0:T(8,128)} %get-tuple-element.108.refs_1_.refs_4_, ...), custom_call_target="tpu_custom_call" | custom-call | tf_op jit(solution)/shard_map/finish_sums/pallas_call | solution.py:940
  408.9 1.2 slice.14
  410.1 22.5 %update_all.1 = (f32[96,12672]{1,0:T(8,128)}, f32[96,12672]{1,0:T(8,128)}, f32[96,12672]{1,0:T(8,128)}, f32[96,512]{1,0:T(8,128)}, f32[96,512]{1,0:T(8,128)}, /*...) custom-call(f32[8,128]{1,0:T(8,128)} %get-tuple-element.111.refs_0_,, ...), custom_call_target="tpu_custom_call" | custom-call | tf_op jit(solution)/shard_map/update_all/pallas_call | solution.py:1601
  (19 shorter events, 0.2 us)
Async XLA Ops:
  7.2 86.7 %all-gather.2.cloned.1.call-start = ((), (), s32[]{:S(2)}) async-start(), calls=%async_computation | async-start | bytes 5677056 | tf_op jit(solution)/shard_map/all_gather | solution.py:1680
  29.0 19.7 %copy-start.5 = (s32[4]{0:T(128)}, s32[4]{0:T(128)S(1)}, u32[]{:S(2)}) copy-start(s32[4]{0:T(128)S(1)} %reduce_sum.27.counts_ref) | copy-start | bytes 52
  34.6 54.1 %copy-start.4 = (s32[4,1,4096]{2,1,0:T(1,128)}, s32[4,1,4096]{2,1,0:T(1,128)S(1)}, u32[]{:S(2)}) copy-start(s32[4,1,4096]{2,1,0:T(1,128)S(1)} %broadcast_in_dim.27.keys_ref) | copy-start | bytes 196612
  37.9 52.7 %copy-start.6 = (f32[768,96]{0,1:T(8,128)S(1)}, f32[768,96]{0,1:T(8,128)}, u32[]{:S(2)}) copy-start(f32[768,96]{0,1:T(8,128)} %param.35) | copy-start | bytes 884740
  88.7 0.9 copy-start.1
  323.7 1.1 copy-start.3
  378.9 1.7 copy-start
  380.5 0.7 copy-start.2
Sparse Core Ops, SparseCore 0:
  11.6 82.2 all-gather.1

commit v5 on v4

--- a/solution.py
+++ b/solution.py
@@ -202,21 +202,18 @@
     )
 
 
+def along_z(z):
+    return [(z + step) % 4 for step in (2, 1, 3)]
+
+
 def greet(z, x, y, c, line):
     signal(device(z, x, y, 1 - c))
     signal(device(z, x, 1 - y, c))
     if line:
         signal(device(z, 1 - x, y, c))
-
-        @pl.when(z < 3)
-        def above():
-            signal(device(z + 1, x, y, c))
-
-        @pl.when(z > 0)
-        def below():
-            signal(device(z - 1, x, y, c))
-
-        pl.semaphore_wait(pltpu.get_barrier_semaphore(), jnp.where((z == 0) | (z == 3), 4, 5))
+        for other in along_z(z):
+            signal(device(other, x, y, c))
+        pl.semaphore_wait(pltpu.get_barrier_semaphore(), 6)
 
 
 def remote(source, target, send, recv, to):
@@ -234,29 +231,27 @@
         (2, 4, half),
         (4, half),
         (4, half),
-        (3, width),
-        (3, width),
+        (4, width),
     )
     shapes = [pltpu.VMEM(lead + (size,), low) for lead in leads for size in sizes]
     count = len(sizes)
     return shapes + [
         pltpu.SemaphoreType.DMA((count, 2)),
-        pltpu.SemaphoreType.DMA((count, 12)),
-        pltpu.SemaphoreType.DMA((count, 12)),
+        pltpu.SemaphoreType.DMA((count, 9)),
+        pltpu.SemaphoreType.DMA((count, 10)),
     ]
 
 
 def sum_stages(spot, grads, totals, chunks, refs):
     count = len(chunks)
-    pair, own, first_a, first_b, second_a, second_b, rise, fall = [
-        refs[count * part : count * (part + 1)] for part in range(8)
+    pair, own, first_a, first_b, second_a, second_b, column = [
+        refs[count * part : count * (part + 1)] for part in range(7)
     ]
-    local_sem, send_sem, recv_sem = refs[8 * count :]
+    local_sem, send_sem, recv_sem = refs[7 * count :]
     z, x, y, c = spot
     half = grads[0].shape[3] // 2
     upper, lower = pl.ds(0, half), pl.ds(half, half)
     core_to, y_to, x_to = device(z, x, y, 1 - c), device(z, x, 1 - y, c), device(z, 1 - x, y, c)
-    up_to, down_to = device(z + 1, x, y, c), device(z - 1, x, y, c)
 
     def columns(part):
         return pl.ds(chunks[part][1], chunks[part][2])
@@ -289,13 +284,23 @@
             link(part, 5, block.at[1 - y, :, x, lower], second_b[part], y_to),
         )
 
-    def rise_copy(part, turn):
-        block = own[part].at[y, lax.clamp(0, 3 + z - turn, 3), x]
-        return link(part, 6 + turn, block, rise[part].at[turn], up_to)
-
-    def fall_copy(part, turn):
-        block = own[part].at[y, lax.clamp(0, turn - 3 + z, 3), x]
-        return link(part, 9 + turn, block, fall[part].at[turn], down_to)
+    def line_copy(part, step, to):
+        return remote(
+            own[part].at[y, to, x],
+            column[part].at[z],
+            send_sem.at[part, 6 + step],
+            recv_sem.at[part, 6 + z],
+            device(to, x, y, c),
+        )
+
+    def line_arrival(part, step, source):
+        return remote(
+            own[part].at[y, z, x],
+            column[part].at[source],
+            send_sem.at[part, 6 + step],
+            recv_sem.at[part, 6 + source],
+            device(source, x, y, c),
+        )
 
     def add(target, source):
         target[...] = (target[...].astype(f32) + source[...].astype(f32)).astype(low)
@@ -304,10 +309,6 @@
         for side in range(2):
             pair_copy(part, side).start()
             local(part, side).start()
-
-    def start():
-        for part in range(min(2, count)):
-            start_pair(part)
 
     def stage_pair(part):
         for side in range(2):
@@ -348,61 +349,22 @@
             return carry
 
         lax.fori_loop(0, 4, step, 0)
-
-    def stage_line(part, turn):
-        @pl.when((z <= turn) & (z < 3))
-        def rises():
-            if turn > 0:
-
-                @pl.when(z > 0)
-                def joined():
-                    rise_copy(part, turn - 1).wait_recv()
-                    add(own[part].at[y, 3 + z - turn, x], rise[part].at[turn - 1])
-
-            rise_copy(part, turn).start()
-
-        @pl.when((3 - z <= turn) & (z > 0))
-        def falls():
-            if turn > 0:
-
-                @pl.when(z < 3)
-                def joined():
-                    fall_copy(part, turn - 1).wait_recv()
-                    add(own[part].at[y, turn - 3 + z, x], fall[part].at[turn - 1])
-
-            fall_copy(part, turn).start()
+        for step, to in enumerate(along_z(z)):
+            line_copy(part, step, to).start()
 
     def stage_total(part):
         total = totals[chunks[part][0]].at[:, columns(part)]
         total[...] = own[part][y, z, x].astype(f32)
-
-        @pl.when(z > 0)
-        def risen():
-            rise_copy(part, 2).wait_recv()
-            total[...] += rise[part][2].astype(f32)
-
-        @pl.when(z < 3)
-        def fallen():
-            fall_copy(part, 2).wait_recv()
-            total[...] += fall[part][2].astype(f32)
-
-        for turn in range(3):
-
-            @pl.when((z <= turn) & (z < 3))
-            def risen_out():
-                rise_copy(part, turn).wait_send()
-
-            @pl.when((3 - z <= turn) & (z > 0))
-            def fallen_out():
-                fall_copy(part, turn).wait_send()
-
-    return start, {
+        for step, other in enumerate(along_z(z)):
+            line_arrival(part, step, other).wait_recv()
+            total[...] += column[part][other].astype(f32)
+        for step, to in enumerate(along_z(z)):
+            line_copy(part, step, to).wait_send()
+
+    return start_pair, {
         "pair": stage_pair,
         "first": stage_first,
         "second": stage_second,
-        "line0": functools.partial(stage_line, turn=0),
-        "line1": functools.partial(stage_line, turn=1),
-        "line2": functools.partial(stage_line, turn=2),
         "total": stage_total,
     }
 
@@ -418,18 +380,17 @@
 BACK_START = (("pair", 0),)
 BACK_SLOTS = {
     0: (("pair", 1),),
-    2: (("first", 0), ("pair", 2)),
-    3: (("first", 1),),
-    4: (("pair", 3), ("second", 0), ("line0", 0)),
-    5: (("first", 2), ("second", 1), ("line0", 1), ("line1", 0)),
-    6: (("line1", 1), ("line2", 0)),
-    7: (("first", 3), ("second", 2), ("line0", 2), ("line2", 1), ("total", 0)),
-    8: (("line1", 2), ("total", 1)),
-    9: (("second", 3), ("line0", 3), ("line2", 2)),
-    10: (("line1", 3), ("total", 2)),
-    11: (("line2", 3),),
+    1: (("first", 0),),
+    2: (("pair", 2),),
+    3: (("first", 1), ("second", 0)),
+    4: (("pair", 3),),
+    5: (("first", 2), ("second", 1), ("total", 0)),
+    6: (("pair", 4),),
+    7: (("first", 3), ("second", 2), ("total", 1)),
+    9: (("first", 4), ("second", 3), ("total", 2)),
+    11: (("second", 4), ("total", 3)),
 }
-BACK_END = (("total", 3),)
+BACK_END = (("total", 4),)
 
 
 def run_all(stages, steps):
@@ -438,17 +399,28 @@
 
 
 def attend_back_sums_kernel(count, chunks, *refs):
-    inputs, grads = refs[:4], refs[4 : 4 + count]
+    inputs, grads = list(refs[:4]), refs[4 : 4 + count]
     outputs, totals = refs[4 + count : 6 + count], refs[6 + count : 6 + 2 * count]
     work, rest = refs[6 + 2 * count : 8 + 2 * count], refs[8 + 2 * count :]
+    probs_ref, load_sem, *rest = rest
+    probs_in, inputs[2] = inputs[2], probs_ref
     groups, heads = inputs[0].shape[0], work[0].shape[0]
+
+    def load(group):
+        part = pl.ds(group * heads, heads)
+        return pltpu.make_async_copy(probs_in.at[part], probs_ref.at[part], load_sem.at[group])
+
+    for group in range(groups):
+        load(group).start()
     spot = place()
     greet(*spot, True)
-    start, stages = sum_stages(spot, grads, totals, chunks, rest)
-    start()
+    start_pair, stages = sum_stages(spot, grads, totals, chunks, rest)
+    for chunk in range(2):
+        start_pair(chunk)
     run_all(stages, BACK_START)
 
     def step(group, carry):
+        load(group).wait()
         for head in range(heads):
             attend_back_head(group, head, *inputs, *outputs, *work)
             for slot, steps in BACK_SLOTS.items():
@@ -469,7 +441,7 @@
     chunks = chunked(sizes)
     return pl.pallas_call(
         functools.partial(attend_back_sums_kernel, len(grads), chunks),
-        in_specs=[IN_VMEM] * 4 + [ANYWHERE] * len(grads),
+        in_specs=[IN_VMEM, IN_VMEM, ANYWHERE, IN_VMEM] + [ANYWHERE] * len(grads),
         out_specs=[IN_VMEM] * (2 + len(grads)),
         out_shape=[
             jax.ShapeDtypeStruct((groups, seq, width3), low),
@@ -479,6 +451,8 @@
         scratch_shapes=[
             pltpu.VMEM((heads, seq, seq), low),
             pltpu.VMEM((2 * heads, HEAD_DIM, 2 * seq), f32),
+            pltpu.VMEM(probs.shape, low),
+            pltpu.SemaphoreType.DMA((groups,)),
         ]
         + sum_scratch(part, [chunk[2] for chunk in chunks]),
         compiler_params=pltpu.CompilerParams(
@@ -713,165 +687,120 @@
     return start, forward, relay, finish
 
 
-def return_sums_kernel(chunks, words_ref, grads_ref, sent_ref, total_ref, *refs):
-    spot = place()
-    z, x, y, c = spot
-    meet_owners(*spot)
-    greet(*spot, False)
-    pl.semaphore_wait(pltpu.get_barrier_semaphore(), 9)
-    start_words, forward, relay, finish = return_stages(spot, words_ref, sent_ref, refs[:5])
-    start_sums, stages = sum_stages(spot, [grads_ref], [total_ref], chunks, refs[5:])
-    start_words()
-    start_sums()
-    forward(0, 1)
-    run_all(stages, (("pair", 0), ("pair", 1)))
-    forward(1, 8)
-    run_all(stages, (("first", 0),))
-    relay(0, 4)
-    run_all(stages, (("first", 1), ("second", 0), ("line0", 0)))
-    relay(4, 8)
-    run_all(stages, (("second", 1), ("line0", 1)))
-    for turn in ("line1", "line2", "total"):
-        run_all(stages, ((turn, 0), (turn, 1)))
-    finish()
-
-
-def return_sums(words, grads, tag):
-    piece = words.shape[1:]
-    size = grads.shape[2]
-    part = grads.shape[1] // 8
-    chunks = chunked([size])
-    return pl.pallas_call(
-        functools.partial(return_sums_kernel, chunks),
-        in_specs=[IN_VMEM, ANYWHERE],
-        out_specs=[IN_VMEM] * 2,
-        out_shape=[
-            jax.ShapeDtypeStruct((8, 4) + piece, low),
-            jax.ShapeDtypeStruct((part, size), f32),
-        ],
-        scratch_shapes=[
-            pltpu.SemaphoreType.DMA,
-            pltpu.SemaphoreType.DMA((7,)),
-            pltpu.SemaphoreType.DMA((8,)),
-            pltpu.SemaphoreType.DMA((3, 8)),
-            pltpu.SemaphoreType.DMA((4, 8)),
-        ]
-        + sum_scratch(part, [chunk[2] for chunk in chunks]),
-        compiler_params=pltpu.CompilerParams(
-            collective_id=tag, has_side_effects=True, vmem_limit_bytes=48 << 20
-        ),
-        name="return_sums",
-    )(words, grads.reshape(4, 4, 2, part, size))
-
-
-def gather_stages(spot, pack_ref, all_ref, local_sem, send_sem, recv_sem):
+def return_scratch():
+    return [
+        pltpu.SemaphoreType.DMA,
+        pltpu.SemaphoreType.DMA((7,)),
+        pltpu.SemaphoreType.DMA((8,)),
+        pltpu.SemaphoreType.DMA((3, 8)),
+        pltpu.SemaphoreType.DMA((4, 8)),
+    ]
+
+
+def gather_stages(spot, pack_ref, all_ref, local_sem, send_sem, recv_sem, line_sem, core_sem):
     z, x, y, c = spot
     half = pack_ref.shape[0] // 2
     core_to, y_to, x_to = device(z, x, y, 1 - c), device(z, x, 1 - y, c), device(z, 1 - x, y, c)
     up_to, down_to = device(z + 1, x, y, c), device(z - 1, x, y, c)
     keep = pltpu.make_async_copy(pack_ref, all_ref.at[y * 2 + c, z * 2 + x], local_sem)
-    UP, DOWN, CROSS, SIDE, CORE = range(5)
-    targets = (up_to, down_to, x_to, y_to, core_to)
-
-    def copy(kind, part, zz, xx, yy, column=c):
+    CROSS, SIDE, UP, DOWN = range(4)
+    targets = (x_to, y_to, up_to, down_to)
+
+    def copy(kind, part, zz, xx, yy):
+        at = lax.clamp(0, zz, 3) * 2 + xx
+        block = all_ref.at[yy * 2 + c, at, pl.ds(part * half, half)]
+        return remote(
+            block, block, send_sem.at[kind, part, yy, at], recv_sem.at[part, yy, at], targets[kind]
+        )
+
+    def line_copy(kind, zz):
         zz = lax.clamp(0, zz, 3)
-        block = all_ref.at[yy * 2 + column, zz * 2 + xx, pl.ds(part * half, half)]
-        return remote(
-            block,
-            block,
-            send_sem.at[kind, part, yy, zz * 2 + xx],
-            recv_sem.at[column, part, yy, zz * 2 + xx],
-            targets[kind],
-        )
+        block = all_ref.at[y * 2 + c, zz * 2 + x]
+        return remote(block, block, line_sem.at[kind - UP, zz], line_sem.at[2, zz], targets[kind])
+
+    def core_copy(zz, yy, column):
+        zz = lax.clamp(0, zz, 3)
+        block = all_ref.at[yy * 2 + column, pl.ds(zz * 2, 2)]
+        return remote(block, block, core_sem.at[0, yy, zz], core_sem.at[1, yy, zz], core_to)
 
     def distances(far):
         if far == 0:
             return [(z, z >= 0, None)]
         return [(z - far, z >= far, UP), (z + far, z <= 3 - far, DOWN)]
 
-    def spread_block(zz):
-        for part in range(2):
-            copy(CROSS if part == 0 else SIDE, part, zz, x, y).start()
-        for part in range(2):
-            copy(SIDE if part == 0 else CROSS, part, zz, x, y).start()
-            copy(CORE, part, zz, x, y).start()
-
-    def along(zz, way):
+    def along(way):
         if way is None:
             return [(UP, z < 3), (DOWN, z > 0)]
         return [(way, z < 3 if way == UP else z > 0)]
 
-    def line(far):
+    def for_each(far, action):
         for zz, exists, way in distances(far):
-
-            @pl.when(exists)
-            def arrived():
-                if way is None:
-                    keep.wait()
-                else:
-                    for part in range(2):
-                        copy(way, part, zz, x, y).wait_recv()
-                for on, possible in along(zz, way):
-
-                    @pl.when(possible)
-                    def onward():
-                        for part in range(2):
-                            copy(on, part, zz, x, y).start()
-
-                spread_block(zz)
-
-    def sides(far):
-        for zz, exists, way in distances(far):
-
-            @pl.when(exists)
-            def arrived():
-                copy(CROSS, 0, zz, 1 - x, y).wait_recv()
-                copy(SIDE, 0, zz, 1 - x, y).start()
-                copy(CORE, 0, zz, 1 - x, y).start()
-                copy(SIDE, 1, zz, x, 1 - y).wait_recv()
-                copy(CROSS, 1, zz, x, 1 - y).start()
-                copy(CORE, 1, zz, x, 1 - y).start()
-
-    def corners(far):
-        for zz, exists, way in distances(far):
-
-            @pl.when(exists)
-            def arrived():
-                for part, xx, yy in ((0, x, 1 - y), (1, 1 - x, y), (0, 1 - x, 1 - y), (1, 1 - x, 1 - y)):
-                    copy(CORE, part, zz, xx, yy).wait_recv()
-                    copy(CORE, part, zz, xx, yy).start()
-
-    def finish():
-        for far in range(4):
-            for zz, exists, way in distances(far):
-
-                @pl.when(exists)
-                def drained():
-                    for on, possible in along(zz, way):
-
-                        @pl.when(possible)
-                        def onward():
-                            for part in range(2):
-                                copy(on, part, zz, x, y).wait_send()
-
-                    for part in range(2):
-                        copy(CROSS, part, zz, x, y).wait_send()
-                        copy(SIDE, part, zz, x, y).wait_send()
-                        for xx in range(2):
-                            for yy in range(2):
-                                copy(CORE, part, zz, xx, yy).wait_send()
-                                copy(CORE, part, zz, xx, yy, 1 - c).wait_recv()
-                    copy(SIDE, 0, zz, 1 - x, y).wait_send()
-                    copy(CROSS, 1, zz, x, 1 - y).wait_send()
-
-    return keep.start, {"line": line, "sides": sides, "corners": corners, "finish": lambda far: finish()}
+            pl.when(exists)(functools.partial(action, zz, way))
+
+    def onward(zz, way, action):
+        for on, possible in along(way):
+            pl.when(possible)(lambda on=on: action(line_copy(on, zz)))
+
+    def line_one(zz, way):
+        if way is None:
+            keep.wait()
+        else:
+            line_copy(way, zz).wait_recv()
+        onward(zz, way, lambda copy: copy.start())
+        copy(CROSS, 0, zz, x, y).start()
+        copy(SIDE, 1, zz, x, y).start()
+
+    def rest_one(zz, way):
+        copy(SIDE, 0, zz, x, y).start()
+        copy(CROSS, 1, zz, x, y).start()
+
+    def sides_one(zz, way):
+        copy(CROSS, 0, zz, 1 - x, y).wait_recv()
+        copy(SIDE, 0, zz, 1 - x, y).start()
+        copy(SIDE, 1, zz, x, 1 - y).wait_recv()
+        copy(CROSS, 1, zz, x, 1 - y).start()
+
+    def corners_one(zz, way):
+        for kind, part, xx, yy in (
+            (SIDE, 0, x, 1 - y),
+            (CROSS, 1, 1 - x, y),
+            (SIDE, 0, 1 - x, 1 - y),
+            (CROSS, 1, 1 - x, 1 - y),
+        ):
+            copy(kind, part, zz, xx, yy).wait_recv()
+        for yy in range(2):
+            core_copy(zz, yy, c).start()
+
+    def finish_one(zz, way):
+        onward(zz, way, lambda copy: copy.wait_send())
+        for part in range(2):
+            copy(CROSS, part, zz, x, y).wait_send()
+            copy(SIDE, part, zz, x, y).wait_send()
+        copy(SIDE, 0, zz, 1 - x, y).wait_send()
+        copy(CROSS, 1, zz, x, 1 - y).wait_send()
+        for yy in range(2):
+            core_copy(zz, yy, c).wait_send()
+            core_copy(zz, yy, 1 - c).wait_recv()
+
+    steps = {
+        "line": line_one,
+        "rest": rest_one,
+        "sides": sides_one,
+        "corners": corners_one,
+        "finish": finish_one,
+    }
+    return keep.start, {
+        name: functools.partial(for_each, action=action) for name, action in steps.items()
+    }
 
 
 def gather_scratch():
     return [
         pltpu.SemaphoreType.DMA,
-        pltpu.SemaphoreType.DMA((5, 2, 2, 8)),
-        pltpu.SemaphoreType.DMA((2, 2, 2, 8)),
+        pltpu.SemaphoreType.DMA((4, 2, 2, 8)),
+        pltpu.SemaphoreType.DMA((2, 2, 8)),
+        pltpu.SemaphoreType.DMA((3, 4)),
+        pltpu.SemaphoreType.DMA((2, 2, 4)),
     ]
 
 
@@ -1187,18 +1116,34 @@
 
 
 GATHER_SLOTS = {
-    1: (("line", 2),),
-    4: (("line", 3), ("sides", 1)),
-    8: (("sides", 2),),
-    9: (("sides", 3), ("corners", 0)),
-    11: (("corners", 1),),
+    1: (("line", 2), ("rest", 1)),
+    3: (("sides", 1),),
+    5: (("line", 3), ("rest", 2)),
+    6: (("sides", 2),),
+    8: (("rest", 3), ("sides", 3), ("corners", 0)),
+    10: (("corners", 1),),
 }
-GATHER_END = (("corners", 2), ("corners", 3), ("finish", 0))
+GATHER_END = (
+    ("corners", 2),
+    ("corners", 3),
+    ("finish", 0),
+    ("finish", 1),
+    ("finish", 2),
+    ("finish", 3),
+)
+
+
+SAVED = (1, 3, 4, 6)
 
 
 def attend_gather_kernel(length_ref, weights_ref, words_ref, pack_ref, *refs):
-    outputs, probs_ref, mixed_ref, all_ref = refs[:7], refs[7], refs[8], refs[9]
-    low_ref, rel_ref, far_ref, *sems = refs[10:]
+    outputs, probs_out, mixed_ref, all_ref = list(refs[:7]), refs[7], refs[8], refs[9]
+    low_ref, rel_ref, far_ref, probs_ref, *kept, save_sem = refs[10:19]
+    sems = refs[19:]
+    saves = []
+    for order, index in enumerate(SAVED):
+        saves.append(pltpu.make_async_copy(kept[order], outputs[index], save_sem.at[order]))
+        outputs[index] = kept[order]
     qkv_ref, table_ref = outputs[3], outputs[6]
     groups, heads = qkv_ref.shape[0], far_ref.shape[0]
     spot = place()
@@ -1208,9 +1153,18 @@
     run_all(steps, (("line", 0),))
 
     def between(group):
+        pl.when(group == 0)(lambda: run_all(steps, (("rest", 0),)))
         pl.when(group == 2)(lambda: run_all(steps, (("line", 1), ("sides", 0))))
 
     prepare_kernel(weights_ref, words_ref, *outputs, low_ref, rel_ref, between=between)
+    for copy in saves:
+        copy.start()
+
+    def save_probs(group):
+        part = pl.ds(group * heads, heads)
+        return pltpu.make_async_copy(
+            probs_ref.at[part], probs_out.at[part], save_sem.at[len(SAVED) + group]
+        )
 
     def step(group, carry):
         for head in range(heads):
@@ -1218,10 +1172,15 @@
             for slot, timed in GATHER_SLOTS.items():
                 if slot % heads == head:
                     pl.when(group == slot // heads)(functools.partial(run_all, steps, timed))
+        save_probs(group).start()
         return carry
 
     lax.fori_loop(0, groups, step, 0)
     run_all(steps, GATHER_END)
+    for copy in saves:
+        copy.wait()
+    for group in range(groups):
+        save_probs(group).wait()
 
 
 def attend_gather(length, weights, words, pack, width, entries, tag):
@@ -1232,14 +1191,19 @@
     return pl.pallas_call(
         attend_gather_kernel,
         in_specs=[pl.BlockSpec(memory_space=pltpu.SMEM), IN_VMEM, IN_VMEM, ANYWHERE],
-        out_specs=[IN_VMEM] * 9 + [ANYWHERE],
+        out_specs=[ANYWHERE if index in SAVED else IN_VMEM for index in range(7)]
+        + [ANYWHERE, IN_VMEM, ANYWHERE],
         out_shape=outputs
         + [
             jax.ShapeDtypeStruct((groups * heads, seq, seq), low),
             jax.ShapeDtypeStruct((groups, seq, width), low),
             jax.ShapeDtypeStruct((4, 8) + pack.shape, low),
         ],
-        scratch_shapes=scratch + [pltpu.VMEM((heads, seq, seq), f32)] + gather_scratch(),
+        scratch_shapes=scratch
+        + [pltpu.VMEM((heads, seq, seq), f32), pltpu.VMEM((groups * heads, seq, seq), low)]
+        + [pltpu.VMEM(outputs[index].shape, outputs[index].dtype) for index in SAVED]
+        + [pltpu.SemaphoreType.DMA((len(SAVED) + groups,))]
+        + gather_scratch(),
         compiler_params=pltpu.CompilerParams(
             collective_id=tag, has_side_effects=True, vmem_limit_bytes=56 << 20
         ),
@@ -1248,18 +1212,22 @@
 
 
 def middle_kernel(
-    weights_ref,
+    weights_in,
     vec_ref,
     white_ref,
     mixed_ref,
     marks_ref,
-    contract_out,
-    expand_out,
+    contract_save,
+    expand_save,
     joint_out,
     mixed_out,
     sum_out,
     vec_out,
     loss_out,
+    weights_ref,
+    contract_out,
+    expand_out,
+    copy_sem,
     combine_ref,
     readout_ref,
     slope_ref,
@@ -1273,6 +1241,33 @@
     seq = white_ref.shape[0]
     width = mixed_ref.shape[2]
     hidden = acts_ref.shape[2]
+
+    def load(group, first, last, sem):
+        part = (group, slice(None), pl.ds(first, last - first))
+        return pltpu.make_async_copy(weights_in.at[part], weights_ref.at[part], copy_sem.at[sem])
+
+    def load_joint(group):
+        return load(group, 2 * hidden, 2 * hidden + 2 * width, group)
+
+    def load_group(group):
+        return load(group, 0, 2 * hidden, groups + group)
+
+    def save(group):
+        return (
+            pltpu.make_async_copy(
+                contract_out.at[group], contract_save.at[group], copy_sem.at[2 * groups + group]
+            ),
+            pltpu.make_async_copy(
+                expand_out.at[group], expand_save.at[group], copy_sem.at[3 * groups + group]
+            ),
+        )
+
+    for group in range(groups):
+        load_joint(group).start()
+    for group in range(groups):
+        load_group(group).start()
+    for group in range(groups):
+        load_joint(group).wait()
     vec = [vec_ref[row : row + 1] for row in range(11)]
     for group in range(groups):
         joint = weights_ref[group, :, 2 * hidden :]
@@ -1288,6 +1283,7 @@
     mid_ref[...] = hidden_mid.astype(low)
 
     def forward(group, carry):
+        load_group(group).wait()
         gate = dot_plain(mid_ref[...], weights_ref[group, :, :hidden])
         share = 0.5 + 0.5 * lax.erf(gate * 0.5**0.5)
         acts_ref[group] = (gate * share).astype(low)
@@ -1332,6 +1328,8 @@
         ).astype(low)
         expand_out[group] = dot_plain(mid_turned, acts_ref[group]).astype(low)
         sum_out[...] += dot_rows(acts_ref[group], weights_ref[group, :, :hidden])
+        for copy in save(group):
+            copy.start()
         return carry
 
     lax.fori_loop(0, groups, backward, 0)
@@ -1345,6 +1343,9 @@
     for group in range(groups):
         mixed_out[group] = dot_plain(gate_ref[...], combine_ref[group]).astype(low)
         joint_out[group, :, width:] = dot_plain(turned, mixed_ref[group]).astype(low)
+    for group in range(groups):
+        for copy in save(group):
+            copy.wait()
 
 
 def middle(weights, vec, white, mixed, marks):
@@ -1363,25 +1364,14 @@
     ]
     return pl.pallas_call(
         middle_kernel,
-        grid=(1,),
-        in_specs=[
-            pl.BlockSpec(
-                array.shape,
-                functools.partial(lambda rank, step: (0,) * rank, array.ndim),
-                pipeline_mode=pl.Buffered(1),
-            )
-            for array in (weights, vec, white, mixed, marks)
-        ],
-        out_specs=[
-            pl.BlockSpec(
-                shape,
-                functools.partial(lambda rank, step: (0,) * rank, len(shape)),
-                pipeline_mode=pl.Buffered(1),
-            )
-            for shape, _ in outputs
-        ],
+        in_specs=[ANYWHERE] + [IN_VMEM] * 4,
+        out_specs=[ANYWHERE] * 2 + [IN_VMEM] * 5,
         out_shape=[jax.ShapeDtypeStruct(*output) for output in outputs],
         scratch_shapes=[
+            pltpu.VMEM(weights.shape, low),
+            pltpu.VMEM((groups, model, hidden), low),
+            pltpu.VMEM((groups, model, hidden), low),
+            pltpu.SemaphoreType.DMA((4 * groups,)),
             pltpu.VMEM((groups, model, width), low),
             pltpu.VMEM((model, model), low),
             pltpu.VMEM((groups, seq, hidden), f32),
@@ -1419,38 +1409,45 @@
     entries = rel_white_ref.shape[0]
     part = entries // groups
     vec = [vec_ref[row : row + 1] for row in range(4)]
+
+    def put(group, first, last, values):
+        values = values.astype(low).reshape(project_out.shape[1:-1] + (last - first,))
+        project_out[group, ..., first:last] = values
+
+    total_ref[...] = sum_ref[...]
+    for group in range(groups):
+        total_ref[...] += dot_rows(grads_ref[group], weights_ref[group, :, : 3 * width])
+    upstream, gain_grad, bias_grad = unwhiten(total_ref[...], vec[0], white_ref[...], rate_ref[...])
+    turned = upstream.T.astype(low)
+    words_out[...] = turned.reshape(words_out.shape)
+    between("words")
     turned = (white_ref[...] * vec[0] + vec[1]).T.astype(low)
     rel_turned = (rel_white_ref[...] * vec[2] + vec[3]).T.astype(low)
     chosen = selection(seq, entries)
-    total_ref[...] = sum_ref[...]
-    between(-1)
     rel_total = jnp.zeros((entries, model), f32)
     for group in range(groups):
         fold_ref[...] = dot_left(chosen, tables_ref[group]).astype(low)
-        total_ref[...] += dot_rows(grads_ref[group], weights_ref[group, :, : 3 * width])
         rel_total += dot_rows(fold_ref[...], weights_ref[group, :, : 2 * width])
-        project_out[group, :, : 2 * width] = (
-            dot_plain(turned, grads_ref[group, :, : 2 * width]) + dot_plain(rel_turned, fold_ref[...])
-        ).astype(low)
-        project_out[group, :, 2 * width : 3 * width] = dot_plain(
-            turned, grads_ref[group, :, 2 * width :]
-        ).astype(low)
+        put(
+            group,
+            0,
+            2 * width,
+            dot_plain(turned, grads_ref[group, :, : 2 * width]) + dot_plain(rel_turned, fold_ref[...]),
+        )
+        put(group, 2 * width, 3 * width, dot_plain(turned, grads_ref[group, :, 2 * width :]))
         between(group)
-    upstream, gain_grad, bias_grad = unwhiten(total_ref[...], vec[0], white_ref[...], rate_ref[...])
-    words_out[...] = upstream.T.astype(low)
-    between(groups)
     rel_up, rel_gain_grad, rel_bias_grad = unwhiten(
         rel_total, vec[2], rel_white_ref[...], rel_rate_ref[...]
     )
     turned = rel_up.T.astype(low)
-    for group in range(groups):
-        project_out[group, :, 3 * width + BLOCK // 2 :] = turned[:, group * part : (group + 1) * part]
     rows = [gain_grad, bias_grad, rel_gain_grad, rel_bias_grad]
     rows += [vec_grads_ref[row : row + 1] for row in range(7)]
     rows += [jnp.zeros((1, model), f32)]
+    middle_column = 3 * width + BLOCK // 2
     for group in range(groups):
+        put(group, middle_column, middle_column + part, turned[:, group * part : (group + 1) * part])
         three = jnp.concatenate(rows[3 * group : 3 * group + 3] + [jnp.zeros((BLOCK - 3, model), f32)], 0)
-        project_out[group, :, 3 * width : 3 * width + BLOCK // 2] = three.T.astype(low)[:, : BLOCK // 2]
+        put(group, 3 * width, middle_column, three.T[:, : BLOCK // 2])
 
 
 def projected_back(weights, white, grads, rel_white):
@@ -1478,49 +1475,67 @@
     )(weights, vec, white, rate, rel_white, rel_rate, total, grads, tables, vec_grads)
 
 
-PROJECT_STEPS = {
-    -1: ("pair",),
-    1: ("first",),
-    2: ("second", "line0"),
-    3: ("line1",),
-    4: ("line2",),
-}
-
-
-def project_back_sums_kernel(count, chunks, *refs):
-    inputs, grads = refs[:10], refs[10 : 10 + count]
-    outputs, totals = refs[10 + count : 12 + count], refs[12 + count : 12 + 2 * count]
-    work, rest = refs[12 + 2 * count : 14 + 2 * count], refs[14 + 2 * count :]
+def project_return_kernel(chunks, *refs):
+    inputs, (sent_ref, total_ref) = refs[:10], refs[10:12]
+    words_ref, project_ref, *work = refs[12:16]
     spot = place()
-    greet(*spot, True)
-    start, stages = sum_stages(spot, grads, totals, chunks, rest)
-    start()
+    meet_owners(*spot)
+    greet(*spot, False)
+    pl.semaphore_wait(pltpu.get_barrier_semaphore(), 9)
+    start_words, forward, relay, finish = return_stages(spot, words_ref, sent_ref, refs[16:21])
+    start_sums, stages = sum_stages(spot, [project_ref], [total_ref], chunks, refs[21:])
+    start_pair = start_sums
 
     def between(point):
-        for name in PROJECT_STEPS.get(point, ()):
-            run_all(stages, [(name, chunk) for chunk in range(len(chunks))])
-
-    project_back_kernel(*inputs, *outputs, *work, between=between)
-    run_all(stages, [("total", chunk) for chunk in range(len(chunks))])
-
-
-def project_back_sums(*inputs, grads, tag):
+        if point == "words":
+            start_words()
+        elif point == 1:
+            forward(0, 2)
+        elif point == 2:
+            forward(2, 4)
+        elif point == 3:
+            start_pair(0)
+            forward(4, 6)
+
+    project_back_kernel(*inputs, words_ref, project_ref, *work, between=between)
+    start_pair(1)
+    run_all(stages, (("pair", 0),))
+    forward(6, 8)
+    run_all(stages, (("pair", 1),))
+    relay(0, 4)
+    run_all(stages, (("first", 0), ("first", 1)))
+    relay(4, 8)
+    run_all(stages, (("second", 0), ("second", 1), ("total", 0), ("total", 1)))
+    finish()
+
+
+def project_return(*inputs, tag):
     weights, white, rel_white, upstream = inputs[0], inputs[2], inputs[4], inputs[7]
-    outputs, scratch = projected_back(weights, white, upstream, rel_white)
-    part = grads[0].shape[1] // 8
-    sizes = [grad.shape[2] for grad in grads]
-    chunks = chunked(sizes)
+    (words, project), scratch = projected_back(weights, white, upstream, rel_white)
+    seq = words.shape[1]
+    size = project.shape[2]
+    part = words.shape[0] // 8
+    chunks = chunked([size])
     return pl.pallas_call(
-        functools.partial(project_back_sums_kernel, len(grads), chunks),
-        in_specs=[IN_VMEM] * 10 + [ANYWHERE] * len(grads),
-        out_specs=[IN_VMEM] * (2 + len(grads)),
-        out_shape=outputs + [jax.ShapeDtypeStruct((part, size), f32) for size in sizes],
-        scratch_shapes=scratch + sum_scratch(part, [chunk[2] for chunk in chunks]),
+        functools.partial(project_return_kernel, chunks),
+        in_specs=[IN_VMEM] * 10,
+        out_specs=[IN_VMEM] * 2,
+        out_shape=[
+            jax.ShapeDtypeStruct((8, 4, part, seq), low),
+            jax.ShapeDtypeStruct((part, size), f32),
+        ],
+        scratch_shapes=[
+            pltpu.VMEM((8, part, seq), low),
+            pltpu.VMEM((4, 4, 2, part, size), low),
+        ]
+        + scratch
+        + return_scratch()
+        + sum_scratch(part, [chunk[2] for chunk in chunks]),
         compiler_params=pltpu.CompilerParams(
-            collective_id=tag, has_side_effects=True, vmem_limit_bytes=56 << 20
+            collective_id=tag, has_side_effects=True, vmem_limit_bytes=60 << 20
         ),
-        name="project_back_sums",
-    )(*inputs, *[grad.reshape(4, 4, 2, part, -1) for grad in grads])
+        name="project_return",
+    )(*inputs)
 
 
 def split_terms(values, count):
@@ -1561,21 +1576,14 @@
     everything = slice(None)
     update(0, (everything, everything), grads[0][...])
 
-    @pl.when(pl.program_id(0) == 0)
-    def small():
-        contract, expand, joint, project = grads[1:]
+    contract, expand, joint, project = grads[1:]
+
+    def at_step(step):
+        return pl.when(pl.program_id(0) == step)
+
+    @at_step(0)
+    def norms():
         factor_ref[...] = jnp.broadcast_to(jnp.sqrt(squares), factor_ref.shape)
-        for group in range(4):
-            part = slice(group * BLOCK, (group + 1) * BLOCK)
-            update(1, (everything, part), shared_ref[group, :, width + BLOCK // 2 :])
-            part = slice(group * width, (group + 1) * width)
-            update(6, (everything, part), shared_ref[group, :, :width])
-        for kind in range(3):
-            part = slice(kind * width, (kind + 1) * width)
-            update(2, (kind,), project[:, part])
-        update(3, (everything, everything), joint[:, width:].T)
-        update(4, (everything, everything), expand[...])
-        update(5, (everything, everything), contract[...])
         count = weights[21].shape[0]
         for group in range(4):
             rows = shared_ref[group, :, BLOCK : 2 * BLOCK].T[BLOCK // 2 :]
@@ -1584,6 +1592,35 @@
             update(7, (slice(first, last), everything), rows[: last - first])
             if group == 1:
                 bias_ref[...] = rows[0:1] * factor
+
+    @at_step(1)
+    def relative_table():
+        for group in range(4):
+            part = slice(group * BLOCK, (group + 1) * BLOCK)
+            update(1, (everything, part), shared_ref[group, :, width + BLOCK // 2 :])
+
+    @at_step(2)
+    def readout_weights():
+        for group in range(4):
+            part = slice(group * width, (group + 1) * width)
+            update(6, (everything, part), shared_ref[group, :, :width])
+
+    @at_step(3)
+    def project_weights():
+        for kind in range(3):
+            update(2, (kind,), project[:, kind * width : (kind + 1) * width])
+
+    @at_step(4)
+    def combine_weights():
+        update(3, (everything, everything), joint[:, width:].T)
+
+    @at_step(5)
+    def expand_weights():
+        update(4, (everything, everything), expand[...])
+
+    @at_step(6)
+    def contract_weights():
+        update(5, (everything, everything), contract[...])
 
 
 def update_all(facts, shared, grads, weights, width):
@@ -1730,20 +1767,14 @@
     back = (first_all, vec_full, white, rate, rel_white, rel_rate, grad_sum)
     if direct:
         qkv_grads, rel_table_grads, *sums = attend_back_sums(
-            qkv, rel_table, probs, grad_mixed, [grad_contract, grad_expand], 4
-        )
-        sent, grad_project, joint_sum = project_back_sums(
-            *back, qkv_grads, rel_table_grads, grad_vec, grads=[grad_joint], tag=7
-        )
-        sums.append(joint_sum)
+            qkv, rel_table, probs, grad_mixed, [grad_contract, grad_expand, grad_joint], 4
+        )
+        sent, project_sum = project_return(*back, qkv_grads, rel_table_grads, grad_vec, tag=5)
+        sums.append(project_sum)
     else:
         qkv_grads, rel_table_grads = attend_back(qkv, rel_table, probs, grad_mixed)
         sent, grad_project = project_back(*back, qkv_grads, rel_table_grads, grad_vec)
-    sent = sent.reshape(owners, width, seq_len)
-    if direct:
-        sent, late_sum = return_sums(sent, grad_project, 5)
-        sums.append(late_sum)
-    else:
+        sent = sent.reshape(owners, width, seq_len)
         sent = lax.all_to_all(sent, "dp", 0, 0, tiled=True)
         sent = lax.all_gather(sent, "heads", axis=0)
         sent = sent.transpose(1, 0, 2, 3)

time: 448 us -> 421 us (0.940)
  Pallas kernels: 396 us -> 371 us
    pallas_call x3 -> x2, Pallas kernels: 129 us -> 105 us  [the longest x1 70.9 us: project_return(): pl.pallas_call(functools.partial(project_return_kernel, chunks), in_specs...]
  transfers between devices with their start and end apart: 1 -> 1, of which waited for: 1 -> 1; matrix products, arithmetic and copies ran while one was open for 4% -> 4% of each run, Pallas kernels for 14% -> 15%
where the time goes in v5:
time: 421 us; the launch traced here: 414 us
  Pallas kernels  371 us (88%)
  between operations  16.6 us (4%)
  other arithmetic  13.5 us (3%)
  local copies, waits for them, and re-layouts  9.32 us (2%)
    pallas_call x1, Pallas kernels, attend_back_sums(): pl.pallas_call(functools.partial(attend_back_sums_kernel, len(grads), chu...  80 us
    pallas_call x1, Pallas kernels, attend_gather(): pl.pallas_call(attend_gather_kernel, in_specs=[pl.BlockSpec(memory_space=...  77 us
    pallas_call x1, Pallas kernels, project_return(): pl.pallas_call(functools.partial(project_return_kernel, chunks), in_specs...  70.9 us
    pallas_call x1, Pallas kernels, exchange_words(): pl.pallas_call(exchange_words_kernel, in_specs=[IN_VMEM], out_specs=IN_VM...  37.9 us
    pallas_call x1, Pallas kernels, middle(): pl.pallas_call(middle_kernel, in_specs=[ANYWHERE] + [IN_VMEM] * 4, out_sp...  34.2 us
    pallas_call x1, Pallas kernels, update_all(): pl.pallas_call(functools.partial(update_kernel, width), grid=(slab // col...  20.9 us
    pallas_call x1, Pallas kernels, finish_sums(): pl.pallas_call(functools.partial(finish_sums_kernel, width), in_specs=[IN...  13.9 us
    pallas_call x1, Pallas kernels, deposit(): pl.pallas_call(deposit_kernel, grid=(steps,), in_specs=[pl.BlockSpec(memo...  13.8 us
  transfers between devices with their start and end apart: 1, of which 1 were waited for; matrix products, arithmetic and copies ran while one was open for 4% of the time, Pallas kernels for 15%

profile of v5, /device:TPU:0, one launch (start us, length us, event | category | flops | bytes accessed | tf_op | source)
XLA Modules:
  0.0 413.6 jit_solution(17569012830503991375)
XLA Ops:
  7.2 0.0 all-gather.2.cloned.1.call-start
  7.3 0.7 fusion.6
  8.0 0.8 constant_dynamic-slice_fusion
  8.8 0.1 copy.76
  8.9 1.0 convert_element_type.60
  9.8 0.2 copy.68
  10.1 0.8 copy.70
  10.9 0.0 all-gather.2.cloned.1.call-update
  11.0 1.0 copy.73
  12.0 1.2 dynamic_slice.12.length_ref
  13.2 1.3 pad_add_fusion.facts_ref
  14.5 10.9 %share_facts.1 = s32[8,8,512]{2,1,0:T(8,128)} custom-call(s32[8,512]{1,0:T(8,128)} %pad_add_fusion.facts_ref), custom_call_target="tpu_custom_call" | custom-call | tf_op jit(solution)/shard_map/share_facts/pallas_call | solution.py:505
  25.5 1.4 slice_reduce_fusion
  27.5 0.1 lt.83
  27.6 1.2 convert_reduce_fusion
  28.8 0.1 reduce_sum.26
  28.9 0.1 reduce_sum.27.counts_ref
  29.0 0.0 copy-start.2
  29.1 0.1 broadcast_bitcast_fusion
  29.2 0.1 sub.26
  29.3 0.1 select_bitcast_fusion
  29.3 5.2 %sort.7 = s32[4096,4]{0,1:T(4,128)S(1)} sort(s32[4096,4]{0,1:T(4,128)S(1)} %select_bitcast_fusion), dimensions={0}, to_apply=%region_2.3 | sort | flops 229376 | bytes 131072 | tf_op jit(solution)/shard_map/sort | solution.py:1738
  34.6 0.0 copy-start.1
  34.6 1.0 convert_element_type.68
  35.6 0.7 convert_bitcast_fusion.1
  36.4 0.6 compare_select_fusion
  37.0 0.9 copy.74.marks_ref
  37.9 0.0 copy-start.3
  37.9 11.2 %lookup.1 = bf16[32,96,512]{2,1,0:T(8,128)(2,1)S(1)} custom-call(s32[4]{0:T(128)S(1)} %reduce_sum.27.counts_ref, s32[4,1,4096]{2,1,0:T(1,128)S(1)} %broadcast_in_dim.27.keys_ref, f32[96,12672]{1,0:T(8,128)} %refs_7_.1), custom_call_target="tpu_custom_call" | custom-call | tf_op jit(solution)/shard_map/lookup/pallas_call | solution.py:940
  49.1 0.0 copy-done.2
  49.1 37.9 %exchange_words.1 = bf16[8,96,512]{2,1,0:T(8,128)(2,1)S(1)} custom-call(bf16[8,4,96,512]{3,2,1,0:T(8,128)(2,1)S(1)} %bitcast.63), custom_call_target="tpu_custom_call" | custom-call | tf_op jit(solution)/shard_map/exchange_words/pallas_call | solution.py:606
  87.0 0.0 copy-done.1
  87.0 0.0 copy-start
  87.0 0.9 copy-done
  87.9 1.0 dynamic-slice_convert_fusion
  88.9 0.0 copy-done.3
  88.9 0.8 concatenate.11.pack_ref
  89.7 3.4 all-gather.2.cloned.1.call-done
  93.2 77.0 %attend_gather.1 = (f32[16,768]{1,0:T(8,128)}, f32[512,768]{1,0:T(8,128)}, f32[512,1]{1,0:T(8,128)}, bf16[4,512,576]{2,1,0:T(8,128)(2,1)}, f32[512,768]{1,0:T(8,...) custom-call(s32[1]{0:T(128)} %dynamic_slice.12.length_ref, ...), custom_call_target="tpu_custom_call" | custom-call | tf_op jit(solution)/shard_map/attend_gather/pallas_call | solution.py:1191
  170.1 34.2 %middle.1 = (bf16[4,768,768]{2,1,0:T(8,128)(2,1)}, bf16[4,768,768]{2,1,0:T(8,128)(2,1)}, bf16[4,768,384]{2,1,0:T(8,128)(2,1)}, bf16[4,512,192]{2,1,0:T(8,128)(2,...) custom-call(bf16[4,768,1920]{2,1,0:T(8,128)(2,1)} %bitcast.67, ...), custom_call_target="tpu_custom_call" | custom-call | tf_op jit(solution)/shard_map/middle/pallas_call | solution.py:1365
  204.4 80.0 %attend_back_sums.1 = (bf16[4,512,576]{2,1,0:T(8,128)(2,1)}, bf16[4,1024,384]{2,1,0:T(8,128)(2,1)}, f32[96,768]{1,0:T(8,128)}, f32[96,768]{1,0:T(8,128)}, f32[96,384]{1,0:T(8,128)}) custom-call(bf16[4,512,576]{2,1,0:T(8,128)(2,1)} %get-tuple-element.91.refs_0_, bf16[4,1024,384]{2,1,0:T(8,128)(2,1)} %get-tuple-element.92.refs_1_, ...), custom_call_target="tpu_custom_call" | custom-call | tf_op jit(solution)/shard_map/attend_back_sums/pallas_call | solution.py:442
  284.4 70.9 %project_return.1 = (bf16[8,4,96,512]{3,2,1,0:T(8,128)(2,1)}, f32[96,768]{1,0:T(8,128)}) custom-call(bf16[4,768,896]{2,1,0:T(8,128)(2,1)} %bitcast.66, f32[16,768]{1,0:T(8,128)} %get-tuple-element.83.vec_ref.refs_1_, f32[512,768]{1,0:T(8,128)} %get-tuple-element.84.white_ref.refs_2_, f32[512,1]{1,0:T(8,128)} %get-tuple-element.87.refs_3_, ...), custom_call_target="tpu_custom_call" | custom-call | tf_op jit(solution)/shard_map/project_return/pallas_call | solution.py:1519
  355.3 13.8 %deposit.1 = (f32[96,12672]{1,0:T(8,128)}, f32[96,128]{1,0:T(8,128)}) custom-call(s32[4]{0:T(128)} %copy-done.2, s32[4,1,4096]{2,1,0:T(1,128)} %copy-done.1, bf16[32,96,512]{2,1,0:T(8,128)(2,1)} %bitcast.70), custom_call_target="tpu_custom_call" | custom-call | tf_op jit(solution)/shard_map/deposit/pallas_call | solution.py:1008
  369.2 13.9 %finish_sums.1 = (f32[8,128]{1,0:T(8,128)}, f32[4,96,384]{2,1,0:T(8,128)}) custom-call(f32[512,1]{1,0:T(8,128)} %get-tuple-element.86.losses_ref, f32[96,128]{1,0:T(8,128)} %get-tuple-element.102.squares_ref, f32[96,768]{1,0:T(8,128)} %get-tuple-element.103.refs_0_.refs_3_, f32[96,768]{1,0:T(8,128)} %get-tuple-element.104.refs_1_.refs_4_, ...), custom_call_target="tpu_custom_call" | custom-call | tf_op jit(solution)/shard_map/finish_sums/pallas_call | solution.py:869
  383.1 1.2 slice.14
  384.3 20.9 %update_all.1 = (f32[96,12672]{1,0:T(8,128)}, f32[96,12672]{1,0:T(8,128)}, f32[96,12672]{1,0:T(8,128)}, f32[96,512]{1,0:T(8,128)}, f32[96,512]{1,0:T(8,128)}, /*...) custom-call(f32[8,128]{1,0:T(8,128)} %get-tuple-element.107.refs_0_,, ...), custom_call_target="tpu_custom_call" | custom-call | tf_op jit(solution)/shard_map/update_all/pallas_call | solution.py:1638
  (14 shorter events, 0.2 us)
Async XLA Ops:
  7.2 86.0 %all-gather.2.cloned.1.call-start = ((), (), s32[]{:S(2)}) async-start(), calls=%async_computation | async-start | bytes 5677056 | tf_op jit(solution)/shard_map/all_gather | solution.py:1717
  29.0 20.0 %copy-start.2 = (s32[4]{0:T(128)}, s32[4]{0:T(128)S(1)}, u32[]{:S(2)}) copy-start(s32[4]{0:T(128)S(1)} %reduce_sum.27.counts_ref) | copy-start | bytes 52
  34.6 52.4 %copy-start.1 = (s32[4,1,4096]{2,1,0:T(1,128)}, s32[4,1,4096]{2,1,0:T(1,128)S(1)}, u32[]{:S(2)}) copy-start(s32[4,1,4096]{2,1,0:T(1,128)S(1)} %broadcast_in_dim.27.keys_ref) | copy-start | bytes 196612
  37.9 51.0 %copy-start.3 = (f32[768,96]{0,1:T(8,128)S(1)}, f32[768,96]{0,1:T(8,128)}, u32[]{:S(2)}) copy-start(f32[768,96]{0,1:T(8,128)} %param.35) | copy-start | bytes 884740
  87.0 0.9 copy-start
Sparse Core Ops, SparseCore 0:
  11.6 81.5 all-gather.1

commit v6 on v5

--- a/solution.py
+++ b/solution.py
@@ -242,7 +242,7 @@
     ]
 
 
-def sum_stages(spot, grads, totals, chunks, refs):
+def sum_stages(spot, grads, totals, chunks, refs, resident=False):
     count = len(chunks)
     pair, own, first_a, first_b, second_a, second_b, column = [
         refs[count * part : count * (part + 1)] for part in range(7)
@@ -308,18 +308,26 @@
     def start_pair(part):
         for side in range(2):
             pair_copy(part, side).start()
-            local(part, side).start()
+            if not resident:
+                local(part, side).start()
 
     def stage_pair(part):
         for side in range(2):
-            local(part, side).wait()
+            if not resident:
+                local(part, side).wait()
             pair_copy(part, side).wait()
         if part + 2 < count:
             start_pair(part + 2)
 
         def step(index, carry):
             side, rest = index // 8, index % 8
-            add(own[part].at[side, rest // 2, rest % 2], pair[part].at[side, rest // 2, rest % 2])
+            spot = (side, rest // 2, rest % 2)
+            kept = own[part].at[spot]
+            if resident:
+                array, first, size = chunks[part]
+                kept = grads[array].at[side * 2 + c, rest // 2, rest % 2, :, pl.ds(first, size)]
+            total = kept[...].astype(f32) + pair[part].at[spot][...].astype(f32)
+            own[part].at[spot][...] = total.astype(low)
             return carry
 
         lax.fori_loop(0, 16, step, 0)
@@ -648,9 +656,10 @@
             grads_ref.at[there], sent_ref.at[there, own], out_sem.at[part], in_sem.at[there], core_to
         )
 
-    def pass_on(slot, row, there, to):
+    def pass_on(slot, row, there, to, source=None):
         block = sent_ref.at[there, row]
-        return remote(block, block, send_sem.at[slot, there], recv_sem.at[row, there], to)
+        source = block if source is None else source
+        return remote(source, block, send_sem.at[slot, there], recv_sem.at[row, there], to)
 
     def start():
         keep.start()
@@ -660,12 +669,12 @@
     def forward(first, last):
         for part in range(first, last):
             there = order[part][0] * 2 + order[part][1]
-            if part == 0:
-                keep.wait()
-            else:
+            source = grads_ref.at[here]
+            if part > 0:
                 in_copy(part - 1, order[part]).wait_recv()
-            pass_on(0, own, there, y_to).start()
-            pass_on(1, own, there, core_to).start()
+                source = None
+            pass_on(0, own, there, y_to, source).start()
+            pass_on(1, own, there, core_to, source).start()
 
     def relay(first, last):
         for part in range(first, last):
@@ -674,6 +683,7 @@
             pass_on(2, other, there, core_to).start()
 
     def finish():
+        keep.wait()
         for part, peer in enumerate(peers(z, x)):
             out_copy(part, peer).wait_send()
         for peer_z, peer_x in order:
@@ -706,17 +716,20 @@
     CROSS, SIDE, UP, DOWN = range(4)
     targets = (x_to, y_to, up_to, down_to)
 
-    def copy(kind, part, zz, xx, yy):
+    def copy(kind, part, zz, xx, yy, own=False):
         at = lax.clamp(0, zz, 3) * 2 + xx
-        block = all_ref.at[yy * 2 + c, at, pl.ds(part * half, half)]
+        rows = pl.ds(part * half, half)
+        block = all_ref.at[yy * 2 + c, at, rows]
+        source = pack_ref.at[rows] if own else block
         return remote(
-            block, block, send_sem.at[kind, part, yy, at], recv_sem.at[part, yy, at], targets[kind]
-        )
-
-    def line_copy(kind, zz):
+            source, block, send_sem.at[kind, part, yy, at], recv_sem.at[part, yy, at], targets[kind]
+        )
+
+    def line_copy(kind, zz, own=False):
         zz = lax.clamp(0, zz, 3)
         block = all_ref.at[y * 2 + c, zz * 2 + x]
-        return remote(block, block, line_sem.at[kind - UP, zz], line_sem.at[2, zz], targets[kind])
+        source = pack_ref if own else block
+        return remote(source, block, line_sem.at[kind - UP, zz], line_sem.at[2, zz], targets[kind])
 
     def core_copy(zz, yy, column):
         zz = lax.clamp(0, zz, 3)
@@ -739,20 +752,20 @@
 
     def onward(zz, way, action):
         for on, possible in along(way):
-            pl.when(possible)(lambda on=on: action(line_copy(on, zz)))
+            pl.when(possible)(lambda on=on: action(line_copy(on, zz, way is None)))
 
     def line_one(zz, way):
-        if way is None:
-            keep.wait()
-        else:
+        own = way is None
+        if not own:
             line_copy(way, zz).wait_recv()
         onward(zz, way, lambda copy: copy.start())
-        copy(CROSS, 0, zz, x, y).start()
-        copy(SIDE, 1, zz, x, y).start()
+        copy(CROSS, 0, zz, x, y, own).start()
+        copy(SIDE, 1, zz, x, y, own).start()
 
     def rest_one(zz, way):
-        copy(SIDE, 0, zz, x, y).start()
-        copy(CROSS, 1, zz, x, y).start()
+        own = way is None
+        copy(SIDE, 0, zz, x, y, own).start()
+        copy(CROSS, 1, zz, x, y, own).start()
 
     def sides_one(zz, way):
         copy(CROSS, 0, zz, 1 - x, y).wait_recv()
@@ -768,6 +781,8 @@
             (CROSS, 1, 1 - x, 1 - y),
         ):
             copy(kind, part, zz, xx, yy).wait_recv()
+        if way is None:
+            keep.wait()
         for yy in range(2):
             core_copy(zz, yy, c).start()
 
@@ -1414,13 +1429,6 @@
         values = values.astype(low).reshape(project_out.shape[1:-1] + (last - first,))
         project_out[group, ..., first:last] = values
 
-    total_ref[...] = sum_ref[...]
-    for group in range(groups):
-        total_ref[...] += dot_rows(grads_ref[group], weights_ref[group, :, : 3 * width])
-    upstream, gain_grad, bias_grad = unwhiten(total_ref[...], vec[0], white_ref[...], rate_ref[...])
-    turned = upstream.T.astype(low)
-    words_out[...] = turned.reshape(words_out.shape)
-    between("words")
     turned = (white_ref[...] * vec[0] + vec[1]).T.astype(low)
     rel_turned = (rel_white_ref[...] * vec[2] + vec[3]).T.astype(low)
     chosen = selection(seq, entries)
@@ -1436,6 +1444,13 @@
         )
         put(group, 2 * width, 3 * width, dot_plain(turned, grads_ref[group, :, 2 * width :]))
         between(group)
+    total_ref[...] = sum_ref[...]
+    for group in range(groups):
+        total_ref[...] += dot_rows(grads_ref[group], weights_ref[group, :, : 3 * width])
+    upstream, gain_grad, bias_grad = unwhiten(total_ref[...], vec[0], white_ref[...], rate_ref[...])
+    turned = upstream.T.astype(low)
+    words_out[...] = turned.reshape(words_out.shape)
+    between("words")
     rel_up, rel_gain_grad, rel_bias_grad = unwhiten(
         rel_total, vec[2], rel_white_ref[...], rel_rate_ref[...]
     )
@@ -1483,29 +1498,29 @@
     greet(*spot, False)
     pl.semaphore_wait(pltpu.get_barrier_semaphore(), 9)
     start_words, forward, relay, finish = return_stages(spot, words_ref, sent_ref, refs[16:21])
-    start_sums, stages = sum_stages(spot, [project_ref], [total_ref], chunks, refs[21:])
+    start_sums, stages = sum_stages(
+        spot, [project_ref], [total_ref], chunks, refs[21:], resident=True
+    )
     start_pair = start_sums
 
     def between(point):
         if point == "words":
             start_words()
-        elif point == 1:
-            forward(0, 2)
-        elif point == 2:
-            forward(2, 4)
+            run_all(stages, (("pair", 0),))
         elif point == 3:
             start_pair(0)
-            forward(4, 6)
 
     project_back_kernel(*inputs, words_ref, project_ref, *work, between=between)
     start_pair(1)
-    run_all(stages, (("pair", 0),))
-    forward(6, 8)
     run_all(stages, (("pair", 1),))
+    forward(0, 2)
+    run_all(stages, (("first", 0),))
+    forward(2, 8)
+    run_all(stages, (("first", 1), ("second", 0)))
     relay(0, 4)
-    run_all(stages, (("first", 0), ("first", 1)))
+    run_all(stages, (("second", 1),))
     relay(4, 8)
-    run_all(stages, (("second", 0), ("second", 1), ("total", 0), ("total", 1)))
+    run_all(stages, (("total", 0), ("total", 1)))
     finish()
 
 
@@ -1515,7 +1530,7 @@
     seq = words.shape[1]
     size = project.shape[2]
     part = words.shape[0] // 8
-    chunks = chunked([size])
+    chunks = [(0, 0, 4 * BLOCK), (0, 4 * BLOCK, size - 4 * BLOCK)]
     return pl.pallas_call(
         functools.partial(project_return_kernel, chunks),
         in_specs=[IN_VMEM] * 10,
@@ -1561,7 +1576,7 @@
 def update_kernel(width, *refs):
     facts_ref, shared_ref, *grads = refs[:7]
     weights, refs = refs[7:31], refs[31:]
-    outputs, (factor_ref, bias_ref) = refs[:24], refs[24:26]
+    outputs, (norm_ref, loss_ref, bias_ref) = refs[:24], refs[24:27]
     squares = jnp.sum(facts_ref[0:1, :], 1, keepdims=True)
     factor = jnp.minimum(1.0, clip_level / jnp.sqrt(squares))
 
@@ -1583,7 +1598,8 @@
 
     @at_step(0)
     def norms():
-        factor_ref[...] = jnp.broadcast_to(jnp.sqrt(squares), factor_ref.shape)
+        norm_ref[...] = jnp.sqrt(squares)
+        loss_ref[...] = facts_ref[1:2, 0:1]
         count = weights[21].shape[0]
         for group in range(4):
             rows = shared_ref[group, :, BLOCK : 2 * BLOCK].T[BLOCK // 2 :]
@@ -1634,7 +1650,7 @@
     in_specs = [full(facts), full(shared), stripe] + [full(grad) for grad in grads[1:]]
     in_specs += [stripe] * 3 + [full(weight) for weight in weights[3:]]
     results = [jax.ShapeDtypeStruct(weight.shape, f32) for weight in weights]
-    results += [jax.ShapeDtypeStruct((1, BLOCK), f32), jax.ShapeDtypeStruct((1, rows), f32)]
+    results += [jax.ShapeDtypeStruct(shape, f32) for shape in ((1, 1), (1, 1), (1, rows))]
     return pl.pallas_call(
         functools.partial(update_kernel, width),
         grid=(slab // columns,),
@@ -1722,7 +1738,6 @@
     all_facts = share_facts(facts, 1) if direct else lax.all_gather(facts, "dp")
     all_ids = all_facts[:, :row_count].reshape(owners * row_count, seq_len)
     all_lengths = all_facts[:, row_count, :row_count].reshape(-1)
-    token_total = jnp.sum(all_lengths).astype(f32)
     local_ids = all_ids - holder * vocab_slab
     inside = (local_ids >= 0) & (local_ids < vocab_slab)
     inside = inside & (jnp.arange(seq_len)[None] < all_lengths[:, None])
@@ -1744,6 +1759,10 @@
     else:
         found = lax.psum_scatter(found, "heads", scatter_dimension=1, tiled=True)[:, 0]
         found = lax.all_to_all(found, "dp", 0, 0, tiled=True)
+    all_lengths, row_lengths, replaced, found = lax.optimization_barrier(
+        (all_lengths, row_lengths, replaced, found)
+    )
+    token_total = jnp.sum(all_lengths).astype(f32)
     own_length = lax.dynamic_slice_in_dim(row_lengths, holder, 1)
     own_live = jnp.arange(seq_len) < own_length
     own_flags = lax.dynamic_slice_in_dim(replaced, holder, 1)[0].astype(f32)
@@ -1816,14 +1835,14 @@
             for part in parts
         ]
         all_facts, shared = finish_sums(losses, own_squares, sums, head_width, 6)
-        *flat, norm_row, bias_row = update_all(
+        *flat, norm, loss_sum, bias_row = update_all(
             all_facts, shared, [grad_embedding, *sums], flat, head_width
         )
         flat = [
             part.transpose(turns[index // 3]) if index // 3 in turns else part
             for index, part in enumerate(flat)
         ]
-        return (all_facts[1, 0], token_total, norm_row[0, 0], *flat, bias_row[0])
+        return (loss_sum[0, 0], token_total, norm[0, 0], *flat, bias_row[0])
 
     squares_local = sum(jnp.sum(part * part) for part in sums) + jnp.sum(own_squares)
     shared = jnp.concatenate([sums[2][:, :head_width], sums[3][:, 3 * head_width :]], 1)

time: 421 us -> 403 us (0.957)
  Pallas kernels: 371 us -> 352 us
    pallas_call x1, Pallas kernels: 77 us -> 64.6 us  [attend_gather(): pl.pallas_call(attend_gather_kernel, in_specs=[pl.BlockSpec(memory_space=...]
    pallas_call x1, Pallas kernels: 37.9 us -> 33.2 us  [exchange_words(): pl.pallas_call(exchange_words_kernel, in_specs=[IN_VMEM], out_specs=IN_VM...]
  transfers between devices with their start and end apart: 1 -> 1, of which waited for: 1 -> 1; matrix products, arithmetic and copies ran while one was open for 4% -> 4% of each run, Pallas kernels for 15% -> 14%
where the time goes in v6:
time: 403 us; the launch traced here: 397 us
  Pallas kernels  352 us (87%)
  between operations  16.6 us (4%)
  other arithmetic  12.7 us (3%)
  local copies, waits for them, and re-layouts  8.33 us (2%)
  waiting for transfers between devices  7.31 us (2%)
    pallas_call x1, Pallas kernels, attend_back_sums(): pl.pallas_call(functools.partial(attend_back_sums_kernel, len(grads), chu...  80 us
    pallas_call x1, Pallas kernels, project_return(): pl.pallas_call(functools.partial(project_return_kernel, chunks), in_specs...  68.8 us
    pallas_call x1, Pallas kernels, attend_gather(): pl.pallas_call(attend_gather_kernel, in_specs=[pl.BlockSpec(memory_space=...  64.6 us
    pallas_call x1, Pallas kernels, middle(): pl.pallas_call(middle_kernel, in_specs=[ANYWHERE] + [IN_VMEM] * 4, out_sp...  34.3 us
    pallas_call x1, Pallas kernels, exchange_words(): pl.pallas_call(exchange_words_kernel, in_specs=[IN_VMEM], out_specs=IN_VM...  33.2 us
    pallas_call x1, Pallas kernels, update_all(): pl.pallas_call(functools.partial(update_kernel, width), grid=(slab // col...  21 us
    pallas_call x1, Pallas kernels, finish_sums(): pl.pallas_call(functools.partial(finish_sums_kernel, width), in_specs=[IN...  14.9 us
    pallas_call x1, Pallas kernels, deposit(): pl.pallas_call(deposit_kernel, grid=(steps,), in_specs=[pl.BlockSpec(memo...  13.7 us
  transfers between devices with their start and end apart: 1, of which 1 were waited for; matrix products, arithmetic and copies ran while one was open for 4% of the time, Pallas kernels for 14%

profile of v6, /device:TPU:0, one launch (start us, length us, event | category | flops | bytes accessed | tf_op | source)
XLA Modules:
  0.0 397.4 jit_solution(4921032428706134534)
XLA Ops:
  7.2 0.0 all-gather.2.cloned.1.call-start
  7.3 0.7 fusion.6
  8.0 0.8 constant_dynamic-slice_fusion
  8.8 0.1 copy.76
  8.9 1.0 convert_element_type.61
  9.8 0.2 copy.70
  10.1 0.8 copy.72
  10.9 0.0 all-gather.2.cloned.1.call-update
  11.0 1.0 copy.73
  12.0 1.3 pad_add_fusion.facts_ref
  13.3 10.9 %share_facts.1 = s32[8,8,512]{2,1,0:T(8,128)} custom-call(s32[8,512]{1,0:T(8,128)} %pad_add_fusion.facts_ref), custom_call_target="tpu_custom_call" | custom-call | tf_op jit(solution)/shard_map/share_facts/pallas_call | solution.py:513
  24.2 0.8 fusion.7
  25.0 0.1 lt.81
  25.1 0.1 reshape_squeeze.3
  25.2 1.2 convert_reduce_fusion
  26.4 0.1 reduce_sum.26
  26.5 0.1 reduce_sum.27.counts_ref
  26.6 0.1 broadcast_bitcast_fusion
  26.7 0.1 sub.23
  26.8 0.1 select_bitcast_fusion
  26.9 5.2 %sort.7 = s32[4096,4]{0,1:T(4,128)S(1)} sort(s32[4096,4]{0,1:T(4,128)S(1)} %select_bitcast_fusion), dimensions={0}, to_apply=%region_2.3 | sort | flops 229376 | bytes 131072 | tf_op jit(solution)/shard_map/sort | solution.py:1753
  32.1 0.0 copy-start.1
  32.2 1.0 convert_element_type.68
  33.2 0.0 copy-start.4
  33.2 0.0 copy-start.3
  33.2 11.0 %lookup.1 = bf16[32,96,512]{2,1,0:T(8,128)(2,1)S(1)} custom-call(s32[4]{0:T(128)S(1)} %reduce_sum.27.counts_ref, s32[4,1,4096]{2,1,0:T(1,128)S(1)} %broadcast_in_dim.26.keys_ref, f32[96,12672]{1,0:T(8,128)} %refs_7_.1), custom_call_target="tpu_custom_call" | custom-call | tf_op jit(solution)/shard_map/lookup/pallas_call | solution.py:955
  44.2 33.2 %exchange_words.1 = bf16[8,96,512]{2,1,0:T(8,128)(2,1)S(1)} custom-call(bf16[8,4,96,512]{3,2,1,0:T(8,128)(2,1)S(1)} %bitcast.63), custom_call_target="tpu_custom_call" | custom-call | tf_op jit(solution)/shard_map/exchange_words/pallas_call | solution.py:614
  77.5 0.0 copy-done.2
  77.5 0.0 copy-done.1
  77.5 0.0 copy-start
  77.5 0.9 copy-done
  78.4 0.6 reduce_sum.28
  79.7 0.0 copy-done.4
  79.7 0.6 dynamic_slice.12.length_ref
  80.3 0.7 convert_bitcast_fusion.1
  81.0 0.6 compare_select_fusion
  81.7 0.9 copy.74.marks_ref
  82.5 1.0 dynamic-slice_convert_fusion
  83.5 0.0 copy-done.3
  83.6 0.8 concatenate.11.pack_ref
  84.4 7.3 %all-gather.2.cloned.1.call-done = bf16[3072,896]{1,0:T(8,128)(2,1)} async-done(((bf16[96,896]{1,0:T(8,128)(2,1)}), bf16[3072,896]{1,0:T(8,128)(2,1)}) %all-gather.2.cloned.1.call-update) | async-done | bytes 5505040 | tf_op jit(solution)/shard_map/all_gather | solution.py:1733
  91.7 64.6 %attend_gather.1 = (f32[16,768]{1,0:T(8,128)}, f32[512,768]{1,0:T(8,128)}, f32[512,1]{1,0:T(8,128)}, bf16[4,512,576]{2,1,0:T(8,128)(2,1)}, f32[512,768]{1,0:T(8,...) custom-call(s32[1]{0:T(128)} %dynamic_slice.12.length_ref, ...), custom_call_target="tpu_custom_call" | custom-call | tf_op jit(solution)/shard_map/attend_gather/pallas_call | solution.py:1206
  156.3 34.3 %middle.1 = (bf16[4,768,768]{2,1,0:T(8,128)(2,1)}, bf16[4,768,768]{2,1,0:T(8,128)(2,1)}, bf16[4,768,384]{2,1,0:T(8,128)(2,1)}, bf16[4,512,192]{2,1,0:T(8,128)(2,...) custom-call(bf16[4,768,1920]{2,1,0:T(8,128)(2,1)} %bitcast.67, ...), custom_call_target="tpu_custom_call" | custom-call | tf_op jit(solution)/shard_map/middle/pallas_call | solution.py:1380
  190.5 80.0 %attend_back_sums.1 = (bf16[4,512,576]{2,1,0:T(8,128)(2,1)}, bf16[4,1024,384]{2,1,0:T(8,128)(2,1)}, f32[96,768]{1,0:T(8,128)}, f32[96,768]{1,0:T(8,128)}, f32[96,384]{1,0:T(8,128)}) custom-call(bf16[4,512,576]{2,1,0:T(8,128)(2,1)} %get-tuple-element.100.refs_0_, bf16[4,1024,384]{2,1,0:T(8,128)(2,1)} %get-tuple-element.101.refs_1_, ...), custom_call_target="tpu_custom_call" | custom-call | tf_op jit(solution)/shard_map/attend_back_sums/pallas_call | solution.py:450
  270.5 68.8 %project_return.1 = (bf16[8,4,96,512]{3,2,1,0:T(8,128)(2,1)}, f32[96,768]{1,0:T(8,128)}) custom-call(bf16[4,768,896]{2,1,0:T(8,128)(2,1)} %bitcast.66, f32[16,768]{1,0:T(8,128)} %get-tuple-element.90.vec_ref.refs_1_, f32[512,768]{1,0:T(8,128)} %get-tuple-element.91.white_ref.refs_2_, f32[512,1]{1,0:T(8,128)} %get-tuple-element.96.refs_3_, ...), custom_call_target="tpu_custom_call" | custom-call | tf_op jit(solution)/shard_map/project_return/pallas_call | solution.py:1534
  339.3 13.7 %deposit.1 = (f32[96,12672]{1,0:T(8,128)}, f32[96,128]{1,0:T(8,128)}) custom-call(s32[4]{0:T(128)} %copy-done.2, s32[4,1,4096]{2,1,0:T(1,128)} %copy-done.1, bf16[32,96,512]{2,1,0:T(8,128)(2,1)} %bitcast.70), custom_call_target="tpu_custom_call" | custom-call | tf_op jit(solution)/shard_map/deposit/pallas_call | solution.py:1023
  353.0 14.9 %finish_sums.1 = (f32[8,128]{1,0:T(8,128)}, f32[4,96,384]{2,1,0:T(8,128)}) custom-call(f32[512,1]{1,0:T(8,128)} %get-tuple-element.95.losses_ref, f32[96,128]{1,0:T(8,128)} %get-tuple-element.111.squares_ref, f32[96,768]{1,0:T(8,128)} %get-tuple-element.112.refs_0_.refs_3_, f32[96,768]{1,0:T(8,128)} %get-tuple-element.113.refs_1_.refs_4_, ...), custom_call_target="tpu_custom_call" | custom-call | tf_op jit(solution)/shard_map/finish_sums/pallas_call | solution.py:884
  367.9 21.0 %update_all.1 = (f32[96,12672]{1,0:T(8,128)}, f32[96,12672]{1,0:T(8,128)}, f32[96,12672]{1,0:T(8,128)}, f32[96,512]{1,0:T(8,128)}, f32[96,512]{1,0:T(8,128)}, /*...) custom-call(f32[8,128]{1,0:T(8,128)} %get-tuple-element.116.refs_0_,, ...), custom_call_target="tpu_custom_call" | custom-call | tf_op jit(solution)/shard_map/update_all/pallas_call | solution.py:1654
  (15 shorter events, 0.2 us)
Async XLA Ops:
  7.2 84.5 %all-gather.2.cloned.1.call-start = ((), (), s32[]{:S(2)}) async-start(), calls=%async_computation | async-start | bytes 5677056 | tf_op jit(solution)/shard_map/all_gather | solution.py:1733
  26.6 50.9 %copy-start.2 = (s32[4]{0:T(128)}, s32[4]{0:T(128)S(1)}, u32[]{:S(2)}) copy-start(s32[4]{0:T(128)S(1)} %reduce_sum.27.counts_ref) | copy-start | bytes 52
  32.1 45.3 %copy-start.1 = (s32[4,1,4096]{2,1,0:T(1,128)}, s32[4,1,4096]{2,1,0:T(1,128)S(1)}, u32[]{:S(2)}) copy-start(s32[4,1,4096]{2,1,0:T(1,128)S(1)} %broadcast_in_dim.26.keys_ref) | copy-start | bytes 196612
  33.2 46.5 %copy-start.4 = (s32[4]{0:T(128)S(1)}, s32[4]{0:T(128)}, u32[]{:S(2)}) copy-start(s32[4]{0:T(128)} %param.28) | copy-start | bytes 52
  33.2 50.4 %copy-start.3 = (f32[768,96]{0,1:T(8,128)S(1)}, f32[768,96]{0,1:T(8,128)}, u32[]{:S(2)}) copy-start(f32[768,96]{0,1:T(8,128)} %param.35) | copy-start | bytes 884740
  77.5 0.9 copy-start
Sparse Core Ops, SparseCore 0:
  11.6 80.0 all-gather.1

commit v7 on v6

--- a/solution.py
+++ b/solution.py
@@ -826,13 +826,14 @@
     *refs,
 ):
     sums, refs = refs[:4], refs[4:]
-    total_ref, all_ref, facts, pair, side, cross, line, local_sem, send_sem, recv_sem, line_send, line_recv = refs
+    total_ref, all_ref, facts, quad, line, shared_send, shared_recv, send_sem, quad_recv, line_recv = refs
     z, x, y, c = place()
-    core_to, y_to, x_to = device(z, x, y, 1 - c), device(z, x, 1 - y, c), device(z, 1 - x, y, c)
-    column = [(z + step) % 4 for step in range(1, 4)]
-    for target in (core_to, y_to, x_to, *[device(other, x, y, c) for other in column]):
-        signal(target)
-    own, other = y * 2 + c, (1 - y) * 2 + c
+    here, own, other = z * 2 + x, y * 2 + c, (1 - y) * 2 + c
+    core_to, y_to = device(z, x, y, 1 - c), device(z, x, 1 - y, c)
+    mates = [(1 - y, 1 - c), (1 - y, c), (y, 1 - c)]
+    meet_owners(z, x, y, c)
+    for mate_y, mate_c in mates:
+        signal(device(z, x, mate_y, mate_c))
     all_ref[own, :, :width] = sums[2][:, :width]
     all_ref[own, :, width:] = sums[3][:, 3 * width :]
     squares = jnp.sum(squares_ref[...], 0, keepdims=True)
@@ -843,40 +844,47 @@
     facts[0:1] = squares
     facts[1:2] = jnp.broadcast_to(jnp.sum(losses_ref[...], 0, keepdims=True), squares.shape)
     facts[2:8] = jnp.zeros((6, BLOCK), f32)
-    pl.semaphore_wait(pltpu.get_barrier_semaphore(), 6)
-    swap_pair = remote(facts, pair, send_sem.at[0], recv_sem.at[0], core_to)
-    swap_pair.start()
-    block = all_ref.at[own]
-    shared_side = remote(block, block, send_sem.at[3], recv_sem.at[3], y_to)
-    shared_pair = remote(block, block, send_sem.at[4], recv_sem.at[4], core_to)
-    swap_pair.wait()
-    total_ref[...] = facts[...] + pair[...]
-    swap_side = remote(total_ref, side, send_sem.at[1], recv_sem.at[1], y_to)
-    swap_side.start()
-    shared_side.start()
-    shared_pair.start()
-    swap_side.wait()
-    total_ref[...] += side[...]
-    swap_cross = remote(total_ref, cross, send_sem.at[2], recv_sem.at[2], x_to)
-    swap_cross.start()
-    swap_cross.wait()
-    total_ref[...] += cross[...]
-    line[z] = total_ref[...]
-    lines = [
-        remote(line.at[z], line.at[z], line_send.at[step], line_recv.at[z], device(to, x, y, c))
-        for step, to in enumerate(column)
-    ]
-    for copy in lines:
-        copy.start()
-    shared_side.wait()
-    relay = remote(all_ref.at[other], all_ref.at[other], send_sem.at[5], recv_sem.at[5], core_to)
-    relay.start()
-    for step, to in enumerate(column):
-        lines[step].wait_send()
-        remote(line.at[to], line.at[to], line_send.at[step], line_recv.at[to], core_to).wait_recv()
-    total_ref[...] = (line[0] + line[1]) + (line[2] + line[3])
-    shared_pair.wait()
-    relay.wait()
+    quad[own] = facts[...]
+
+    def quad_copy(step, source, to):
+        block = quad.at[source]
+        return remote(block, block, send_sem.at[step], quad_recv.at[source], to)
+
+    def line_copy(step, source, to):
+        block = line.at[source]
+        return remote(block, block, send_sem.at[3 + step], line_recv.at[source], to)
+
+    def shared_copy(step, source, to):
+        block = all_ref.at[source]
+        return remote(block, block, shared_send.at[step], shared_recv.at[source], to)
+
+    pl.semaphore_wait(pltpu.get_barrier_semaphore(), 10)
+    for step, mate in enumerate(mates):
+        quad_copy(step, own, device(z, x, *mate)).start()
+    shared_copy(0, own, y_to).start()
+    shared_copy(1, own, core_to).start()
+    for step, (mate_y, mate_c) in enumerate(mates):
+        quad_copy(step, mate_y * 2 + mate_c, core_to).wait_recv()
+    line[here] = (quad[0] + quad[1]) + (quad[2] + quad[3])
+    for step, (peer_z, peer_x) in enumerate(peers(z, x)):
+        line_copy(step, here, device(peer_z, peer_x, y, c)).start()
+    shared_copy(0, other, y_to).wait_recv()
+    shared_copy(2, other, core_to).start()
+    for step, (peer_z, peer_x) in enumerate(peers(z, x)):
+        line_copy(step, peer_z * 2 + peer_x, core_to).wait_recv()
+    total = line[0]
+    for index in range(1, 8):
+        total = total + line[index]
+    total_ref[...] = total
+    shared_copy(1, y * 2 + 1 - c, core_to).wait_recv()
+    shared_copy(2, (1 - y) * 2 + 1 - c, core_to).wait_recv()
+    for step, mate in enumerate(mates):
+        quad_copy(step, own, device(z, x, *mate)).wait_send()
+    for step, (peer_z, peer_x) in enumerate(peers(z, x)):
+        line_copy(step, here, device(peer_z, peer_x, y, c)).wait_send()
+    shared_copy(0, own, y_to).wait_send()
+    shared_copy(1, own, core_to).wait_send()
+    shared_copy(2, other, core_to).wait_send()
 
 
 def finish_sums(losses, squares, sums, width, tag):
@@ -889,14 +897,15 @@
             jax.ShapeDtypeStruct(small, f32),
             jax.ShapeDtypeStruct((4, squares.shape[0], 2 * width), f32),
         ],
-        scratch_shapes=[pltpu.VMEM(small, f32)] * 4
-        + [
+        scratch_shapes=[
+            pltpu.VMEM(small, f32),
             pltpu.VMEM((4,) + small, f32),
-            pltpu.SemaphoreType.DMA,
-            pltpu.SemaphoreType.DMA((6,)),
-            pltpu.SemaphoreType.DMA((6,)),
+            pltpu.VMEM((8,) + small, f32),
             pltpu.SemaphoreType.DMA((3,)),
             pltpu.SemaphoreType.DMA((4,)),
+            pltpu.SemaphoreType.DMA((10,)),
+            pltpu.SemaphoreType.DMA((4,)),
+            pltpu.SemaphoreType.DMA((8,)),
         ],
         compiler_params=pltpu.CompilerParams(collective_id=tag, has_side_effects=True),
         name="finish_sums",

time: 403 us -> 401 us (level)
  no operation moved by 1% of the time
where the time goes in v7:
time: 401 us; the launch traced here: 394 us
  Pallas kernels  349 us (87%)
  between operations  16.6 us (4%)
  other arithmetic  12.7 us (3%)
  local copies, waits for them, and re-layouts  8.33 us (2%)
  waiting for transfers between devices  7.45 us (2%)
    pallas_call x1, Pallas kernels, attend_back_sums(): pl.pallas_call(functools.partial(attend_back_sums_kernel, len(grads), chu...  80 us
    pallas_call x1, Pallas kernels, project_return(): pl.pallas_call(functools.partial(project_return_kernel, chunks), in_specs...  68.8 us
    pallas_call x1, Pallas kernels, attend_gather(): pl.pallas_call(attend_gather_kernel, in_specs=[pl.BlockSpec(memory_space=...  64.6 us
    pallas_call x1, Pallas kernels, middle(): pl.pallas_call(middle_kernel, in_specs=[ANYWHERE] + [IN_VMEM] * 4, out_sp...  34.2 us
    pallas_call x1, Pallas kernels, exchange_words(): pl.pallas_call(exchange_words_kernel, in_specs=[IN_VMEM], out_specs=IN_VM...  32.9 us
    pallas_call x1, Pallas kernels, update_all(): pl.pallas_call(functools.partial(update_kernel, width), grid=(slab // col...  21 us
    pallas_call x1, Pallas kernels, deposit(): pl.pallas_call(deposit_kernel, grid=(steps,), in_specs=[pl.BlockSpec(memo...  13.6 us
    pallas_call x1, Pallas kernels, finish_sums(): pl.pallas_call(functools.partial(finish_sums_kernel, width), in_specs=[IN...  11.8 us
  transfers between devices with their start and end apart: 1, of which 1 were waited for; matrix products, arithmetic and copies ran while one was open for 4% of the time, Pallas kernels for 14%

profile of v7, /device:TPU:0, one launch (start us, length us, event | category | flops | bytes accessed | tf_op | source)
XLA Modules:
  0.0 393.9 jit_solution(9409044222953093608)
XLA Ops:
  7.2 0.0 all-gather.2.cloned.1.call-start
  7.3 0.7 fusion.6
  8.0 0.8 constant_dynamic-slice_fusion
  8.8 0.1 copy.76
  8.9 1.0 convert_element_type.61
  9.8 0.2 copy.70
  10.1 0.8 copy.72
  10.9 0.0 all-gather.2.cloned.1.call-update
  11.0 1.0 copy.73
  12.0 1.3 pad_add_fusion.facts_ref
  13.3 10.9 %share_facts.1 = s32[8,8,512]{2,1,0:T(8,128)} custom-call(s32[8,512]{1,0:T(8,128)} %pad_add_fusion.facts_ref), custom_call_target="tpu_custom_call" | custom-call | tf_op jit(solution)/shard_map/share_facts/pallas_call | solution.py:513
  24.2 0.8 fusion.7
  25.0 0.1 lt.81
  25.1 0.1 reshape_squeeze.3
  25.2 1.2 convert_reduce_fusion
  26.4 0.1 reduce_sum.26
  26.5 0.1 reduce_sum.27.counts_ref
  26.6 0.1 broadcast_bitcast_fusion
  26.7 0.1 sub.23
  26.8 0.1 select_bitcast_fusion
  26.9 5.2 %sort.7 = s32[4096,4]{0,1:T(4,128)S(1)} sort(s32[4096,4]{0,1:T(4,128)S(1)} %select_bitcast_fusion), dimensions={0}, to_apply=%region_2.3 | sort | flops 229376 | bytes 131072 | tf_op jit(solution)/shard_map/sort | solution.py:1762
  32.1 0.0 copy-start.1
  32.2 1.0 convert_element_type.68
  33.2 0.0 copy-start.4
  33.2 0.0 copy-start.3
  33.2 11.0 %lookup.1 = bf16[32,96,512]{2,1,0:T(8,128)(2,1)S(1)} custom-call(s32[4]{0:T(128)S(1)} %reduce_sum.27.counts_ref, s32[4,1,4096]{2,1,0:T(1,128)S(1)} %broadcast_in_dim.26.keys_ref, f32[96,12672]{1,0:T(8,128)} %refs_7_.1), custom_call_target="tpu_custom_call" | custom-call | tf_op jit(solution)/shard_map/lookup/pallas_call | solution.py:964
  44.2 32.9 %exchange_words.1 = bf16[8,96,512]{2,1,0:T(8,128)(2,1)S(1)} custom-call(bf16[8,4,96,512]{3,2,1,0:T(8,128)(2,1)S(1)} %bitcast.63), custom_call_target="tpu_custom_call" | custom-call | tf_op jit(solution)/shard_map/exchange_words/pallas_call | solution.py:614
  77.1 0.0 copy-done.2
  77.1 0.0 copy-done.1
  77.1 0.0 copy-start
  77.1 0.9 copy-done
  78.0 0.6 reduce_sum.28
  79.3 0.0 copy-done.4
  79.3 0.6 dynamic_slice.12.length_ref
  79.9 0.7 convert_bitcast_fusion.1
  80.6 0.6 compare_select_fusion
  81.3 0.9 copy.74.marks_ref
  82.1 1.0 dynamic-slice_convert_fusion
  83.1 0.0 copy-done.3
  83.2 0.8 concatenate.11.pack_ref
  84.0 7.4 %all-gather.2.cloned.1.call-done = bf16[3072,896]{1,0:T(8,128)(2,1)} async-done(((bf16[96,896]{1,0:T(8,128)(2,1)}), bf16[3072,896]{1,0:T(8,128)(2,1)}) %all-gather.2.cloned.1.call-update) | async-done | bytes 5505040 | tf_op jit(solution)/shard_map/all_gather | solution.py:1742
  91.4 64.6 %attend_gather.1 = (f32[16,768]{1,0:T(8,128)}, f32[512,768]{1,0:T(8,128)}, f32[512,1]{1,0:T(8,128)}, bf16[4,512,576]{2,1,0:T(8,128)(2,1)}, f32[512,768]{1,0:T(8,...) custom-call(s32[1]{0:T(128)} %dynamic_slice.12.length_ref, ...), custom_call_target="tpu_custom_call" | custom-call | tf_op jit(solution)/shard_map/attend_gather/pallas_call | solution.py:1215
  156.0 34.2 %middle.1 = (bf16[4,768,768]{2,1,0:T(8,128)(2,1)}, bf16[4,768,768]{2,1,0:T(8,128)(2,1)}, bf16[4,768,384]{2,1,0:T(8,128)(2,1)}, bf16[4,512,192]{2,1,0:T(8,128)(2,...) custom-call(bf16[4,768,1920]{2,1,0:T(8,128)(2,1)} %bitcast.67, ...), custom_call_target="tpu_custom_call" | custom-call | tf_op jit(solution)/shard_map/middle/pallas_call | solution.py:1389
  190.3 80.0 %attend_back_sums.1 = (bf16[4,512,576]{2,1,0:T(8,128)(2,1)}, bf16[4,1024,384]{2,1,0:T(8,128)(2,1)}, f32[96,768]{1,0:T(8,128)}, f32[96,768]{1,0:T(8,128)}, f32[96,384]{1,0:T(8,128)}) custom-call(bf16[4,512,576]{2,1,0:T(8,128)(2,1)} %get-tuple-element.100.refs_0_, bf16[4,1024,384]{2,1,0:T(8,128)(2,1)} %get-tuple-element.101.refs_1_, ...), custom_call_target="tpu_custom_call" | custom-call | tf_op jit(solution)/shard_map/attend_back_sums/pallas_call | solution.py:450
  270.3 68.8 %project_return.1 = (bf16[8,4,96,512]{3,2,1,0:T(8,128)(2,1)}, f32[96,768]{1,0:T(8,128)}) custom-call(bf16[4,768,896]{2,1,0:T(8,128)(2,1)} %bitcast.66, f32[16,768]{1,0:T(8,128)} %get-tuple-element.90.vec_ref.refs_1_, f32[512,768]{1,0:T(8,128)} %get-tuple-element.91.white_ref.refs_2_, f32[512,1]{1,0:T(8,128)} %get-tuple-element.96.refs_3_, ...), custom_call_target="tpu_custom_call" | custom-call | tf_op jit(solution)/shard_map/project_return/pallas_call | solution.py:1543
  339.0 13.6 %deposit.1 = (f32[96,12672]{1,0:T(8,128)}, f32[96,128]{1,0:T(8,128)}) custom-call(s32[4]{0:T(128)} %copy-done.2, s32[4,1,4096]{2,1,0:T(1,128)} %copy-done.1, bf16[32,96,512]{2,1,0:T(8,128)(2,1)} %bitcast.70), custom_call_target="tpu_custom_call" | custom-call | tf_op jit(solution)/shard_map/deposit/pallas_call | solution.py:1032
  352.7 11.8 %finish_sums.1 = (f32[8,128]{1,0:T(8,128)}, f32[4,96,384]{2,1,0:T(8,128)}) custom-call(f32[512,1]{1,0:T(8,128)} %get-tuple-element.95.losses_ref, f32[96,128]{1,0:T(8,128)} %get-tuple-element.111.squares_ref, f32[96,768]{1,0:T(8,128)} %get-tuple-element.112.refs_0_.refs_3_, f32[96,768]{1,0:T(8,128)} %get-tuple-element.113.refs_1_.refs_4_, ...), custom_call_target="tpu_custom_call" | custom-call | tf_op jit(solution)/shard_map/finish_sums/pallas_call | solution.py:892
  364.4 21.0 %update_all.1 = (f32[96,12672]{1,0:T(8,128)}, f32[96,12672]{1,0:T(8,128)}, f32[96,12672]{1,0:T(8,128)}, f32[96,512]{1,0:T(8,128)}, f32[96,512]{1,0:T(8,128)}, /*...) custom-call(f32[8,128]{1,0:T(8,128)} %get-tuple-element.116.refs_0_,, ...), custom_call_target="tpu_custom_call" | custom-call | tf_op jit(solution)/shard_map/update_all/pallas_call | solution.py:1663
  (15 shorter events, 0.2 us)
Async XLA Ops:
  7.2 84.2 %all-gather.2.cloned.1.call-start = ((), (), s32[]{:S(2)}) async-start(), calls=%async_computation | async-start | bytes 5677056 | tf_op jit(solution)/shard_map/all_gather | solution.py:1742
  26.6 50.5 %copy-start.2 = (s32[4]{0:T(128)}, s32[4]{0:T(128)S(1)}, u32[]{:S(2)}) copy-start(s32[4]{0:T(128)S(1)} %reduce_sum.27.counts_ref) | copy-start | bytes 52
  32.1 44.9 %copy-start.1 = (s32[4,1,4096]{2,1,0:T(1,128)}, s32[4,1,4096]{2,1,0:T(1,128)S(1)}, u32[]{:S(2)}) copy-start(s32[4,1,4096]{2,1,0:T(1,128)S(1)} %broadcast_in_dim.26.keys_ref) | copy-start | bytes 196612
  33.2 46.1 %copy-start.4 = (s32[4]{0:T(128)S(1)}, s32[4]{0:T(128)}, u32[]{:S(2)}) copy-start(s32[4]{0:T(128)} %param.28) | copy-start | bytes 52
  33.2 50.0 %copy-start.3 = (f32[768,96]{0,1:T(8,128)S(1)}, f32[768,96]{0,1:T(8,128)}, u32[]{:S(2)}) copy-start(f32[768,96]{0,1:T(8,128)} %param.35) | copy-start | bytes 884740
  77.1 0.9 copy-start
Sparse Core Ops, SparseCore 0:
  11.6 79.7 all-gather.1
